TPU v7x, 32 devices: a whole 2x2x4 slice. The times are simulated.
32 devices in a mesh: dp: 8 (over z, x), tensor: 4 (over y, core).
Axes of the slice: x: 2, y: 2, z: 4, core: 2. Of those that a mesh axis runs over, the one named last changes fastest.
Arguments:
- inputs: bfloat16 [8192, 2048], P(('dp', 'tensor')), may hold values from -6 to 6
- lengths: int32 [8], P('dp'), may hold values from 128 to 1024, as said below
- cotangent: bfloat16 [8192, 2048], P(('dp', 'tensor')), may hold values from -6 to 6
- norm_attn: float32 [2048], replicated, may hold values from 0.5 to 1.5
- norm_ffn: float32 [2048], replicated, may hold values from 0.5 to 1.5
- norm_heads: float32 [256], replicated, may hold values from 0.5 to 1.5
- w_query: bfloat16 [2048, 2048], P('dp', 'tensor'), may hold values from -0.125 to 0.125
- w_key: bfloat16 [2048, 2048], P('dp', 'tensor'), may hold values from -0.125 to 0.125
- w_value: bfloat16 [2048, 4096], P('dp', 'tensor'), may hold values from -0.125 to 0.125
- w_out_gate: bfloat16 [2048, 4096], P('dp', 'tensor'), may hold values from -0.125 to 0.125
- w_decay: bfloat16 [2048, 16], P('dp', 'tensor'), may hold values from -0.125 to 0.125
- w_beta: bfloat16 [2048, 16], P('dp', 'tensor'), may hold values from -0.125 to 0.125
- w_output: bfloat16 [4096, 2048], P('tensor', 'dp'), may hold values from -0.1875 to 0.1875
- conv_query: float32 [4, 2048], replicated, may hold values from -3 to 3
- conv_key: float32 [4, 2048], replicated, may hold values from -3 to 3
- conv_value: float32 [4, 4096], replicated, may hold values from -3 to 3
- decay_log: float32 [16], replicated, may hold values from -7 to -2.5
- decay_bias: float32 [16], replicated, may hold values from -2 to 1
- w_ffn_gate: bfloat16 [2048, 5632], P('dp', 'tensor'), may hold values from -0.125 to 0.125
- w_ffn_up: bfloat16 [2048, 5632], P('dp', 'tensor'), may hold values from -0.125 to 0.125
- w_ffn_down: bfloat16 [5632, 2048], P('tensor', 'dp'), may hold values from -0.15625 to 0.15625
Outputs:
- outputs: bfloat16 [8192, 2048], P(('dp', 'tensor'))
- statistics: float32 [3], replicated
- grad_inputs: float32 [8192, 2048], P(('dp', 'tensor'))
- grad_norm_attn: float32 [2048], replicated
- grad_norm_ffn: float32 [2048], replicated
- grad_norm_heads: float32 [256], replicated
- grad_w_query: float32 [2048, 2048], P('dp', 'tensor')
- grad_w_key: float32 [2048, 2048], P('dp', 'tensor')
- grad_w_value: float32 [2048, 4096], P('dp', 'tensor')
- grad_w_out_gate: float32 [2048, 4096], P('dp', 'tensor')
- grad_w_decay: float32 [2048, 16], P('dp', 'tensor')
- grad_w_beta: float32 [2048, 16], P('dp', 'tensor')
- grad_w_output: float32 [4096, 2048], P('tensor', 'dp')
- grad_conv_query: float32 [4, 2048], replicated
- grad_conv_key: float32 [4, 2048], replicated
- grad_conv_value: float32 [4, 4096], replicated
- grad_decay_log: float32 [16], replicated
- grad_decay_bias: float32 [16], replicated
- grad_w_ffn_gate: float32 [2048, 5632], P('dp', 'tensor')
- grad_w_ffn_up: float32 [2048, 5632], P('dp', 'tensor')
- grad_w_ffn_down: float32 [5632, 2048], P('tensor', 'dp')
Inputs may be any that keep to these rules, and one draw needn't show every extreme that they name: Each sequence fills the first lengths rows of its group's 1024 rows; some length equals 1024 in every draw.
All inputs are finite; a program needn't handle non-finite values.
Results may differ from a plain program's by a relative error of at most 0.014.
The roundings to bfloat16 on the way count: a program that leaves them out, or rounds other values in their place, can miss the bound.
Values may be sent and summed in bfloat16 or wider, within the bound.
No kernel may reach another device: no remote copies, remote signals or barrier semaphores. Data moves between devices by JAX's collectives and lax.ppermute only.
A program may use at most 320 MiB of HBM per device.

v0:
```python
import jax
import jax.numpy as jnp
from jax import lax
from jax.sharding import PartitionSpec as P

DK = 128
SPAN = 64


def causal_conv(projected, kernel):
    width = kernel.shape[0]
    length = projected.shape[0]
    padded = jnp.pad(projected, ((width - 1, 0), (0, 0)))
    total = kernel[0] * padded[0:length]
    for offset in range(1, width):
        total = total + kernel[offset] * padded[offset : offset + length]
    return total


def unit_heads(mixed, heads, factor):
    shaped = mixed.reshape(mixed.shape[0], heads, -1)
    return shaped * lax.rsqrt(jnp.sum(shaped * shaped, axis=-1, keepdims=True) + 1e-06) * factor


def block_step(running_state, items):
    query_block, key_block, value_blk, beta_blk, decay_blk = items
    width = decay_blk.shape[1]
    highest_precision = lax.Precision.HIGHEST
    cumul = jnp.cumsum(decay_blk, axis=1)
    order = jnp.arange(width)
    lower = order[:, None] >= order[None, :]
    strict = order[:, None] > order[None, :]
    spread = cumul[:, :, None] - cumul[:, None, :]
    decay = jnp.where(lower, jnp.exp(jnp.where(lower, spread, 0.0)), 0.0)
    inner = jnp.einsum("htk,hsk->hts", key_block, key_block, precision=highest_precision)
    coupling = jnp.where(strict, beta_blk[:, :, None] * inner * decay, 0.0)
    system = jnp.eye(width, dtype=jnp.float32) + coupling
    opening_state = jnp.exp(cumul)
    carried_state = jnp.einsum(
        "zoa,zal->zol", key_block, running_state, precision=highest_precision
    )
    driving = beta_blk[:, :, None] * (value_blk - opening_state[:, :, None] * carried_state)
    solved_system = jax.scipy.linalg.solve_triangular(
        system, driving, lower=True, unit_diagonal=True
    )
    scores = jnp.einsum("htk,hsk->hts", query_block, key_block, precision=highest_precision) * decay
    output_rows = opening_state[:, :, None] * jnp.einsum(
        "zoa,zal->zol", query_block, running_state, precision=highest_precision
    )
    output_rows = output_rows + jnp.einsum(
        "hts,hsv->htv", scores, solved_system, precision=highest_precision
    )
    closing_state = jnp.exp(cumul[:, -1:] - cumul)
    running_state = jnp.exp(cumul[:, -1])[:, None, None] * running_state
    running_state = running_state + jnp.einsum(
        "cif,cie->cfe",
        key_block * closing_state[:, :, None],
        solved_system,
        precision=highest_precision,
    )
    return (running_state, output_rows)


def delta_rule(query, key, value, beta, log_decay):
    length, heads, key_size = query.shape
    value_size = value.shape[2]
    blocks = length // SPAN

    def arrange(array):
        return jnp.moveaxis(array.reshape((blocks, SPAN) + array.shape[1:]), 2, 1)

    items = (arrange(query), arrange(key), arrange(value), arrange(beta), arrange(log_decay))
    running_state = jnp.zeros((heads, key_size, value_size), jnp.float32)
    _, output_rows = lax.scan(jax.checkpoint(block_step), running_state, items)
    return jnp.moveaxis(output_rows, 1, 2).reshape(length, heads, value_size)


def mixer_front(query_proj, key_proj, value_proj, conv_query, conv_key, conv_value):
    heads = query_proj.shape[1] // DK
    length = query_proj.shape[0]
    query = unit_heads(jax.nn.silu(causal_conv(query_proj, conv_query)), heads, DK ** (-0.5))
    key = unit_heads(jax.nn.silu(causal_conv(key_proj, conv_key)), heads, 1.0)
    value = jax.nn.silu(causal_conv(value_proj, conv_value)).reshape(length, heads, -1)
    return (query, key, value)


def mixer_rest(
    query, key, value, gate_proj, decay_proj, beta_proj, decay_log, decay_bias, norm_heads
):
    length = query.shape[0]
    heads = query.shape[1]
    beta = jax.nn.sigmoid(beta_proj)
    log_decay = -jnp.exp(decay_log) * jax.nn.softplus(decay_proj + decay_bias)
    heads_out = delta_rule(query, key, value, beta, log_decay)
    scaled = (
        heads_out
        * lax.rsqrt(jnp.mean(heads_out * heads_out, axis=-1, keepdims=True) + 1e-05)
        * norm_heads
    )
    gated = scaled * jax.nn.silu(gate_proj.reshape(length, heads, -1))
    return gated.reshape(length, -1)


def rounded_copy(values):
    return lax.optimization_barrier(values.astype(jnp.bfloat16)).astype(jnp.float32)


def spread_rows(normed):
    return lax.all_gather(normed, "tensor", axis=0, tiled=True)


def spread_grads(grads):
    return lax.all_gather(grads, "tensor", axis=0, tiled=True)


def fetch_attention(w_query, w_key, w_value, w_out_gate, w_decay, w_beta, w_output):
    return (
        lax.all_gather(w_query, "dp", axis=0, tiled=True),
        lax.all_gather(w_key, "dp", axis=0, tiled=True),
        lax.all_gather(w_value, "dp", axis=0, tiled=True),
        lax.all_gather(w_out_gate, "dp", axis=0, tiled=True),
        lax.all_gather(w_decay, "dp", axis=0, tiled=True),
        lax.all_gather(w_beta, "dp", axis=0, tiled=True),
        lax.all_gather(w_output, "dp", axis=1, tiled=True),
    )


def fetch_ffn(w_ffn_gate, w_ffn_up, w_ffn_down):
    return (
        lax.all_gather(w_ffn_gate, "dp", axis=0, tiled=True),
        lax.all_gather(w_ffn_up, "dp", axis=0, tiled=True),
        lax.all_gather(w_ffn_down, "dp", axis=1, tiled=True),
    )


def branch_rows(left, right):
    return lax.psum_scatter(
        jnp.dot(left, right, preferred_element_type=jnp.float32),
        "tensor",
        scatter_dimension=0,
        tiled=True,
    )


def back_rows(pairs, rows):
    total = jnp.zeros((lax.axis_size("tensor") * rows, pairs[0][1].shape[0]), jnp.float32)
    for grad_part, weight in pairs:
        total = total + lax.dot_general(
            grad_part, weight, (((1,), (1,)), ((), ())), preferred_element_type=jnp.float32
        )
    return lax.psum_scatter(total, "tensor", scatter_dimension=0, tiled=True)


def contract_rows(left, right):
    return lax.dot_general(
        left, right, (((0,), (0,)), ((), ())), preferred_element_type=jnp.float32
    )


def times_transposed(left, right):
    return lax.dot_general(
        left, right, (((1,), (1,)), ((), ())), preferred_element_type=jnp.float32
    )


def norm_back(values, inverse, gain, incoming):
    scaled = incoming * gain
    width = values.shape[1]
    grad_values = (
        inverse * scaled
        - values
        * inverse
        * inverse
        * inverse
        * jnp.sum(scaled * values, axis=1, keepdims=True)
        / width
    )
    grad_gain = jnp.sum(incoming * values * inverse, axis=0)
    return (grad_values, grad_gain)


def place_slice(local, whole, rank, axis):
    return lax.dynamic_update_slice_in_dim(
        jnp.zeros_like(whole), local, rank * local.shape[axis], axis
    )


def shards(
    inputs,
    lengths,
    cotangent,
    norm_attn,
    norm_ffn,
    norm_heads,
    w_query,
    w_key,
    w_value,
    w_out_gate,
    w_decay,
    w_beta,
    w_output,
    conv_query,
    conv_key,
    conv_value,
    decay_log,
    decay_bias,
    w_ffn_gate,
    w_ffn_up,
    w_ffn_down,
):
    rows = inputs.shape[0]
    width = inputs.shape[1]
    tensor_rank = lax.axis_index("tensor")
    positions = tensor_rank * rows + jnp.arange(rows, dtype=jnp.int32)
    valid = (positions < lengths[0]).astype(jnp.float32)[:, None]
    stream_in = inputs.astype(jnp.float32)
    inverse_in = lax.rsqrt(jnp.mean(stream_in * stream_in, axis=1, keepdims=True) + 1e-06)
    normed_in = (stream_in * inverse_in * norm_attn).astype(jnp.bfloat16)
    full_in = spread_rows(normed_in)
    query_full, key_full, value_full, gate_full, decay_full, beta_full, output_full = (
        fetch_attention(w_query, w_key, w_value, w_out_gate, w_decay, w_beta, w_output)
    )
    query_proj = jnp.dot(full_in, query_full, preferred_element_type=jnp.float32)
    key_proj = jnp.dot(full_in, key_full, preferred_element_type=jnp.float32)
    value_proj = jnp.dot(full_in, value_full, preferred_element_type=jnp.float32)
    gate_proj = jnp.dot(full_in, gate_full, preferred_element_type=jnp.float32)
    decay_proj = jnp.dot(full_in, decay_full, preferred_element_type=jnp.float32)
    beta_proj = jnp.dot(full_in, beta_full, preferred_element_type=jnp.float32)
    heads_here = decay_full.shape[1]
    conv_query_here = lax.dynamic_slice_in_dim(
        conv_query, tensor_rank * query_full.shape[1], query_full.shape[1], 1
    )
    conv_key_here = lax.dynamic_slice_in_dim(
        conv_key, tensor_rank * key_full.shape[1], key_full.shape[1], 1
    )
    conv_value_here = lax.dynamic_slice_in_dim(
        conv_value, tensor_rank * value_full.shape[1], value_full.shape[1], 1
    )
    decay_log_here = lax.dynamic_slice_in_dim(decay_log, tensor_rank * heads_here, heads_here, 0)
    decay_bias_here = lax.dynamic_slice_in_dim(decay_bias, tensor_rank * heads_here, heads_here, 0)
    front_values, front_pullback = jax.vjp(
        mixer_front,
        query_proj,
        key_proj,
        value_proj,
        conv_query_here,
        conv_key_here,
        conv_value_here,
    )
    query_low = rounded_copy(front_values[0])
    key_low = rounded_copy(front_values[1])
    value_low = rounded_copy(front_values[2])
    mixer_value, back_pullback = jax.vjp(
        mixer_rest,
        query_low,
        key_low,
        value_low,
        gate_proj,
        decay_proj,
        beta_proj,
        decay_log_here,
        decay_bias_here,
        norm_heads,
    )
    mixer = mixer_value.astype(jnp.bfloat16)
    branch_attn = branch_rows(mixer, output_full)
    stream = stream_in + branch_attn
    inverse_mid = lax.rsqrt(jnp.mean(stream * stream, axis=1, keepdims=True) + 1e-06)
    normed_mid = (stream * inverse_mid * norm_ffn).astype(jnp.bfloat16)
    full_mid = spread_rows(normed_mid)
    gate_ffn, up_ffn, down_ffn = fetch_ffn(w_ffn_gate, w_ffn_up, w_ffn_down)
    ffn_gate = jnp.dot(full_mid, gate_ffn, preferred_element_type=jnp.float32)
    ffn_up = jnp.dot(full_mid, up_ffn, preferred_element_type=jnp.float32)
    sigma = jax.nn.sigmoid(ffn_gate)
    silu_gate = ffn_gate * sigma
    hidden = (silu_gate * ffn_up).astype(jnp.bfloat16)
    branch_ffn = branch_rows(hidden, down_ffn)
    outputs = (valid * (stream + branch_ffn)).astype(jnp.bfloat16)
    sum_inputs = jnp.sum(valid * stream_in * stream_in)
    sum_attn = jnp.sum(valid * branch_attn * branch_attn)
    sum_ffn = jnp.sum(valid * branch_ffn * branch_ffn)
    count_here = jnp.sum(valid)
    stat_sums = lax.psum((sum_inputs, sum_attn, sum_ffn, count_here), ("dp", "tensor"))
    grad_out = valid * cotangent.astype(jnp.float32)
    grad_ffn = spread_grads(grad_out.astype(jnp.bfloat16))
    gate_ffn, up_ffn, down_ffn = fetch_ffn(w_ffn_gate, w_ffn_up, w_ffn_down)
    grad_hidden = times_transposed(grad_ffn, down_ffn)
    grad_gate_in = (grad_hidden * ffn_up * sigma * (1.0 + ffn_gate * (1.0 - sigma))).astype(
        jnp.bfloat16
    )
    grad_up_in = (grad_hidden * silu_gate).astype(jnp.bfloat16)
    grad_mid = back_rows(((grad_gate_in, gate_ffn), (grad_up_in, up_ffn)), rows)
    grad_down = contract_rows(hidden, grad_ffn)
    grad_gate_weight = contract_rows(full_mid, grad_gate_in)
    grad_up_weight = contract_rows(full_mid, grad_up_in)
    owned_gate, owned_up, owned_down = (
        lax.psum_scatter(grad_gate_weight, "dp", scatter_dimension=0, tiled=True),
        lax.psum_scatter(grad_up_weight, "dp", scatter_dimension=0, tiled=True),
        lax.psum_scatter(grad_down, "dp", scatter_dimension=1, tiled=True),
    )
    grad_through, grad_norm_ffn = norm_back(stream, inverse_mid, norm_ffn, grad_mid)
    grad_stream = grad_out + grad_through
    grad_attn = spread_grads(grad_stream.astype(jnp.bfloat16))
    query_full, key_full, value_full, gate_full, decay_full, beta_full, output_full = (
        fetch_attention(w_query, w_key, w_value, w_out_gate, w_decay, w_beta, w_output)
    )
    grad_output_weight = contract_rows(mixer, grad_attn)
    grad_mixer = times_transposed(grad_attn, output_full)
    rest_grads = back_pullback(grad_mixer)
    front_grads = front_pullback((rest_grads[0], rest_grads[1], rest_grads[2]))
    grad_query_proj = front_grads[0].astype(jnp.bfloat16)
    grad_key_proj = front_grads[1].astype(jnp.bfloat16)
    grad_value_proj = front_grads[2].astype(jnp.bfloat16)
    grad_gate_proj = rest_grads[3].astype(jnp.bfloat16)
    grad_decay_proj = rest_grads[4].astype(jnp.bfloat16)
    grad_beta_proj = rest_grads[5].astype(jnp.bfloat16)
    grad_query_weight = contract_rows(full_in, grad_query_proj)
    grad_key_weight = contract_rows(full_in, grad_key_proj)
    grad_value_weight = contract_rows(full_in, grad_value_proj)
    grad_gate_weight_attn = contract_rows(full_in, grad_gate_proj)
    grad_decay_weight = contract_rows(full_in, grad_decay_proj)
    grad_beta_weight = contract_rows(full_in, grad_beta_proj)
    grad_normed = back_rows(
        (
            (grad_query_proj, query_full),
            (grad_key_proj, key_full),
            (grad_value_proj, value_full),
            (grad_gate_proj, gate_full),
            (grad_decay_proj, decay_full),
            (grad_beta_proj, beta_full),
        ),
        rows,
    )
    owned_query, owned_key, owned_value, owned_out_gate, owned_decay, owned_beta, owned_output = (
        lax.psum_scatter(grad_query_weight, "dp", scatter_dimension=0, tiled=True),
        lax.psum_scatter(grad_key_weight, "dp", scatter_dimension=0, tiled=True),
        lax.psum_scatter(grad_value_weight, "dp", scatter_dimension=0, tiled=True),
        lax.psum_scatter(grad_gate_weight_attn, "dp", scatter_dimension=0, tiled=True),
        lax.psum_scatter(grad_decay_weight, "dp", scatter_dimension=0, tiled=True),
        lax.psum_scatter(grad_beta_weight, "dp", scatter_dimension=0, tiled=True),
        lax.psum_scatter(grad_output_weight, "dp", scatter_dimension=1, tiled=True),
    )
    grad_through_in, grad_norm_attn = norm_back(stream_in, inverse_in, norm_attn, grad_normed)
    grad_inputs = grad_stream + grad_through_in
    conv_query_grad = place_slice(front_grads[3], conv_query, tensor_rank, 1)
    conv_key_grad = place_slice(front_grads[4], conv_key, tensor_rank, 1)
    conv_value_grad = place_slice(front_grads[5], conv_value, tensor_rank, 1)
    decay_log_grad = place_slice(rest_grads[6], decay_log, tensor_rank, 0)
    decay_bias_grad = place_slice(rest_grads[7], decay_bias, tensor_rank, 0)
    heads_gain_grad = rest_grads[8]
    (
        total_attn_gain,
        total_ffn_gain,
        total_heads_gain,
        total_conv_query,
        total_conv_key,
        total_conv_value,
        total_decay_log,
        total_decay_bias,
    ) = lax.psum(
        (
            grad_norm_attn,
            grad_norm_ffn,
            heads_gain_grad,
            conv_query_grad,
            conv_key_grad,
            conv_value_grad,
            decay_log_grad,
            decay_bias_grad,
        ),
        ("dp", "tensor"),
    )
    denominator = stat_sums[3] * width
    statistics = jnp.sqrt(jnp.stack([stat_sums[0], stat_sums[1], stat_sums[2]]) / denominator)
    return (
        outputs,
        statistics,
        grad_inputs,
        total_attn_gain,
        total_ffn_gain,
        total_heads_gain,
        owned_query,
        owned_key,
        owned_value,
        owned_out_gate,
        owned_decay,
        owned_beta,
        owned_output,
        total_conv_query,
        total_conv_key,
        total_conv_value,
        total_decay_log,
        total_decay_bias,
        owned_gate,
        owned_up,
        owned_down,
    )


def solution(mesh):
    in_specs = (
        P(("dp", "tensor"), None),
        P("dp"),
        P(("dp", "tensor"), None),
        P(),
        P(),
        P(),
        P("dp", "tensor"),
        P("dp", "tensor"),
        P("dp", "tensor"),
        P("dp", "tensor"),
        P("dp", "tensor"),
        P("dp", "tensor"),
        P("tensor", "dp"),
        P(),
        P(),
        P(),
        P(),
        P(),
        P("dp", "tensor"),
        P("dp", "tensor"),
        P("tensor", "dp"),
    )
    out_specs = (
        P(("dp", "tensor"), None),
        P(),
        P(("dp", "tensor"), None),
        P(),
        P(),
        P(),
        P("dp", "tensor"),
        P("dp", "tensor"),
        P("dp", "tensor"),
        P("dp", "tensor"),
        P("dp", "tensor"),
        P("dp", "tensor"),
        P("tensor", "dp"),
        P(),
        P(),
        P(),
        P(),
        P(),
        P("dp", "tensor"),
        P("dp", "tensor"),
        P("tensor", "dp"),
    )
    return jax.shard_map(shards, mesh=mesh, in_specs=in_specs, out_specs=out_specs, check_vma=False)
```

profile of v0, /device:TPU:0, one launch (start us, length us, event | category | flops | bytes accessed | tf_op | source)
XLA Modules:
  0.0 3654.4 jit_solution(7808922593041729502)
XLA Ops:
  15.4 27.8 all_gather.53
  43.3 26.2 all_gather.55
  71.5 26.1 all-gather.13.cloned.1.call-done
  114.7 34.4 all-gather.19.cloned.1.call-done
  173.7 49.3 %all-gather.17.cloned.1.call-done = bf16[2048,1024]{1,0:T(8,128)(2,1)} async-done(((bf16[256,1024]{1,0:T(8,128)(2,1)}), bf16[2048,1024]{1,0:T(8,128)(2,1)}) %all-gather.17.cloned.1.call-update) | async-done | bytes 4194320 | tf_op jit(solution)/shard_map/all_gather | solution.py:120
  244.9 488.6 %while.44 = (s32[]{:T(128)}, f32[4,128,256]{2,1,0:T(8,128)S(1)}, f32[16,4,64,256]{3,2,1,0:T(8,128)}, f32[16,4,128,256]{3,2,1,0:T(8,128)}, f32[16,4,64]{2,1,0:T(4...) while((s32[]{:T(128)}, f32[4,128,256]{2,1,0:T(8,128)S(1)}, ...), condition=%wide.region_5.7_spmd.clone.clone, body=%wide.region_3.6_spmd.clone.clone.sunk | while | flops 454381632 | bytes 6717690 | solution.py:74
  247.3 19.7 custom-call.26
  277.9 19.7 custom-call.26
  308.4 19.7 custom-call.26
  338.9 19.7 custom-call.26
  369.5 19.7 custom-call.26
  430.6 19.7 custom-call.26
  770.6 69.3 %reduce-scatter.19.cloned.1.call-done = f32[256,2048]{1,0:T(8,128)} async-done(((f32[1024,2048]{1,0:T(8,128)}), f32[256,2048]{1,0:T(8,128)}) %reduce-scatter.19.cloned.1.call-update) | async-done | bytes 2097168 | tf_op jit(solution)/shard_map/reduce_scatter | solution.py:137
  846.4 88.7 %all-gather.27.cloned.1.call-done = bf16[2048,1408]{1,0:T(8,128)(2,1)} async-done(((bf16[256,1408]{1,0:T(8,128)(2,1)}), bf16[2048,1408]{1,0:T(8,128)(2,1)}) %all-gather.27.cloned.1.call-update) | async-done | bytes 5767184 | tf_op jit(solution)/shard_map/all_gather | solution.py:130
  935.0 34.9 all-gather.25.cloned.1.call-done
  981.8 83.1 %all-gather.29.cloned.1.call-done = bf16[2048,1408]{1,0:T(8,128)(2,1)} async-done(((bf16[256,1408]{1,0:T(8,128)(2,1)}), bf16[2048,1408]{1,0:T(8,128)(2,1)}) %all-gather.29.cloned.1.call-update) | async-done | bytes 5767184 | tf_op jit(solution)/shard_map/all_gather | solution.py:131
  1076.6 23.3 all-gather.33.cloned.1.call-done
  1099.8 95.7 %all-gather.31.cloned.1.call-done = bf16[1408,2048]{1,0:T(8,128)(2,1)} async-done(((bf16[1408,256]{1,0:T(8,128)(2,1)}), bf16[1408,2048]{1,0:T(8,128)(2,1)}) %all-gather.31.cloned.1.call-update) | async-done | bytes 5767184 | tf_op jit(solution)/shard_map/all_gather | solution.py:132
  1231.4 69.8 %reduce-scatter.23.cloned.1.call-done = f32[256,2048]{1,0:T(8,128)} async-done(((f32[1024,2048]{1,0:T(8,128)}), f32[256,2048]{1,0:T(8,128)}) %reduce-scatter.23.cloned.1.call-update) | async-done | bytes 2097168 | tf_op jit(solution)/shard_map/reduce_scatter | solution.py:151
  1312.3 29.0 all-gather.35.cloned.1.call-done
  1379.4 625.3 %while.43 = (s32[]{:T(128)}, f32[4,128,256]{2,1,0:T(8,128)S(1)}, f32[16,4,64,128]{3,2,1,0:T(8,128)}, f32[16,4,64,128]{3,2,1,0:T(8,128)}, f32[16,4,64,256]{3,2,1,...) while((s32[]{:T(128)}, f32[4,128,256]{2,1,0:T(8,128)S(1)}, ...), condition=%wide.region_33.35_spmd.clone, body=%wide.region_21.34_spmd.clone.sunk | while | flops 1223996672 | bytes 21090280 | solution.py:74
  2219.5 70.1 %reduce-scatter.25.cloned.1.call-done = f32[256,2048]{1,0:T(8,128)} async-done(((f32[1024,2048]{1,0:T(8,128)}), f32[256,2048]{1,0:T(8,128)}) %reduce-scatter.25.cloned.1.call-update) | async-done | bytes 2097168 | tf_op jit(solution)/shard_map/reduce_scatter | solution.py:151
  2294.6 44.8 %all-reduce.34 = (f32[1]{0:T(128)}, f32[1]{0:T(128)}, f32[1]{0:T(128)}, f32[]{:T(128)}, f32[2048]{0:T(1024)}, /*index=5*/f32[2048]{0:T(1024)}, f32[256]{0:T(256)...) all-reduce(f32[1]{0:T(128)} %bitcast.25, ...), channel_id=1, replica_groups=mesh['dp'=8,'tensor'=4] {'dp','tensor'}, use_global_device_ids=true, to_apply=%region_15.17 | all-reduce | flops 20772 | bytes 166176 | tf_op jit(solution)/shard_map/psum | solution.py:283
  2346.8 140.6 %reduce-scatter.37.cloned.1.call-done = f32[256,1408]{1,0:T(8,128)} async-done(((f32[2048,1408]{1,0:T(8,128)}), f32[256,1408]{1,0:T(8,128)}) %reduce-scatter.37.cloned.1.call-update) | async-done | bytes 1441808 | tf_op jit(solution)/shard_map/reduce_scatter | solution.py:297
  2487.4 195.8 %reduce-scatter.39.cloned.1.call-done = f32[256,1408]{1,0:T(8,128)} async-done(((f32[2048,1408]{1,0:T(8,128)}), f32[256,1408]{1,0:T(8,128)}) %reduce-scatter.39.cloned.1.call-update) | async-done | bytes 1441808 | tf_op jit(solution)/shard_map/reduce_scatter | solution.py:298
  2683.3 196.4 %reduce-scatter.41.cloned.1.call-done = f32[1408,256]{1,0:T(8,128)} async-done(((f32[1408,2048]{1,0:T(8,128)}), f32[1408,256]{1,0:T(8,128)}) %reduce-scatter.41.cloned.1.call-update) | async-done | bytes 1441808 | tf_op jit(solution)/shard_map/reduce_scatter | solution.py:299
  2879.7 122.8 %all-reduce.33.cloned.1.call-done = f32[4,4096]{1,0:T(4,128)} async-done(((f32[4,4096]{1,0:T(4,128)}), f32[4,4096]{1,0:T(4,128)}) %all-reduce.33.cloned.1.call-update) | async-done | bytes 65552 | tf_op jit(solution)/shard_map/psum | solution.py:360
  3002.5 92.9 %reduce-scatter.29.cloned.1.call-done = f32[256,512]{1,0:T(8,128)} async-done(((f32[2048,512]{1,0:T(8,128)}), f32[256,512]{1,0:T(8,128)}) %reduce-scatter.29.cloned.1.call-update) | async-done | bytes 524304 | tf_op jit(solution)/shard_map/reduce_scatter | solution.py:336
  3095.4 92.3 %reduce-scatter.27.cloned.1.call-done = f32[256,512]{1,0:T(8,128)} async-done(((f32[2048,512]{1,0:T(8,128)}), f32[256,512]{1,0:T(8,128)}) %reduce-scatter.27.cloned.1.call-update) | async-done | bytes 524304 | tf_op jit(solution)/shard_map/reduce_scatter | solution.py:335
  3187.8 153.4 %reduce-scatter.35.cloned.1.call-done = f32[1024,256]{1,0:T(8,128)} async-done(((f32[1024,2048]{1,0:T(8,128)}), f32[1024,256]{1,0:T(8,128)}) %reduce-scatter.35.cloned.1.call-update) | async-done | bytes 1048592 | tf_op jit(solution)/shard_map/reduce_scatter | solution.py:341
  3341.2 152.5 %reduce-scatter.31.cloned.1.call-done = f32[256,1024]{1,0:T(8,128)} async-done(((f32[2048,1024]{1,0:T(8,128)}), f32[256,1024]{1,0:T(8,128)}) %reduce-scatter.31.cloned.1.call-update) | async-done | bytes 1048592 | tf_op jit(solution)/shard_map/reduce_scatter | solution.py:337
  3493.7 152.1 %reduce-scatter.33.cloned.1.call-done = f32[256,1024]{1,0:T(8,128)} async-done(((f32[2048,1024]{1,0:T(8,128)}), f32[256,1024]{1,0:T(8,128)}) %reduce-scatter.33.cloned.1.call-update) | async-done | bytes 1048592 | tf_op jit(solution)/shard_map/reduce_scatter | solution.py:338
  (1400 shorter events, 1442.8 us)
Async XLA Ops:
  7.2 64.4 %all-gather.15.cloned.1.call-start = ((), (), s32[]{:S(2)}) async-start(), calls=%async_computation.15 | async-start | bytes 2359296 | tf_op jit(solution)/shard_map/all_gather | solution.py:119
  7.9 89.7 %all-gather.13.cloned.1.call-start = ((), (), s32[]{:S(2)}) async-start(), calls=%async_computation.14 | async-start | bytes 5242880 | tf_op jit(solution)/shard_map/all_gather | solution.py:109
  12.7 136.4 %all-gather.19.cloned.1.call-start = ((), (), s32[]{:S(2)}) async-start(), calls=%async_computation.17 | async-start | bytes 2359296 | tf_op jit(solution)/shard_map/all_gather | solution.py:118
  13.4 209.5 %all-gather.17.cloned.1.call-start = ((), (), s32[]{:S(2)}) async-start(), calls=%async_computation.16 | async-start | bytes 4718592 | tf_op jit(solution)/shard_map/all_gather | solution.py:120
  14.0 733.3 %all-gather.21.cloned.1.call-start = ((), (), s32[]{:S(2)}) async-start(), calls=%async_computation.18 | async-start | bytes 4718592 | tf_op jit(solution)/shard_map/all_gather | solution.py:121
  14.6 745.6 %all-gather.23.cloned.1.call-start = ((), (), s32[]{:S(2)}) async-start(), calls=%async_computation.19 | async-start | bytes 4718592 | tf_op jit(solution)/shard_map/all_gather | solution.py:124
  15.2 824.8 %reduce-scatter.19.cloned.1.call-start = ((), (), s32[]{:S(2)}) async-start(), calls=%async_computation.20 | async-start | bytes 10485760 | tf_op jit(solution)/shard_map/reduce_scatter | solution.py:137
  70.4 160.1 %copy-start.49 = (f32[1,1024]{1,0:T(1,128)}, f32[1,1024]{1,0:T(1,128)S(1)}, u32[]{:S(2)}) copy-start(f32[1,1024]{1,0:T(1,128)S(1)} %get-tuple-element.832) | copy-start | bytes 12292
  70.4 160.1 %copy-start.51 = (f32[1,1024]{1,0:T(1,128)}, f32[1,1024]{1,0:T(1,128)S(1)}, u32[]{:S(2)}) copy-start(f32[1,1024]{1,0:T(1,128)S(1)} %get-tuple-element.833) | copy-start | bytes 12292
  70.5 160.1 %copy-start.53 = (f32[1,1024]{1,0:T(1,128)}, f32[1,1024]{1,0:T(1,128)S(1)}, u32[]{:S(2)}) copy-start(f32[1,1024]{1,0:T(1,128)S(1)} %get-tuple-element.834) | copy-start | bytes 12292
  769.8 165.2 %all-gather.27.cloned.1.call-start = ((), (), s32[]{:S(2)}) async-start(), calls=%async_computation.22 | async-start | bytes 6488064 | tf_op jit(solution)/shard_map/all_gather | solution.py:130
  770.6 199.4 %all-gather.25.cloned.1.call-start = ((), (), s32[]{:S(2)}) async-start(), calls=%async_computation.21 | async-start | bytes 5242880 | tf_op jit(solution)/shard_map/all_gather | solution.py:109
  841.9 462.1 %copy-start.3 = (f32[256,2048]{1,0:T(8,128)}, f32[256,2048]{1,0:T(8,128)S(1)}, u32[]{:S(2)}) copy-start(f32[256,2048]{1,0:T(8,128)S(1)} %get-tuple-element.784) | copy-start | bytes 6291460
  843.2 221.7 %all-gather.29.cloned.1.call-start = ((), (), s32[]{:S(2)}) async-start(), calls=%async_computation.23 | async-start | bytes 6488064 | tf_op jit(solution)/shard_map/all_gather | solution.py:131
  843.8 256.0 %all-gather.33.cloned.1.call-start = ((), (), s32[]{:S(2)}) async-start(), calls=%async_computation.26 | async-start | bytes 5242880 | tf_op jit(solution)/shard_map/all_gather | solution.py:113
  844.5 459.6 %copy-start.76 = (f32[256]{0:T(256)}, f32[256]{0:T(256)S(1)}, u32[]{:S(2)}) copy-start(f32[256]{0:T(256)S(1)} %compare_convert_fusion) | copy-start | bytes 3076
  845.7 349.8 %all-gather.31.cloned.1.call-start = ((), (), s32[]{:S(2)}) async-start(), calls=%async_computation.24 | async-start | bytes 6488064 | tf_op jit(solution)/shard_map/all_gather | solution.py:132
  846.3 454.8 %reduce-scatter.23.cloned.1.call-start = ((), (), s32[]{:S(2)}) async-start(), calls=%async_computation.27 | async-start | bytes 10485760 | tf_op jit(solution)/shard_map/reduce_scatter | solution.py:151
  1231.1 110.2 %all-gather.35.cloned.1.call-start = ((), (), s32[]{:S(2)}) async-start(), calls=%async_computation.28 | async-start | bytes 5242880 | tf_op jit(solution)/shard_map/all_gather | solution.py:113
  1306.6 909.7 %reduce-scatter.45.cloned.1.call-start = ((), (), s32[]{:S(2)}) async-start(), calls=%async_computation.40 | async-start | bytes 1179648
  2011.6 206.2 %reduce-scatter.43.cloned.1.call-start = ((), (), s32[]{:S(2)}) async-start(), calls=%async_computation.39 | async-start | bytes 1179648
  2017.2 202.2 %reduce-scatter.21.cloned.1.call-start = ((), (), s32[]{:S(2)}) async-start(), calls=%async_computation.25 | async-start | bytes 10485760 | tf_op jit(solution)/shard_map/reduce_scatter | solution.py:137
  2028.1 261.4 %reduce-scatter.25.cloned.1.call-start = ((), (), s32[]{:S(2)}) async-start(), calls=%async_computation.29 | async-start | bytes 10485760 | tf_op jit(solution)/shard_map/reduce_scatter | solution.py:151
  2131.4 356.0 %reduce-scatter.37.cloned.1.call-start = ((), (), s32[]{:S(2)}) async-start(), calls=%async_computation.36 | async-start | bytes 12976128 | tf_op jit(solution)/shard_map/reduce_scatter | solution.py:297
  2143.3 539.9 %reduce-scatter.39.cloned.1.call-start = ((), (), s32[]{:S(2)}) async-start(), calls=%async_computation.37 | async-start | bytes 12976128 | tf_op jit(solution)/shard_map/reduce_scatter | solution.py:298
  2156.3 723.3 %reduce-scatter.41.cloned.1.call-start = ((), (), s32[]{:S(2)}) async-start(), calls=%async_computation.38 | async-start | bytes 12976128 | tf_op jit(solution)/shard_map/reduce_scatter | solution.py:299
  2168.5 834.0 %all-reduce.33.cloned.1.call-start = ((), (), s32[]{:S(2)}) async-start(), calls=%async_computation.35 | async-start | bytes 131072 | tf_op jit(solution)/shard_map/psum | solution.py:360
  2169.3 926.1 %reduce-scatter.29.cloned.1.call-start = ((), (), s32[]{:S(2)}) async-start(), calls=%async_computation.31 | async-start | bytes 4718592 | tf_op jit(solution)/shard_map/reduce_scatter | solution.py:336
  2176.1 1011.6 %reduce-scatter.27.cloned.1.call-start = ((), (), s32[]{:S(2)}) async-start(), calls=%async_computation.30 | async-start | bytes 4718592 | tf_op jit(solution)/shard_map/reduce_scatter | solution.py:335
  2182.9 1158.3 %reduce-scatter.35.cloned.1.call-start = ((), (), s32[]{:S(2)}) async-start(), calls=%async_computation.34 | async-start | bytes 9437184 | tf_op jit(solution)/shard_map/reduce_scatter | solution.py:341
  2193.4 1300.3 %reduce-scatter.31.cloned.1.call-start = ((), (), s32[]{:S(2)}) async-start(), calls=%async_computation.32 | async-start | bytes 9437184 | tf_op jit(solution)/shard_map/reduce_scatter | solution.py:337
  2204.1 1441.7 %reduce-scatter.33.cloned.1.call-start = ((), (), s32[]{:S(2)}) async-start(), calls=%async_computation.33 | async-start | bytes 9437184 | tf_op jit(solution)/shard_map/reduce_scatter | solution.py:338
  (101 other events, 2096.2 us)
Sparse Core Ops, SparseCore 0:
  10.1 52.1 all-gather.14
  64.5 33.0 all-gather.12
  99.7 49.2 all-gather.18
  151.1 71.8 all-gather.16
  224.9 71.7 all-gather.20
  298.7 74.4 all-gather.22
  770.0 69.9 reduce-scatter.18
  842.4 92.6 all-gather.26
  937.3 32.6 all-gather.24
  972.2 92.6 all-gather.28
  1067.1 32.6 all-gather.32
  1101.9 93.5 all-gather.30
  1231.2 69.9 reduce-scatter.22
  1306.8 34.4 all-gather.34
  2011.8 63.4 reduce-scatter.44
  2079.5 62.4 reduce-scatter.42
  2144.4 70.7 reduce-scatter.20
  2217.8 71.7 reduce-scatter.24
  2293.7 193.6 reduce-scatter.36
  2491.4 191.7 reduce-scatter.38
  2687.5 192.1 reduce-scatter.40
  2885.8 116.6 all-reduce.32
  3006.7 88.6 reduce-scatter.28
  3099.9 87.8 reduce-scatter.26
  3192.0 149.1 reduce-scatter.34
  3345.7 147.9 reduce-scatter.30
  3497.8 147.9 reduce-scatter.32
where the time goes:
time: 3660 us; the launch traced here: 3650 us
  waiting for transfers between devices  1980 us (54%)
  other arithmetic  775 us (21%)
  matrix products  595 us (16%)
  local copies, waits for them, and re-layouts  184 us (5%)
  blocking collectives  98.8 us (3%)
    another operation x128, other arithmetic, block_step(): jax.scipy.linalg.solve_triangular(system, driving, lower=True, unit_diago...  634 us
    reduce_scatter x1, waiting for transfers between devices, shards(): lax.psum_scatter(grad_down, 'dp', scatter_dimension=1, tiled=True)  196 us
    reduce_scatter x1, waiting for transfers between devices, shards(): lax.psum_scatter(grad_up_weight, 'dp', scatter_dimension=0, tiled=True)  196 us
    reduce_scatter x1, waiting for transfers between devices, shards(): lax.psum_scatter(grad_output_weight, 'dp', scatter_dimension=1, tiled=True)  153 us
    reduce_scatter x1, waiting for transfers between devices, shards(): lax.psum_scatter(grad_value_weight, 'dp', scatter_dimension=0, tiled=True)  153 us
    reduce_scatter x1, waiting for transfers between devices, shards(): lax.psum_scatter(grad_gate_weight_attn, 'dp', scatter_dimension=0, tiled=...  152 us
    reduce_scatter x1, waiting for transfers between devices, shards(): lax.psum_scatter(grad_gate_weight, 'dp', scatter_dimension=0, tiled=True)  141 us
    reduce_scatter x2, waiting for transfers between devices, back_rows(): return lax.psum_scatter(total, 'tensor', scatter_dimension=0, tiled=True)  140 us
  transfers between devices with their start and end apart: 27, of which 21 were waited for; matrix products, arithmetic and copies ran while one was open for 22% of the time, Pallas kernels for 0%

commit v1 on v0

--- a/solution.py
+++ b/solution.py
@@ -1,10 +1,157 @@
+import functools
+
 import jax
 import jax.numpy as jnp
 from jax import lax
+from jax.experimental import pallas as pl
+from jax.experimental.pallas import tpu as pltpu
 from jax.sharding import PartitionSpec as P
 
 DK = 128
-SPAN = 64
+BF=jnp.bfloat16; F32=jnp.float32
+CHUNK=128
+
+def dot1(a,b,ca=1,cb=0):
+    return lax.dot_general(a,b,(((ca,),(cb,)),((),())),preferred_element_type=F32)
+def split(a):
+    if a.dtype==BF: return a,None
+    h=a.astype(BF); return h,(a-h.astype(F32)).astype(BF)
+def mm(a,b,ca=1,cb=0):
+    ah,al=a if isinstance(a,tuple) else split(a)
+    bh,bl=b if isinstance(b,tuple) else split(b)
+    r=dot1(ah,bh,ca,cb)
+    if bl is not None: r=r+dot1(ah,bl,ca,cb)
+    if al is not None: r=r+dot1(al,bh,ca,cb)
+    return r
+
+def inverses(As):
+    C=As[0].shape[0]
+    i=lax.broadcasted_iota(jnp.int32,(C,C),0); j=lax.broadcasted_iota(jnp.int32,(C,C),1)
+    eye=jnp.where(i==j,1.0,0.0).astype(F32)
+    same=lambda s: lax.shift_right_logical(i,s)==lax.shift_right_logical(j,s)
+    m3=same(3)
+    Bs=[jnp.where(m3,A,0.0) for A in As]
+    B2=[mm(s,s) for s in map(split,Bs)]
+    X=[eye-B for B in Bs]
+    B2s=[split(b) for b in B2]
+    B4=[mm(b,b) for b in B2s]
+    X=[x+mm(x,b) for x,b in zip(X,B2s)]
+    X=[x+mm(x,b) for x,b in zip(X,B4)]
+    s=3
+    while (1<<s)<C:
+        m=jnp.logical_and(same(s+1),jnp.logical_not(same(s)))
+        Xs=[split(x) for x in X]
+        Y=[mm(jnp.where(m,A,0.0),x) for A,x in zip(As,Xs)]
+        X=[x-mm(xs,y) for x,xs,y in zip(X,Xs,Y)]
+        s+=1
+    return X
+
+def fwd_kernel(H,DK,DV,NC,q_ref,k_ref,v_ref,bc_ref,gc_ref,gr_ref,o_ref,u_ref,t_ref,s_ref,S):
+    C=CHUNK
+    @pl.when(pl.program_id(0)==0)
+    def _():
+        S[...]=jnp.zeros_like(S)
+    i=lax.broadcasted_iota(jnp.int32,(C,C),0); j=lax.broadcasted_iota(jnp.int32,(C,C),1)
+    low=i>=j; strict=i>j
+    idx=[(c,h) for c in range(NC) for h in range(H)]
+    rows=lambda c: slice(c*C,(c+1)*C)
+    q={x:q_ref[rows(x[0]),x[1]*DK:(x[1]+1)*DK] for x in idx}
+    k={x:k_ref[rows(x[0]),x[1]*DK:(x[1]+1)*DK] for x in idx}
+    v={x:v_ref[rows(x[0]),x[1]*DV:(x[1]+1)*DV] for x in idx}
+    b={x:bc_ref[rows(x[0]),x[1]:x[1]+1] for x in idx}
+    g={x:gc_ref[rows(x[0]),x[1]:x[1]+1] for x in idx}
+    gr={x:gr_ref[x[0],x[1]:x[1]+1,:] for x in idx}
+    D={x:jnp.exp(jnp.where(low,g[x]-gr[x],-1e30)) for x in idx}
+    A={x:jnp.where(strict,dot1(k[x],k[x],1,1)*b[x]*D[x],0.0) for x in idx}
+    T=dict(zip(idx,inverses([A[x] for x in idx])))
+    P={x:dot1(q[x],k[x],1,1)*D[x] for x in idx}
+    gam={x:jnp.exp(g[x]) for x in idx}
+    Ts={x:split(T[x]) for x in idx}
+    TV={x:mm(Ts[x],b[x]*v[x].astype(F32)) for x in idx}
+    W={x:mm(Ts[x],b[x]*gam[x]*k[x].astype(F32)) for x in idx}
+    for c in range(NC):
+        for h in range(H):
+            x=(c,h)
+            t_ref[rows(c),h*C:(h+1)*C]=T[x]
+            S0=S[h*DK:(h+1)*DK,:]
+            s_ref[c,h*DK:(h+1)*DK,:]=S0
+            Ss=split(S0)
+            U=TV[x]-mm(W[x],Ss)
+            Us=split(U)
+            u_ref[rows(c),h*DV:(h+1)*DV]=U
+            o_ref[rows(c),h*DV:(h+1)*DV]=gam[x]*mm(q[x],Ss)+mm(P[x],Us)
+            gl=gr[x][:,C-1:C]
+            S[h*DK:(h+1)*DK,:]=jnp.exp(gl)*S0+mm(k[x].astype(F32)*jnp.exp(gl-g[x]),Us,0,0)
+
+def bwd_kernel(H,DK,DV,NC,q_ref,k_ref,v_ref,bc_ref,gc_ref,gr_ref,u_ref,t_ref,s_ref,do_ref,
+               dq_ref,dk_ref,dv_ref,dbc_ref,dgc_ref,dgr_ref,dS):
+    C=CHUNK
+    @pl.when(pl.program_id(0)==0)
+    def _():
+        dS[...]=jnp.zeros_like(dS)
+    i=lax.broadcasted_iota(jnp.int32,(C,C),0); j=lax.broadcasted_iota(jnp.int32,(C,C),1)
+    low=i>=j; strict=i>j
+    last=lax.broadcasted_iota(jnp.int32,(C,1),0)==C-1
+    rows=lambda c: slice(c*C,(c+1)*C)
+    for c in reversed(range(NC)):
+        for h in range(H):
+            q=q_ref[rows(c),h*DK:(h+1)*DK]; k=k_ref[rows(c),h*DK:(h+1)*DK]
+            v=v_ref[rows(c),h*DV:(h+1)*DV]
+            b=bc_ref[rows(c),h:h+1]; g=gc_ref[rows(c),h:h+1]; gr=gr_ref[c,h:h+1,:]
+            U=split(u_ref[rows(c),h*DV:(h+1)*DV]); T=split(t_ref[rows(c),h*C:(h+1)*C])
+            S0=s_ref[c,h*DK:(h+1)*DK,:]; Ss=split(S0)
+            dO=split(do_ref[rows(c),h*DV:(h+1)*DV])
+            qf=q.astype(F32); kf=k.astype(F32)
+            D=jnp.exp(jnp.where(low,g-gr,-1e30))
+            kk=dot1(k,k,1,1); qk=dot1(q,k,1,1)
+            bD=b*D
+            A=jnp.where(strict,kk*bD,0.0); P=qk*D
+            gam=jnp.exp(g); gl=gr[:,C-1:C]; e=jnp.exp(gl-g); G=jnp.exp(gl)
+            dSv=dS[h*DK:(h+1)*DK,:]; dSs=split(dSv)
+            dU=mm(P,dO,0,0)+mm(kf*e,dSs)
+            dR=mm(T,dU,0,0); dRs=split(dR)
+            dS[h*DK:(h+1)*DK,:]=G*dSv+mm(qf*gam,dO,0,0)-mm(kf*(b*gam),dRs,0,0)
+            dP=jnp.where(low,mm(dO,U,1,1),0.0)
+            dA=jnp.where(strict,-mm(dRs,U,1,1),0.0)
+            Rb=v.astype(F32)-gam*mm(k,Ss)
+            dv_ref[rows(c),h*DV:(h+1)*DV]=b*dR
+            db=jnp.sum(dR*Rb,axis=1,keepdims=True)+jnp.sum(dA*kk*D,axis=1,keepdims=True)
+            dOS=mm(dO,Ss,1,1); dRS=mm(dRs,Ss,1,1); UdS=mm(U,dSs,1,1)
+            M1=split(dP*D); M2=split(dA*bD)
+            dOS=gam*dOS; dRS=(b*gam)*dRS; UdS=e*UdS
+            dq_ref[rows(c),h*DK:(h+1)*DK]=dOS+mm(M1,k)
+            dk_ref[rows(c),h*DK:(h+1)*DK]=UdS-dRS+mm(M1,q,0,0)+mm(M2,k)+mm(M2,k,0,0)
+            X=dP*P+dA*A
+            uk=jnp.sum(UdS*kf,axis=1,keepdims=True)
+            tot=jnp.sum(uk,axis=0,keepdims=True)+G*jnp.sum(jnp.sum(S0*dSv,axis=1,keepdims=True),axis=0,keepdims=True)
+            dgc=jnp.sum(dOS*qf-dRS*kf+X,axis=1,keepdims=True)-uk
+            dbc_ref[rows(c),h:h+1]=db
+            dgc_ref[rows(c),h:h+1]=dgc+jnp.where(last,tot,0.0)
+            dgr_ref[c,h:h+1,:]=jnp.sum(X,axis=0,keepdims=True)
+
+def specs(C,H,DK,DV,NC,rev,n):
+    ix=(lambda s: n-1-s) if rev else (lambda s: s)
+    r=lambda w: pl.BlockSpec((NC*C,w),lambda s:(ix(s),0))
+    t=lambda a,w: pl.BlockSpec((NC,a,w),lambda s:(ix(s),0,0))
+    return r,t
+def delta_fwd(q,k,v,bc,gc,gr,NC=1):
+    L,HK=q.shape; H=bc.shape[1]; DK=HK//H; DV=v.shape[1]//H; C=CHUNK; n=L//C//NC
+    r,t=specs(C,H,DK,DV,NC,False,n)
+    return pl.pallas_call(functools.partial(fwd_kernel,H,DK,DV,NC),grid=(n,),
+        in_specs=[r(HK),r(HK),r(H*DV),r(H),r(H),t(H,C)],
+        out_specs=[r(H*DV),r(H*DV),r(H*C),t(H*DK,DV)],
+        out_shape=[jax.ShapeDtypeStruct((L,H*DV),F32),jax.ShapeDtypeStruct((L,H*DV),F32),jax.ShapeDtypeStruct((L,H*C),F32),jax.ShapeDtypeStruct((L//C,H*DK,DV),F32)],
+        scratch_shapes=[pltpu.VMEM((H*DK,DV),F32)],
+        compiler_params=pltpu.CompilerParams(vmem_limit_bytes=56*2**20),name="delta_fwd")(q,k,v,bc,gc,gr)
+def delta_bwd(q,k,v,bc,gc,gr,u,tt,s,do,NC=1):
+    L,HK=q.shape; H=bc.shape[1]; DK=HK//H; DV=v.shape[1]//H; C=CHUNK; n=L//C//NC
+    r,t=specs(C,H,DK,DV,NC,True,n)
+    return pl.pallas_call(functools.partial(bwd_kernel,H,DK,DV,NC),grid=(n,),
+        in_specs=[r(HK),r(HK),r(H*DV),r(H),r(H),t(H,C),r(H*DV),r(H*C),t(H*DK,DV),r(H*DV)],
+        out_specs=[r(HK),r(HK),r(H*DV),r(H),r(H),t(H,C)],
+        out_shape=[jax.ShapeDtypeStruct((L,HK),F32),jax.ShapeDtypeStruct((L,HK),F32),jax.ShapeDtypeStruct((L,H*DV),F32),jax.ShapeDtypeStruct((L,H),F32),jax.ShapeDtypeStruct((L,H),F32),jax.ShapeDtypeStruct((L//C,H,C),F32)],
+        scratch_shapes=[pltpu.VMEM((H*DK,DV),F32)],
+        compiler_params=pltpu.CompilerParams(vmem_limit_bytes=56*2**20),name="delta_bwd")(q,k,v,bc,gc,gr,u,tt,s,do)
 
 
 def causal_conv(projected, kernel):
@@ -19,90 +166,42 @@
 
 def unit_heads(mixed, heads, factor):
     shaped = mixed.reshape(mixed.shape[0], heads, -1)
-    return shaped * lax.rsqrt(jnp.sum(shaped * shaped, axis=-1, keepdims=True) + 1e-06) * factor
-
-
-def block_step(running_state, items):
-    query_block, key_block, value_blk, beta_blk, decay_blk = items
-    width = decay_blk.shape[1]
-    highest_precision = lax.Precision.HIGHEST
-    cumul = jnp.cumsum(decay_blk, axis=1)
-    order = jnp.arange(width)
-    lower = order[:, None] >= order[None, :]
-    strict = order[:, None] > order[None, :]
-    spread = cumul[:, :, None] - cumul[:, None, :]
-    decay = jnp.where(lower, jnp.exp(jnp.where(lower, spread, 0.0)), 0.0)
-    inner = jnp.einsum("htk,hsk->hts", key_block, key_block, precision=highest_precision)
-    coupling = jnp.where(strict, beta_blk[:, :, None] * inner * decay, 0.0)
-    system = jnp.eye(width, dtype=jnp.float32) + coupling
-    opening_state = jnp.exp(cumul)
-    carried_state = jnp.einsum(
-        "zoa,zal->zol", key_block, running_state, precision=highest_precision
-    )
-    driving = beta_blk[:, :, None] * (value_blk - opening_state[:, :, None] * carried_state)
-    solved_system = jax.scipy.linalg.solve_triangular(
-        system, driving, lower=True, unit_diagonal=True
-    )
-    scores = jnp.einsum("htk,hsk->hts", query_block, key_block, precision=highest_precision) * decay
-    output_rows = opening_state[:, :, None] * jnp.einsum(
-        "zoa,zal->zol", query_block, running_state, precision=highest_precision
-    )
-    output_rows = output_rows + jnp.einsum(
-        "hts,hsv->htv", scores, solved_system, precision=highest_precision
-    )
-    closing_state = jnp.exp(cumul[:, -1:] - cumul)
-    running_state = jnp.exp(cumul[:, -1])[:, None, None] * running_state
-    running_state = running_state + jnp.einsum(
-        "cif,cie->cfe",
-        key_block * closing_state[:, :, None],
-        solved_system,
-        precision=highest_precision,
-    )
-    return (running_state, output_rows)
-
-
-def delta_rule(query, key, value, beta, log_decay):
-    length, heads, key_size = query.shape
-    value_size = value.shape[2]
-    blocks = length // SPAN
-
-    def arrange(array):
-        return jnp.moveaxis(array.reshape((blocks, SPAN) + array.shape[1:]), 2, 1)
-
-    items = (arrange(query), arrange(key), arrange(value), arrange(beta), arrange(log_decay))
-    running_state = jnp.zeros((heads, key_size, value_size), jnp.float32)
-    _, output_rows = lax.scan(jax.checkpoint(block_step), running_state, items)
-    return jnp.moveaxis(output_rows, 1, 2).reshape(length, heads, value_size)
+    scaled = shaped * lax.rsqrt(jnp.sum(shaped * shaped, axis=-1, keepdims=True) + 1e-06) * factor
+    return scaled.reshape(mixed.shape)
 
 
 def mixer_front(query_proj, key_proj, value_proj, conv_query, conv_key, conv_value):
     heads = query_proj.shape[1] // DK
-    length = query_proj.shape[0]
     query = unit_heads(jax.nn.silu(causal_conv(query_proj, conv_query)), heads, DK ** (-0.5))
     key = unit_heads(jax.nn.silu(causal_conv(key_proj, conv_key)), heads, 1.0)
-    value = jax.nn.silu(causal_conv(value_proj, conv_value)).reshape(length, heads, -1)
+    value = jax.nn.silu(causal_conv(value_proj, conv_value))
     return (query, key, value)
 
 
-def mixer_rest(
-    query, key, value, gate_proj, decay_proj, beta_proj, decay_log, decay_bias, norm_heads
-):
-    length = query.shape[0]
-    heads = query.shape[1]
+def decay_terms(decay_proj, beta_proj, decay_log, decay_bias):
     beta = jax.nn.sigmoid(beta_proj)
     log_decay = -jnp.exp(decay_log) * jax.nn.softplus(decay_proj + decay_bias)
-    heads_out = delta_rule(query, key, value, beta, log_decay)
+    return (beta, running_sum(log_decay))
+
+
+def running_sum(values):
+    length, heads = values.shape
+    blocks = values.reshape(length // CHUNK, CHUNK, heads)
+    order = jnp.arange(CHUNK)
+    ones = (order[:, None] >= order[None, :]).astype(jnp.float32)
+    return jnp.einsum("ts,bsh->bth", ones, blocks, precision=lax.Precision.HIGHEST).reshape(
+        length, heads
+    )
+
+
+def gated_heads(heads_out, gate_proj, norm_heads):
+    length = heads_out.shape[0]
+    shaped = heads_out.reshape(length, -1, norm_heads.shape[0])
     scaled = (
-        heads_out
-        * lax.rsqrt(jnp.mean(heads_out * heads_out, axis=-1, keepdims=True) + 1e-05)
-        * norm_heads
-    )
-    gated = scaled * jax.nn.silu(gate_proj.reshape(length, heads, -1))
+        shaped * lax.rsqrt(jnp.mean(shaped * shaped, axis=-1, keepdims=True) + 1e-05) * norm_heads
+    )
+    gated = scaled * jax.nn.silu(gate_proj.reshape(shaped.shape))
     return gated.reshape(length, -1)
-
-
-def rounded_copy(values):
-    return lax.optimization_barrier(values.astype(jnp.bfloat16)).astype(jnp.float32)
 
 
 def spread_rows(normed):
@@ -161,6 +260,12 @@
     return lax.dot_general(
         left, right, (((1,), (1,)), ((), ())), preferred_element_type=jnp.float32
     )
+
+
+def own_rows(grad, dim):
+    return lax.psum_scatter(
+        grad.astype(jnp.bfloat16), "dp", scatter_dimension=dim, tiled=True
+    ).astype(jnp.float32)
 
 
 def norm_back(values, inverse, gain, incoming):
@@ -247,21 +352,14 @@
         conv_key_here,
         conv_value_here,
     )
-    query_low = rounded_copy(front_values[0])
-    key_low = rounded_copy(front_values[1])
-    value_low = rounded_copy(front_values[2])
-    mixer_value, back_pullback = jax.vjp(
-        mixer_rest,
-        query_low,
-        key_low,
-        value_low,
-        gate_proj,
-        decay_proj,
-        beta_proj,
-        decay_log_here,
-        decay_bias_here,
-        norm_heads,
-    )
+    query_low, key_low, value_low = (part.astype(jnp.bfloat16) for part in front_values)
+    (beta, running), decay_pullback = jax.vjp(
+        decay_terms, decay_proj, beta_proj, decay_log_here, decay_bias_here
+    )
+    running_rows = jnp.moveaxis(running.reshape(-1, CHUNK, heads_here), 1, 2)
+    delta_args = (query_low, key_low, value_low, beta, running, running_rows)
+    heads_out, written, inverse, states = delta_fwd(*delta_args, NC=2)
+    mixer_value, gated_pullback = jax.vjp(gated_heads, heads_out, gate_proj, norm_heads)
     mixer = mixer_value.astype(jnp.bfloat16)
     branch_attn = branch_rows(mixer, output_full)
     stream = stream_in + branch_attn
@@ -283,7 +381,6 @@
     stat_sums = lax.psum((sum_inputs, sum_attn, sum_ffn, count_here), ("dp", "tensor"))
     grad_out = valid * cotangent.astype(jnp.float32)
     grad_ffn = spread_grads(grad_out.astype(jnp.bfloat16))
-    gate_ffn, up_ffn, down_ffn = fetch_ffn(w_ffn_gate, w_ffn_up, w_ffn_down)
     grad_hidden = times_transposed(grad_ffn, down_ffn)
     grad_gate_in = (grad_hidden * ffn_up * sigma * (1.0 + ffn_gate * (1.0 - sigma))).astype(
         jnp.bfloat16
@@ -294,26 +391,28 @@
     grad_gate_weight = contract_rows(full_mid, grad_gate_in)
     grad_up_weight = contract_rows(full_mid, grad_up_in)
     owned_gate, owned_up, owned_down = (
-        lax.psum_scatter(grad_gate_weight, "dp", scatter_dimension=0, tiled=True),
-        lax.psum_scatter(grad_up_weight, "dp", scatter_dimension=0, tiled=True),
-        lax.psum_scatter(grad_down, "dp", scatter_dimension=1, tiled=True),
+        own_rows(grad_gate_weight, 0),
+        own_rows(grad_up_weight, 0),
+        own_rows(grad_down, 1),
     )
     grad_through, grad_norm_ffn = norm_back(stream, inverse_mid, norm_ffn, grad_mid)
     grad_stream = grad_out + grad_through
     grad_attn = spread_grads(grad_stream.astype(jnp.bfloat16))
-    query_full, key_full, value_full, gate_full, decay_full, beta_full, output_full = (
-        fetch_attention(w_query, w_key, w_value, w_out_gate, w_decay, w_beta, w_output)
-    )
     grad_output_weight = contract_rows(mixer, grad_attn)
     grad_mixer = times_transposed(grad_attn, output_full)
-    rest_grads = back_pullback(grad_mixer)
-    front_grads = front_pullback((rest_grads[0], rest_grads[1], rest_grads[2]))
+    grad_heads, grad_gate, heads_gain_grad = gated_pullback(grad_mixer)
+    grad_query, grad_key, grad_value, grad_beta, grad_run, grad_run_rows = delta_bwd(
+        *delta_args, written, inverse, states, grad_heads, NC=1
+    )
+    grad_run = grad_run - jnp.moveaxis(grad_run_rows, 1, 2).reshape(grad_run.shape)
+    grad_decay, grad_beta_in, grad_decay_log, grad_decay_bias = decay_pullback((grad_beta, grad_run))
+    front_grads = front_pullback((grad_query, grad_key, grad_value))
     grad_query_proj = front_grads[0].astype(jnp.bfloat16)
     grad_key_proj = front_grads[1].astype(jnp.bfloat16)
     grad_value_proj = front_grads[2].astype(jnp.bfloat16)
-    grad_gate_proj = rest_grads[3].astype(jnp.bfloat16)
-    grad_decay_proj = rest_grads[4].astype(jnp.bfloat16)
-    grad_beta_proj = rest_grads[5].astype(jnp.bfloat16)
+    grad_gate_proj = grad_gate.astype(jnp.bfloat16)
+    grad_decay_proj = grad_decay.astype(jnp.bfloat16)
+    grad_beta_proj = grad_beta_in.astype(jnp.bfloat16)
     grad_query_weight = contract_rows(full_in, grad_query_proj)
     grad_key_weight = contract_rows(full_in, grad_key_proj)
     grad_value_weight = contract_rows(full_in, grad_value_proj)
@@ -332,22 +431,21 @@
         rows,
     )
     owned_query, owned_key, owned_value, owned_out_gate, owned_decay, owned_beta, owned_output = (
-        lax.psum_scatter(grad_query_weight, "dp", scatter_dimension=0, tiled=True),
-        lax.psum_scatter(grad_key_weight, "dp", scatter_dimension=0, tiled=True),
-        lax.psum_scatter(grad_value_weight, "dp", scatter_dimension=0, tiled=True),
-        lax.psum_scatter(grad_gate_weight_attn, "dp", scatter_dimension=0, tiled=True),
-        lax.psum_scatter(grad_decay_weight, "dp", scatter_dimension=0, tiled=True),
-        lax.psum_scatter(grad_beta_weight, "dp", scatter_dimension=0, tiled=True),
-        lax.psum_scatter(grad_output_weight, "dp", scatter_dimension=1, tiled=True),
+        own_rows(grad_query_weight, 0),
+        own_rows(grad_key_weight, 0),
+        own_rows(grad_value_weight, 0),
+        own_rows(grad_gate_weight_attn, 0),
+        own_rows(grad_decay_weight, 0),
+        own_rows(grad_beta_weight, 0),
+        own_rows(grad_output_weight, 1),
     )
     grad_through_in, grad_norm_attn = norm_back(stream_in, inverse_in, norm_attn, grad_normed)
     grad_inputs = grad_stream + grad_through_in
     conv_query_grad = place_slice(front_grads[3], conv_query, tensor_rank, 1)
     conv_key_grad = place_slice(front_grads[4], conv_key, tensor_rank, 1)
     conv_value_grad = place_slice(front_grads[5], conv_value, tensor_rank, 1)
-    decay_log_grad = place_slice(rest_grads[6], decay_log, tensor_rank, 0)
-    decay_bias_grad = place_slice(rest_grads[7], decay_bias, tensor_rank, 0)
-    heads_gain_grad = rest_grads[8]
+    decay_log_grad = place_slice(grad_decay_log, decay_log, tensor_rank, 0)
+    decay_bias_grad = place_slice(grad_decay_bias, decay_bias, tensor_rank, 0)
     (
         total_attn_gain,
         total_ffn_gain,

time: 3660 us -> 2130 us (0.58)
  other arithmetic: 775 us -> 140 us
  waiting for transfers between devices: 1980 us -> 1460 us
  matrix products: 595 us -> 244 us
  local copies, waits for them, and re-layouts: 184 us -> 85.8 us
  Pallas kernels: 0 us -> 73.1 us
    reduce_scatter x8, waiting for transfers between devices: 1180 us -> 471 us  [own_rows(): lax.psum_scatter(grad.astype(jnp.bfloat16), 'dp', scatter_dimension=dim,...]
    another operation x211 -> x3, other arithmetic: 660 us -> 12.8 us  [the longest x128 634 us: block_step(): jax.scipy.linalg.solve_triangular(system, driving, lower=True, unit_diago...]
    dot_general x368 -> x2, matrix products: 291 us -> 0.42 us  [running_sum(): jnp.einsum('ts,bsh->bth', ones, blocks, precision=lax.Precision.HIGHEST)]
    unnamed x29, waiting for transfers between devices: 5.03 us -> 131 us
    pallas_call x0 -> x2, Pallas kernels: none -> 73.1 us  [the longest x1 42.9 us: delta_bwd(): pl.pallas_call(functools.partial(bwd_kernel, H, DK, DV, NC), grid=(n,), i...]
    reduce_scatter x2, waiting for transfers between devices: 69.3 us -> 141 us  [branch_rows(): lax.psum_scatter(jnp.dot(left, right, preferred_element_type=jnp.float32)...]
    squeeze x64 -> x0, local copies, waits for them, and re-layouts: 61.6 us -> none  [delta_rule(): _, output_rows = lax.scan(jax.checkpoint(block_step), running_state, items)]
    psum x1, waiting for transfers between devices: 123 us -> 70.8 us  [shards(): lax.psum((grad_norm_attn, grad_norm_ffn, heads_gain_grad, conv_query_grad...]
  transfers between devices with their start and end apart: 27 -> 27, of which waited for: 21 -> 23; matrix products, arithmetic and copies ran while one was open for 22% -> 19% of each run, Pallas kernels for 0% -> 3%
where the time goes in v1:
time: 2130 us; the launch traced here: 2120 us
  waiting for transfers between devices  1460 us (69%)
  matrix products  244 us (11%)
  other arithmetic  140 us (7%)
  blocking collectives  95.4 us (4%)
  local copies, waits for them, and re-layouts  85.8 us (4%)
  Pallas kernels  73.1 us (3%)
    reduce_scatter x8, waiting for transfers between devices, own_rows(): lax.psum_scatter(grad.astype(jnp.bfloat16), 'dp', scatter_dimension=dim,...  471 us
    reduce_scatter x2, waiting for transfers between devices, back_rows(): return lax.psum_scatter(total, 'tensor', scatter_dimension=0, tiled=True)  144 us
    reduce_scatter x2, waiting for transfers between devices, branch_rows(): lax.psum_scatter(jnp.dot(left, right, preferred_element_type=jnp.float32)...  141 us
    unnamed x29, waiting for transfers between devices  131 us
    all_gather x1, waiting for transfers between devices, fetch_ffn(): lax.all_gather(w_ffn_down, 'dp', axis=1, tiled=True)  95.7 us
    all_gather x1, waiting for transfers between devices, fetch_ffn(): lax.all_gather(w_ffn_gate, 'dp', axis=0, tiled=True)  88.7 us
    all_gather x1, waiting for transfers between devices, fetch_ffn(): lax.all_gather(w_ffn_up, 'dp', axis=0, tiled=True)  82.9 us
    psum x1, waiting for transfers between devices, shards(): lax.psum((grad_norm_attn, grad_norm_ffn, heads_gain_grad, conv_query_grad...  70.8 us
  transfers between devices with their start and end apart: 27, of which 23 were waited for; matrix products, arithmetic and copies ran while one was open for 19% of the time, Pallas kernels for 3%

profile of v1, /device:TPU:0, one launch (start us, length us, event | category | flops | bytes accessed | tf_op | source)
XLA Modules:
  0.0 2119.5 jit_solution(6542487985469558620)
XLA Ops:
  15.2 27.8 %all_gather.46 = bf16[2048,4]{0,1:T(4,128)(2,1)S(1)} all-gather(bf16[256,4]{0,1:T(4,128)(2,1)S(1)} %copy-done.84), channel_id=1, replica_groups=mesh['dp'=8,'tensor'=4] {'dp'}, dimensions={0}, use_global_device_ids=true | all-gather | bytes 18432 | tf_op jit(solution)/shard_map/all_gather | solution.py:222
  43.0 26.2 %all_gather.47 = bf16[2048,4]{0,1:T(4,128)(2,1)S(1)} all-gather(bf16[256,4]{0,1:T(4,128)(2,1)S(1)} %copy-done.85), channel_id=1, replica_groups=mesh['dp'=8,'tensor'=4] {'dp'}, dimensions={0}, use_global_device_ids=true | all-gather | bytes 18432 | tf_op jit(solution)/shard_map/all_gather | solution.py:221
  71.5 26.3 %all-gather.13.cloned.1.call-done = bf16[1024,2048]{1,0:T(8,128)(2,1)} async-done(((bf16[256,2048]{1,0:T(8,128)(2,1)}), bf16[1024,2048]{1,0:T(8,128)(2,1)}) %all-gather.13.cloned.1.call-update) | async-done | bytes 4194320 | tf_op jit(solution)/shard_map/all_gather | solution.py:208
  111.0 38.3 %all-gather.17.cloned.1.call-done = bf16[2048,512]{1,0:T(8,128)(2,1)} async-done(((bf16[256,512]{1,0:T(8,128)(2,1)}), bf16[2048,512]{1,0:T(8,128)(2,1)}) %all-gather.17.cloned.1.call-update) | async-done | bytes 2097168 | tf_op jit(solution)/shard_map/all_gather | solution.py:218
  182.0 41.2 %all-gather.21.cloned.1.call-done = bf16[2048,1024]{1,0:T(8,128)(2,1)} async-done(((bf16[256,1024]{1,0:T(8,128)(2,1)}), bf16[2048,1024]{1,0:T(8,128)(2,1)}) %all-gather.21.cloned.1.call-update) | async-done | bytes 4194320 | tf_op jit(solution)/shard_map/all_gather | solution.py:220
  238.6 58.2 %all-gather.19.cloned.1.call-done = bf16[2048,1024]{1,0:T(8,128)(2,1)} async-done(((bf16[256,1024]{1,0:T(8,128)(2,1)}), bf16[2048,1024]{1,0:T(8,128)(2,1)}) %all-gather.19.cloned.1.call-update) | async-done | bytes 4194320 | tf_op jit(solution)/shard_map/all_gather | solution.py:219
  308.7 30.3 %delta_fwd.1 = (f32[1024,1024]{1,0:T(8,128)}, f32[1024,1024]{1,0:T(8,128)}, f32[1024,512]{1,0:T(8,128)}, f32[8,512,256]{2,1,0:T(8,128)}) custom-call(bf16[1024,512]{1,0:T(8,128)(2,1)} %fusion.30.q_ref, bf16[1024,512]{1,0:T(8,128)(2,1)} %fusion.28.k_ref, bf16[1024,1024]{1,0:T(8,128)(2,1)} %get-tuple-element.82.v_ref, f32[1024,4]{1,0:T(8,128)} %fusion.38.bc_ref, ...), custom_call_target="tpu_custom_call" | custom-call | tf_op jit(solution)/shard_map/delta_fwd/pallas_call | solution.py:140
  358.4 14.7 all-gather.23.cloned.1.call-done
  382.8 68.4 %reduce-scatter.19.cloned.1.call-done = f32[256,2048]{1,0:T(8,128)} async-done(((f32[1024,2048]{1,0:T(8,128)}), f32[256,2048]{1,0:T(8,128)}) %reduce-scatter.19.cloned.1.call-update) | async-done | bytes 2097168 | tf_op jit(solution)/shard_map/reduce_scatter | solution.py:236
  457.5 88.7 %all-gather.27.cloned.1.call-done = bf16[2048,1408]{1,0:T(8,128)(2,1)} async-done(((bf16[256,1408]{1,0:T(8,128)(2,1)}), bf16[2048,1408]{1,0:T(8,128)(2,1)}) %all-gather.27.cloned.1.call-update) | async-done | bytes 5767184 | tf_op jit(solution)/shard_map/all_gather | solution.py:229
  546.2 34.9 %all-gather.25.cloned.1.call-done = bf16[1024,2048]{1,0:T(8,128)(2,1)} async-done(((bf16[256,2048]{1,0:T(8,128)(2,1)}), bf16[1024,2048]{1,0:T(8,128)(2,1)}) %all-gather.25.cloned.1.call-update) | async-done | bytes 4194320 | tf_op jit(solution)/shard_map/all_gather | solution.py:208
  581.1 12.1 fusion.71
  593.2 82.9 %all-gather.29.cloned.1.call-done = bf16[2048,1408]{1,0:T(8,128)(2,1)} async-done(((bf16[256,1408]{1,0:T(8,128)(2,1)}), bf16[2048,1408]{1,0:T(8,128)(2,1)}) %all-gather.29.cloned.1.call-update) | async-done | bytes 5767184 | tf_op jit(solution)/shard_map/all_gather | solution.py:230
  676.1 11.7 fusion.72
  687.7 23.3 %all-gather.33.cloned.1.call-done = bf16[1024,2048]{1,0:T(8,128)(2,1)} async-done(((bf16[256,2048]{1,0:T(8,128)(2,1)}), bf16[1024,2048]{1,0:T(8,128)(2,1)}) %all-gather.33.cloned.1.call-update) | async-done | bytes 4194320 | tf_op jit(solution)/shard_map/all_gather | solution.py:212
  711.0 95.7 %all-gather.31.cloned.1.call-done = bf16[1408,2048]{1,0:T(8,128)(2,1)} async-done(((bf16[1408,256]{1,0:T(8,128)(2,1)}), bf16[1408,2048]{1,0:T(8,128)(2,1)}) %all-gather.31.cloned.1.call-update) | async-done | bytes 5767184 | tf_op jit(solution)/shard_map/all_gather | solution.py:231
  806.7 15.6 multiply_convert_fusion
  842.3 69.8 %reduce-scatter.23.cloned.1.call-done = f32[256,2048]{1,0:T(8,128)} async-done(((f32[1024,2048]{1,0:T(8,128)}), f32[256,2048]{1,0:T(8,128)}) %reduce-scatter.23.cloned.1.call-update) | async-done | bytes 2097168 | tf_op jit(solution)/shard_map/reduce_scatter | solution.py:250
  999.1 42.9 %delta_bwd.1 = (f32[1024,512]{1,0:T(8,128)}, f32[1024,512]{1,0:T(8,128)}, f32[1024,1024]{1,0:T(8,128)}, f32[1024,4]{1,0:T(8,128)}, f32[1024,4]{1,0:T(8,128)}, /*index=5*/f32[8,4,128]{2,1,0:T(4,128)}) custom-call(bf16[1024,512]{1,0:T(8,128)(2,1)} %fusion.30.q_ref, bf16[1024,512]{1,0:T(8,128)(2,1)} %fusion.28.k_ref, ...), custom_call_target="tpu_custom_call" | custom-call | tf_op jit(solution)/shard_map/delta_bwd/pallas_call | solution.py:149
  1203.0 18.4 add_add_fusion
  1226.9 65.9 %reduce-scatter.41.cloned.1.call-done = bf16[1408,256]{1,0:T(8,128)(2,1)} async-done(((bf16[1408,2048]{1,0:T(8,128)(2,1)}), bf16[1408,256]{1,0:T(8,128)(2,1)}) %reduce-scatter.41.cloned.1.call-update) | async-done | bytes 720912 | tf_op jit(solution)/shard_map/reduce_scatter | solution.py:266
  1296.2 62.2 %reduce-scatter.43.cloned.1.call-done = bf16[256,4]{1,0:T(8,128)(2,1)} async-done(((bf16[2048,4]{1,0:T(8,128)(2,1)}), bf16[256,4]{1,0:T(8,128)(2,1)}) %reduce-scatter.43.cloned.1.call-update) | async-done | bytes 2064
  1359.9 63.6 %reduce-scatter.45.cloned.1.call-done = bf16[256,4]{1,0:T(8,128)(2,1)} async-done(((bf16[2048,4]{1,0:T(8,128)(2,1)}), bf16[256,4]{1,0:T(8,128)(2,1)}) %reduce-scatter.45.cloned.1.call-update) | async-done | bytes 2064
  1425.0 68.6 %reduce-scatter.27.cloned.1.call-done = bf16[256,512]{1,0:T(8,128)(2,1)} async-done(((bf16[2048,512]{1,0:T(8,128)(2,1)}), bf16[256,512]{1,0:T(8,128)(2,1)}) %reduce-scatter.27.cloned.1.call-update) | async-done | bytes 262160 | tf_op jit(solution)/shard_map/reduce_scatter | solution.py:266
  1495.4 68.4 %reduce-scatter.29.cloned.1.call-done = bf16[256,512]{1,0:T(8,128)(2,1)} async-done(((bf16[2048,512]{1,0:T(8,128)(2,1)}), bf16[256,512]{1,0:T(8,128)(2,1)}) %reduce-scatter.29.cloned.1.call-update) | async-done | bytes 262160 | tf_op jit(solution)/shard_map/reduce_scatter | solution.py:266
  1565.7 88.7 %reduce-scatter.31.cloned.1.call-done = bf16[256,1024]{1,0:T(8,128)(2,1)} async-done(((bf16[2048,1024]{1,0:T(8,128)(2,1)}), bf16[256,1024]{1,0:T(8,128)(2,1)}) %reduce-scatter.31.cloned.1.call-update) | async-done | bytes 524304 | tf_op jit(solution)/shard_map/reduce_scatter | solution.py:266
  1656.6 89.7 %reduce-scatter.33.cloned.1.call-done = bf16[256,1024]{1,0:T(8,128)(2,1)} async-done(((bf16[2048,1024]{1,0:T(8,128)(2,1)}), bf16[256,1024]{1,0:T(8,128)(2,1)}) %reduce-scatter.33.cloned.1.call-update) | async-done | bytes 524304 | tf_op jit(solution)/shard_map/reduce_scatter | solution.py:266
  1748.4 89.6 %reduce-scatter.35.cloned.1.call-done = bf16[1024,256]{1,0:T(8,128)(2,1)} async-done(((bf16[1024,2048]{1,0:T(8,128)(2,1)}), bf16[1024,256]{1,0:T(8,128)(2,1)}) %reduce-scatter.35.cloned.1.call-update) | async-done | bytes 524304 | tf_op jit(solution)/shard_map/reduce_scatter | solution.py:266
  1840.1 72.2 %reduce-scatter.21.cloned.1.call-done = f32[256,2048]{1,0:T(8,128)} async-done(((f32[1024,2048]{1,0:T(8,128)}), f32[256,2048]{1,0:T(8,128)}) %reduce-scatter.21.cloned.1.call-update) | async-done | bytes 2097168 | tf_op jit(solution)/shard_map/reduce_scatter | solution.py:236
  1912.3 74.2 %reduce-scatter.25.cloned.1.call-done = f32[256,2048]{1,0:T(8,128)} async-done(((f32[1024,2048]{1,0:T(8,128)}), f32[256,2048]{1,0:T(8,128)}) %reduce-scatter.25.cloned.1.call-update) | async-done | bytes 2097168 | tf_op jit(solution)/shard_map/reduce_scatter | solution.py:250
  1991.5 41.3 %all-reduce.32 = (f32[1]{0:T(128)}, f32[1]{0:T(128)}, f32[1]{0:T(128)}, f32[]{:T(128)}, f32[2048]{0:T(1024)}, /*index=5*/f32[2048]{0:T(1024)}, f32[256]{0:T(256)...) all-reduce(f32[1]{0:T(128)} %bitcast.18, ...), channel_id=1, replica_groups=mesh['dp'=8,'tensor'=4] {'dp','tensor'}, use_global_device_ids=true, to_apply=%region_12.13 | all-reduce | flops 20772 | bytes 166176 | tf_op jit(solution)/shard_map/psum | solution.py:381
  2040.2 70.8 %all-reduce.31.cloned.1.call-done = f32[4,4096]{1,0:T(4,128)} async-done(((f32[4,4096]{1,0:T(4,128)}), f32[4,4096]{1,0:T(4,128)}) %all-reduce.31.cloned.1.call-update) | async-done | bytes 65552 | tf_op jit(solution)/shard_map/psum | solution.py:458
  (400 shorter events, 419.8 us)
Async XLA Ops:
  7.2 64.3 %all-gather.15.cloned.1.call-start = ((), (), s32[]{:S(2)}) async-start(), calls=%async_computation.15 | async-start | bytes 2359296 | tf_op jit(solution)/shard_map/all_gather | solution.py:217
  7.9 89.9 %all-gather.13.cloned.1.call-start = ((), (), s32[]{:S(2)}) async-start(), calls=%async_computation.14 | async-start | bytes 5242880 | tf_op jit(solution)/shard_map/all_gather | solution.py:208
  12.7 136.6 %all-gather.17.cloned.1.call-start = ((), (), s32[]{:S(2)}) async-start(), calls=%async_computation.16 | async-start | bytes 2359296 | tf_op jit(solution)/shard_map/all_gather | solution.py:218
  13.4 209.8 %all-gather.21.cloned.1.call-start = ((), (), s32[]{:S(2)}) async-start(), calls=%async_computation.18 | async-start | bytes 4718592 | tf_op jit(solution)/shard_map/all_gather | solution.py:220
  14.0 282.9 %all-gather.19.cloned.1.call-start = ((), (), s32[]{:S(2)}) async-start(), calls=%async_computation.17 | async-start | bytes 4718592 | tf_op jit(solution)/shard_map/all_gather | solution.py:219
  14.6 358.5 %all-gather.23.cloned.1.call-start = ((), (), s32[]{:S(2)}) async-start(), calls=%async_computation.19 | async-start | bytes 4718592 | tf_op jit(solution)/shard_map/all_gather | solution.py:223
  15.1 436.0 %reduce-scatter.19.cloned.1.call-start = ((), (), s32[]{:S(2)}) async-start(), calls=%async_computation.20 | async-start | bytes 10485760 | tf_op jit(solution)/shard_map/reduce_scatter | solution.py:236
  382.0 164.2 %all-gather.27.cloned.1.call-start = ((), (), s32[]{:S(2)}) async-start(), calls=%async_computation.22 | async-start | bytes 6488064 | tf_op jit(solution)/shard_map/all_gather | solution.py:229
  382.7 198.4 %all-gather.25.cloned.1.call-start = ((), (), s32[]{:S(2)}) async-start(), calls=%async_computation.21 | async-start | bytes 5242880 | tf_op jit(solution)/shard_map/all_gather | solution.py:208
  453.1 462.0 %copy-start.5 = (f32[256,2048]{1,0:T(8,128)}, f32[256,2048]{1,0:T(8,128)S(1)}, u32[]{:S(2)}) copy-start(f32[256,2048]{1,0:T(8,128)S(1)} %get-tuple-element.79) | copy-start | bytes 6291460
  454.4 221.7 %all-gather.29.cloned.1.call-start = ((), (), s32[]{:S(2)}) async-start(), calls=%async_computation.23 | async-start | bytes 6488064 | tf_op jit(solution)/shard_map/all_gather | solution.py:230
  454.9 256.0 %all-gather.33.cloned.1.call-start = ((), (), s32[]{:S(2)}) async-start(), calls=%async_computation.26 | async-start | bytes 5242880 | tf_op jit(solution)/shard_map/all_gather | solution.py:212
  455.7 459.4 %copy-start.79 = (f32[256]{0:T(256)}, f32[256]{0:T(256)S(1)}, u32[]{:S(2)}) copy-start(f32[256]{0:T(256)S(1)} %compare_convert_fusion) | copy-start | bytes 3076
  456.9 349.8 %all-gather.31.cloned.1.call-start = ((), (), s32[]{:S(2)}) async-start(), calls=%async_computation.24 | async-start | bytes 6488064 | tf_op jit(solution)/shard_map/all_gather | solution.py:231
  457.5 454.7 %reduce-scatter.23.cloned.1.call-start = ((), (), s32[]{:S(2)}) async-start(), calls=%async_computation.27 | async-start | bytes 10485760 | tf_op jit(solution)/shard_map/reduce_scatter | solution.py:250
  842.1 117.5 %all-gather.35.cloned.1.call-start = ((), (), s32[]{:S(2)}) async-start(), calls=%async_computation.28 | async-start | bytes 5242880 | tf_op jit(solution)/shard_map/all_gather | solution.py:212
  917.7 304.6 %reduce-scatter.37.cloned.1.call-start = ((), (), s32[]{:S(2)}) async-start(), calls=%async_computation.36 | async-start | bytes 6488064 | tf_op jit(solution)/shard_map/reduce_scatter | solution.py:266
  928.8 295.8 %reduce-scatter.39.cloned.1.call-start = ((), (), s32[]{:S(2)}) async-start(), calls=%async_computation.37 | async-start | bytes 6488064 | tf_op jit(solution)/shard_map/reduce_scatter | solution.py:266
  941.5 351.3 %reduce-scatter.41.cloned.1.call-start = ((), (), s32[]{:S(2)}) async-start(), calls=%async_computation.38 | async-start | bytes 6488064 | tf_op jit(solution)/shard_map/reduce_scatter | solution.py:266
  954.0 404.4 %reduce-scatter.43.cloned.1.call-start = ((), (), s32[]{:S(2)}) async-start(), calls=%async_computation.39 | async-start | bytes 589824
  1069.5 354.0 %reduce-scatter.45.cloned.1.call-start = ((), (), s32[]{:S(2)}) async-start(), calls=%async_computation.40 | async-start | bytes 589824
  1073.5 420.2 %reduce-scatter.27.cloned.1.call-start = ((), (), s32[]{:S(2)}) async-start(), calls=%async_computation.30 | async-start | bytes 2359296 | tf_op jit(solution)/shard_map/reduce_scatter | solution.py:266
  1083.0 480.8 %reduce-scatter.29.cloned.1.call-start = ((), (), s32[]{:S(2)}) async-start(), calls=%async_computation.31 | async-start | bytes 2359296 | tf_op jit(solution)/shard_map/reduce_scatter | solution.py:266
  1109.2 545.2 %reduce-scatter.31.cloned.1.call-start = ((), (), s32[]{:S(2)}) async-start(), calls=%async_computation.32 | async-start | bytes 4718592 | tf_op jit(solution)/shard_map/reduce_scatter | solution.py:266
  1140.8 605.4 %reduce-scatter.33.cloned.1.call-start = ((), (), s32[]{:S(2)}) async-start(), calls=%async_computation.33 | async-start | bytes 4718592 | tf_op jit(solution)/shard_map/reduce_scatter | solution.py:266
  1150.8 687.2 %reduce-scatter.35.cloned.1.call-start = ((), (), s32[]{:S(2)}) async-start(), calls=%async_computation.34 | async-start | bytes 4718592 | tf_op jit(solution)/shard_map/reduce_scatter | solution.py:266
  1160.9 751.5 %reduce-scatter.21.cloned.1.call-start = ((), (), s32[]{:S(2)}) async-start(), calls=%async_computation.25 | async-start | bytes 10485760 | tf_op jit(solution)/shard_map/reduce_scatter | solution.py:236
  1173.0 813.5 %reduce-scatter.25.cloned.1.call-start = ((), (), s32[]{:S(2)}) async-start(), calls=%async_computation.29 | async-start | bytes 10485760 | tf_op jit(solution)/shard_map/reduce_scatter | solution.py:250
  1221.5 889.5 %all-reduce.31.cloned.1.call-start = ((), (), s32[]{:S(2)}) async-start(), calls=%async_computation.35 | async-start | bytes 131072 | tf_op jit(solution)/shard_map/psum | solution.py:458
  1565.7 420.8 %copy-start.48 = (f32[2048]{0:T(1024)S(1)}, f32[2048]{0:T(1024)}, u32[]{:S(2)}) copy-start(f32[2048]{0:T(1024)} %param.24) | copy-start | bytes 24580
  1565.7 420.8 %copy-start.78 = (f32[256]{0:T(256)S(1)}, f32[256]{0:T(256)}, u32[]{:S(2)}) copy-start(f32[256]{0:T(256)} %copy-done.77) | copy-start | bytes 3076
  1565.7 420.8 %copy-start.80 = (f32[256]{0:T(256)S(1)}, f32[256]{0:T(256)}, u32[]{:S(2)}) copy-start(f32[256]{0:T(256)} %copy-done.79) | copy-start | bytes 3076
  (95 other events, 3535.2 us)
Sparse Core Ops, SparseCore 0:
  10.1 52.3 all-gather.14
  64.7 33.0 all-gather.12
  100.0 49.2 all-gather.16
  151.3 71.8 all-gather.20
  225.2 71.6 all-gather.18
  298.7 74.3 all-gather.22
  382.1 68.9 reduce-scatter.18
  453.5 92.6 all-gather.26
  548.4 32.6 all-gather.24
  583.4 92.6 all-gather.28
  678.3 32.6 all-gather.32
  713.1 93.5 all-gather.30
  842.2 69.9 reduce-scatter.22
  917.8 34.4 all-gather.34
  955.8 109.9 reduce-scatter.36
  1069.3 109.7 reduce-scatter.38
  1182.6 110.1 reduce-scatter.40
  1296.5 61.7 reduce-scatter.42
  1362.6 60.8 reduce-scatter.44
  1426.9 66.7 reduce-scatter.26
  1497.2 66.6 reduce-scatter.28
  1567.5 86.9 reduce-scatter.30
  1658.5 87.7 reduce-scatter.32
  1749.8 88.1 reduce-scatter.34
  1840.8 71.5 reduce-scatter.20
  1914.8 71.6 reduce-scatter.24
  1993.4 117.5 all-reduce.30

commit v2 on v0

v2 whole, which is shorter than its diff:
```python
import functools

import jax
import jax.numpy as jnp
from jax import lax
from jax.experimental import pallas as pl
from jax.experimental.pallas import tpu as pltpu
from jax.sharding import PartitionSpec as P

BF=jnp.bfloat16; F32=jnp.float32
DK = 128
CHUNK = 128
HALO = 8


def dot1(a, b, ca=1, cb=0):
    return lax.dot_general(a, b, (((ca,), (cb,)), ((), ())), preferred_element_type=F32)


def split(a):
    if a.dtype == BF:
        return a, None
    high = a.astype(BF)
    return high, (a - high.astype(F32)).astype(BF)


def mm(a, b, ca=1, cb=0):
    a_high, a_low = a if isinstance(a, tuple) else split(a)
    b_high, b_low = b if isinstance(b, tuple) else split(b)
    total = dot1(a_high, b_high, ca, cb)
    if b_low is not None:
        total = total + dot1(a_high, b_low, ca, cb)
    if a_low is not None:
        total = total + dot1(a_low, b_high, ca, cb)
    return total


def exact_sum(ones, values, ca):
    high, rest = split(values)
    middle, low = split(values - high.astype(F32))
    return dot1(ones, high, ca) + (dot1(ones, middle, ca) + dot1(ones, low, ca))


def grids(size):
    return (
        lax.broadcasted_iota(jnp.int32, (size, size), 0),
        lax.broadcasted_iota(jnp.int32, (size, size), 1),
    )


def inverses(couplings):
    size = couplings[0].shape[0]
    i, j = grids(size)
    eye = jnp.where(i == j, 1.0, 0.0).astype(F32)

    def same(bits):
        return lax.shift_right_logical(i, bits) == lax.shift_right_logical(j, bits)

    inside = same(3)
    near = [jnp.where(inside, a, 0.0) for a in couplings]
    second = [split(mm(a, a)) for a in map(split, near)]
    fourth = [mm(a, a) for a in second]
    found = [eye - a for a in near]
    found = [x + mm(x, a) for x, a in zip(found, second)]
    found = [x + mm(x, a) for x, a in zip(found, fourth)]
    bits = 3
    while (1 << bits) < size:
        across = jnp.logical_and(same(bits + 1), jnp.logical_not(same(bits)))
        parts = [split(x) for x in found]
        moved = [mm(jnp.where(across, a, 0.0), x) for a, x in zip(couplings, parts)]
        found = [x - mm(p, y) for x, p, y in zip(found, parts, moved)]
        bits += 1
    return found


def conv_of(taps_ref, ext, columns, rows, start=HALO - 3):
    total = taps_ref[0:1, columns] * ext[start : start + rows, columns]
    for tap in range(1, 4):
        total = total + taps_ref[tap : tap + 1, columns] * ext[
            start + tap : start + tap + rows, columns
        ]
    return total


def decay_of(tail, par_ref):
    i, j = grids(CHUNK)
    ones = jnp.where(i >= j, 1.0, 0.0).astype(BF)
    raised = tail + par_ref[1:2, :]
    log_decay = par_ref[0:1, :] * (
        jnp.maximum(raised, 0.0) + jnp.log1p(jnp.exp(-jnp.abs(raised)))
    )
    return exact_sum(ones, log_decay, 1), log_decay, jax.nn.sigmoid(tail), raised


def fwd_kernel(H, DV, NC, p_ref, taps_ref, par_ref, o_ref, u_ref, t_ref, s_ref, S, ext):
    C = CHUNK
    R = NC * C
    W = H * (2 * DK + DV)

    @pl.when(pl.program_id(0) == 0)
    def _():
        S[...] = jnp.zeros_like(S)
        ext[0:HALO, :] = jnp.zeros((HALO, W), F32)

    @pl.when(pl.program_id(0) > 0)
    def _():
        ext[0:HALO, :] = ext[R : R + HALO, :]

    ext[HALO : HALO + R, :] = p_ref[:, 0:W]
    i, j = grids(C)
    low, strict = i >= j, i > j
    idx = [(c, h) for c in range(NC) for h in range(H)]
    rows = [slice(c * C, (c + 1) * C) for c in range(NC)]
    q, k, v, b, g, gr = {}, {}, {}, {}, {}, {}
    for h in range(H):
        for part, out, base, size, factor in (
            (0, q, h * DK, DK, DK**-0.5),
            (1, k, H * DK + h * DK, DK, 1.0),
            (2, v, 2 * H * DK + h * DV, DV, None),
        ):
            mixed = conv_of(taps_ref, ext, slice(base, base + size), R)
            mixed = mixed * jax.nn.sigmoid(mixed)
            if factor is not None:
                mixed = mixed * (
                    lax.rsqrt(jnp.sum(mixed * mixed, axis=1, keepdims=True) + 1e-06) * factor
                )
            mixed = mixed.astype(BF)
            for c in range(NC):
                out[c, h] = mixed[rows[c], :]
    for c in range(NC):
        running, _, beta, _ = decay_of(p_ref[rows[c], W : W + 128], par_ref)
        across = jnp.transpose(running)
        for h in range(H):
            b[c, h] = beta[:, H + h : H + h + 1]
            g[c, h] = running[:, h : h + 1]
            gr[c, h] = across[h : h + 1, :]
    D = {x: jnp.exp(jnp.where(low, g[x] - gr[x], -1e30)) for x in idx}
    A = [jnp.where(strict, dot1(k[x], k[x], 1, 1) * b[x] * D[x], 0.0) for x in idx]
    T = dict(zip(idx, inverses(A)))
    P = {x: dot1(q[x], k[x], 1, 1) * D[x] for x in idx}
    gam = {x: jnp.exp(g[x]) for x in idx}
    Ts = {x: split(T[x]) for x in idx}
    TV = {x: mm(Ts[x], b[x] * v[x].astype(F32)) for x in idx}
    TK = {x: mm(Ts[x], b[x] * gam[x] * k[x].astype(F32)) for x in idx}
    for c in range(NC):
        for h in range(H):
            x = (c, h)
            t_ref[rows[c], h * C : (h + 1) * C] = T[x]
            S0 = S[h * DK : (h + 1) * DK, :]
            s_ref[c, h * DK : (h + 1) * DK, :] = S0
            Ss = split(S0)
            U = TV[x] - mm(TK[x], Ss)
            Us = split(U)
            u_ref[rows[c], h * DV : (h + 1) * DV] = U
            o_ref[rows[c], h * DV : (h + 1) * DV] = gam[x] * mm(q[x], Ss) + mm(P[x], Us)
            last = gr[x][:, C - 1 : C]
            S[h * DK : (h + 1) * DK, :] = jnp.exp(last) * S0 + mm(
                k[x].astype(F32) * jnp.exp(last - g[x]), Us, 0, 0
            )


def bwd_kernel(
    H, DV, steps, p_ref, halo_ref, taps_ref, par_ref, u_ref, t_ref, s_ref, do_ref,
    dp_ref, dtaps_ref, dpar_ref, dS, ext, dext,
):
    C = CHUNK
    W = H * (2 * DK + DV)
    step = pl.program_id(0)

    @pl.when(step == 0)
    def _():
        dS[...] = jnp.zeros_like(dS)
        dext[C : C + HALO, :] = jnp.zeros((HALO, W), F32)
        dtaps_ref[...] = jnp.zeros_like(dtaps_ref)
        dpar_ref[...] = jnp.zeros_like(dpar_ref)

    @pl.when(step > 0)
    def _():
        dext[C : C + HALO, :] = dext[0:HALO, :]

    @pl.when(step == steps - 1)
    def _():
        ext[0:HALO, :] = jnp.zeros((HALO, W), F32)

    @pl.when(step < steps - 1)
    def _():
        ext[0:HALO, :] = halo_ref[:, 0:W]

    ext[HALO : HALO + C, :] = p_ref[:, 0:W]
    i, j = grids(C)
    low, strict = i >= j, i > j
    lane = lax.broadcasted_iota(jnp.int32, (C, 128), 1)
    last_row = lax.broadcasted_iota(jnp.int32, (C, 1), 0) == C - 1
    tail = p_ref[:, W : W + 128]
    running, log_decay, beta, raised = decay_of(tail, par_ref)
    across = jnp.transpose(running)
    d_running = jnp.zeros((C, 128), F32)
    d_beta = jnp.zeros((C, 128), F32)

    def gradient_in(columns, mixed, sig, d_act):
        dext[0:C, columns] = d_act * sig * (1.0 + mixed * (1.0 - sig))

    for h in range(H):
        q_columns = slice(h * DK, (h + 1) * DK)
        k_columns = slice(H * DK + h * DK, H * DK + (h + 1) * DK)
        v_columns = slice(2 * H * DK + h * DV, 2 * H * DK + (h + 1) * DV)
        q_mixed = conv_of(taps_ref, ext, q_columns, C)
        k_mixed = conv_of(taps_ref, ext, k_columns, C)
        v_mixed = conv_of(taps_ref, ext, v_columns, C)
        q_sig, k_sig, v_sig = (jax.nn.sigmoid(x) for x in (q_mixed, k_mixed, v_mixed))
        q_act, k_act = q_mixed * q_sig, k_mixed * k_sig
        q_inv = lax.rsqrt(jnp.sum(q_act * q_act, axis=1, keepdims=True) + 1e-06)
        k_inv = lax.rsqrt(jnp.sum(k_act * k_act, axis=1, keepdims=True) + 1e-06)
        q = (q_act * (q_inv * DK**-0.5)).astype(BF)
        k = (k_act * k_inv).astype(BF)
        v = (v_mixed * v_sig).astype(BF)
        b, g, gr = beta[:, H + h : H + h + 1], running[:, h : h + 1], across[h : h + 1, :]
        hv = slice(h * DV, (h + 1) * DV)
        hk = slice(h * DK, (h + 1) * DK)
        U = split(u_ref[:, hv])
        T = split(t_ref[:, h * C : (h + 1) * C])
        S0 = s_ref[0, hk, :]
        Ss = split(S0)
        dO = split(do_ref[:, hv])
        qf, kf = q.astype(F32), k.astype(F32)
        D = jnp.exp(jnp.where(low, g - gr, -1e30))
        kk, qk = dot1(k, k, 1, 1), dot1(q, k, 1, 1)
        bD = b * D
        A, P = jnp.where(strict, kk * bD, 0.0), qk * D
        last = gr[:, C - 1 : C]
        gam, e, G = jnp.exp(g), jnp.exp(last - g), jnp.exp(last)
        dS1 = dS[hk, :]
        dSs = split(dS1)
        dU = mm(P, dO, 0, 0) + mm(kf * e, dSs)
        dR = mm(T, dU, 0, 0)
        dRs = split(dR)
        dS[hk, :] = G * dS1 + mm(qf * gam, dO, 0, 0) - mm(kf * (b * gam), dRs, 0, 0)
        dP = jnp.where(low, mm(dO, U, 1, 1), 0.0)
        dA = jnp.where(strict, -mm(dRs, U, 1, 1), 0.0)
        Rb = v.astype(F32) - gam * mm(k, Ss)
        db = jnp.sum(dR * Rb, axis=1, keepdims=True) + jnp.sum(dA * kk * D, axis=1, keepdims=True)
        dOS = gam * mm(dO, Ss, 1, 1)
        dRS = (b * gam) * mm(dRs, Ss, 1, 1)
        UdS = e * mm(U, dSs, 1, 1)
        M1, M2 = split(dP * D), split(dA * bD)
        dq = dOS + mm(M1, k)
        dk = UdS - dRS + mm(M1, q, 0, 0) + mm(M2, k) + mm(M2, k, 0, 0)
        X = dP * P + dA * A
        uk = jnp.sum(UdS * kf, axis=1, keepdims=True)
        total = jnp.sum(uk, axis=0, keepdims=True) + G * jnp.sum(
            jnp.sum(S0 * dS1, axis=1, keepdims=True), axis=0, keepdims=True
        )
        dg = (
            jnp.sum(dOS * qf - dRS * kf + X - jnp.transpose(X), axis=1, keepdims=True)
            - uk
            + jnp.where(last_row, total, 0.0)
        )
        d_running = jnp.where(lane == h, dg, d_running)
        d_beta = jnp.where(lane == H + h, db, d_beta)
        q_in = jnp.sum(dq * q_act, axis=1, keepdims=True) * (q_inv * q_inv)
        gradient_in(q_columns, q_mixed, q_sig, (q_inv * DK**-0.5) * (dq - q_act * q_in))
        k_in = jnp.sum(dk * k_act, axis=1, keepdims=True) * (k_inv * k_inv)
        gradient_in(k_columns, k_mixed, k_sig, k_inv * (dk - k_act * k_in))
        gradient_in(v_columns, v_mixed, v_sig, b * dR)
    for start in range(0, W, 512):
        columns = slice(start, start + 512)
        here = dext[0:C, columns]
        total = taps_ref[3:4, columns] * here
        dtaps_ref[3:4, columns] += jnp.sum(
            here * ext[HALO : HALO + C, columns], axis=0, keepdims=True
        )
        for tap in range(3):
            total = total + taps_ref[tap : tap + 1, columns] * dext[3 - tap : 3 - tap + C, columns]
            dtaps_ref[tap : tap + 1, columns] += jnp.sum(
                here * ext[HALO - 3 + tap : HALO - 3 + tap + C, columns], axis=0, keepdims=True
            )
        dp_ref[:, columns] = total.astype(BF)
    ones = jnp.where(i >= j, 1.0, 0.0).astype(BF)
    d_log = exact_sum(ones, d_running, 0)
    d_raised = d_log * par_ref[0:1, :] * jax.nn.sigmoid(raised)
    d_tail = d_raised + d_beta * beta * (1.0 - beta)
    dp_ref[:, W : W + 128] = d_tail.astype(BF)
    dpar_ref[0:1, :] += jnp.sum(d_log * log_decay, axis=0, keepdims=True)
    dpar_ref[1:2, :] += jnp.sum(d_raised, axis=0, keepdims=True)


LIMIT = pltpu.CompilerParams(vmem_limit_bytes=56 * 2**20)


def row_block(rows, width, at=lambda s: s):
    return pl.BlockSpec((rows, width), lambda s: (at(s), 0))


def whole_block(array):
    return pl.BlockSpec(array.shape, lambda s: (0,) * array.ndim)


def mixer_fwd(projected, taps, par, heads, NC=2):
    L, wide = projected.shape
    H, C = heads, CHUNK
    DV = taps.shape[1] // H - 2 * DK
    f = jax.ShapeDtypeStruct
    return pl.pallas_call(
        functools.partial(fwd_kernel, H, DV, NC),
        grid=(L // C // NC,),
        in_specs=[row_block(NC * C, wide), whole_block(taps), whole_block(par)],
        out_specs=[
            row_block(NC * C, H * DV),
            row_block(NC * C, H * DV),
            row_block(NC * C, H * C),
            pl.BlockSpec((NC, H * DK, DV), lambda s: (s, 0, 0)),
        ],
        out_shape=[
            f((L, H * DV), F32), f((L, H * DV), F32), f((L, H * C), F32), f((L // C, H * DK, DV), F32),
        ],
        scratch_shapes=[pltpu.VMEM((H * DK, DV), F32), pltpu.VMEM((NC * C + HALO, taps.shape[1]), F32)],
        compiler_params=LIMIT,
        cost_estimate=pl.CostEstimate(flops=35 * 10**9, bytes_accessed=30 * 2**20, transcendentals=0),
        name="mixer_fwd",
    )(projected, taps, par)


def mixer_bwd(projected, taps, par, written, inverse, states, grad_heads, heads):
    L, wide = projected.shape
    H, C = heads, CHUNK
    DV = taps.shape[1] // H - 2 * DK
    W = taps.shape[1]
    n = L // C
    f = jax.ShapeDtypeStruct

    def back(s):
        return n - 1 - s

    return pl.pallas_call(
        functools.partial(bwd_kernel, H, DV, n),
        grid=(n,),
        in_specs=[
            row_block(C, wide, back),
            row_block(HALO, wide, lambda s: jnp.maximum(back(s) * (C // HALO) - 1, 0)),
            whole_block(taps),
            whole_block(par),
            row_block(C, H * DV, back),
            row_block(C, H * C, back),
            pl.BlockSpec((1, H * DK, DV), lambda s: (back(s), 0, 0)),
            row_block(C, H * DV, back),
        ],
        out_specs=[row_block(C, wide, back), whole_block(taps), whole_block(par)],
        out_shape=[f((L, wide), BF), f(taps.shape, F32), f(par.shape, F32)],
        scratch_shapes=[
            pltpu.VMEM((H * DK, DV), F32),
            pltpu.VMEM((C + HALO, W), F32),
            pltpu.VMEM((C + HALO, W), F32),
        ],
        compiler_params=LIMIT,
        cost_estimate=pl.CostEstimate(flops=55 * 10**9, bytes_accessed=36 * 2**20, transcendentals=0),
        name="mixer_bwd",
    )(projected, projected, taps, par, written, inverse, states, grad_heads)


def gate_fwd_kernel(DV, o_ref, gate_ref, gain_ref, out_ref):
    for start in range(0, o_ref.shape[1], DV):
        cut = slice(start, start + DV)
        heads, gate = o_ref[:, cut], gate_ref[:, cut]
        inverse = lax.rsqrt(jnp.mean(heads * heads, axis=1, keepdims=True) + 1e-05)
        out_ref[:, cut] = (heads * inverse * gain_ref[...] * (gate * jax.nn.sigmoid(gate))).astype(BF)


def gate_fwd(heads_out, gate_proj, gain):
    L, width = heads_out.shape
    rows = L // 8
    return pl.pallas_call(
        functools.partial(gate_fwd_kernel, gain.shape[1]),
        grid=(8,),
        in_specs=[row_block(rows, width), row_block(rows, width), whole_block(gain)],
        out_specs=row_block(rows, width),
        out_shape=jax.ShapeDtypeStruct((L, width), BF),
        cost_estimate=pl.CostEstimate(flops=5 * 10**9, bytes_accessed=10 * 2**20, transcendentals=0),
        name="gate_fwd",
    )(heads_out, gate_proj, gain)


def gate_bwd_kernel(DV, o_ref, gate_ref, gain_ref, in_ref, do_ref, dgate_ref, dgain_ref):
    @pl.when(pl.program_id(0) == 0)
    def _():
        dgain_ref[...] = jnp.zeros_like(dgain_ref)

    for start in range(0, o_ref.shape[1], DV):
        cut = slice(start, start + DV)
        heads, gate, grad = o_ref[:, cut], gate_ref[:, cut], in_ref[:, cut]
        inverse = lax.rsqrt(jnp.mean(heads * heads, axis=1, keepdims=True) + 1e-05)
        normed = heads * inverse
        sig = jax.nn.sigmoid(gate)
        dgate_ref[:, cut] = (
            grad * (normed * gain_ref[...]) * (sig * (1.0 + gate * (1.0 - sig)))
        ).astype(BF)
        d_scaled = grad * (gate * sig)
        dgain_ref[...] += jnp.sum(d_scaled * normed, axis=0, keepdims=True)
        d_normed = d_scaled * gain_ref[...]
        do_ref[:, cut] = inverse * (
            d_normed - normed * jnp.mean(d_normed * normed, axis=1, keepdims=True)
        )


def gate_bwd(heads_out, gate_proj, gain, grad_mixer):
    L, width = heads_out.shape
    rows = L // 8
    f = jax.ShapeDtypeStruct
    return pl.pallas_call(
        functools.partial(gate_bwd_kernel, gain.shape[1]),
        grid=(8,),
        in_specs=[row_block(rows, width), row_block(rows, width), whole_block(gain), row_block(rows, width)],
        out_specs=[row_block(rows, width), row_block(rows, width), whole_block(gain)],
        out_shape=[f((L, width), F32), f((L, width), BF), f(gain.shape, F32)],
        cost_estimate=pl.CostEstimate(flops=7 * 10**9, bytes_accessed=18 * 2**20, transcendentals=0),
        name="gate_bwd",
    )(heads_out, gate_proj, gain, grad_mixer)


def at_place(place, n):
    return jnp.where(place < n // 2, 2 * place, 2 * (n - place) - 1)


def place_of(index, n):
    return jnp.where(index % 2 == 0, index // 2, n - (index + 1) // 2)


def ring_pairs(n):
    order = list(range(0, n, 2)) + list(range(n - 1, 0, -2))
    ahead = [(order[i], order[(i + 1) % n]) for i in range(n)]
    return ahead, [(d, s) for s, d in ahead]


def to_relative(array):
    n = lax.axis_size("dp")
    block = array.shape[-1] // n
    place = place_of(lax.axis_index("dp"), n)
    return jnp.concatenate(
        [
            lax.dynamic_slice_in_dim(
                array, at_place((place - d + n) % n, n) * block, block, array.ndim - 1
            )
            for d in range(n)
        ],
        axis=-1,
    )


def to_absolute(array):
    n = lax.axis_size("dp")
    block = array.shape[-1] // n
    place = place_of(lax.axis_index("dp"), n)
    return jnp.concatenate(
        [
            lax.dynamic_slice_in_dim(
                array,
                ((place - place_of(jnp.int32(index), n) + n) % n) * block,
                block,
                array.ndim - 1,
            )
            for index in range(n)
        ],
        axis=-1,
    )


def after(array, other):
    return lax.optimization_barrier((array, other))[0]


def ring_gather(shard, earlier=None, hops=0):
    n = lax.axis_size("dp")
    ahead, behind = ring_pairs(n)
    half = shard.shape[0] // 2
    if earlier is not None:
        shard = after(shard, earlier[min(hops, n - 1)][0])
    first, second = [shard[:half]], [shard[half:]]
    for _ in range(n - 1):
        first.append(lax.ppermute(first[-1], "dp", ahead))
        second.append(lax.ppermute(second[-1], "dp", behind))
    return [(first[d], second[(n - d) % n]) for d in range(n)]


def stacked(pieces):
    return jnp.concatenate([half for pair in pieces for half in pair], axis=0)


def side_by_side(pieces):
    return jnp.concatenate([jnp.concatenate(pair, axis=0) for pair in pieces], axis=1)


def ring_scatter(first_of, second_of, earlier=()):
    n = lax.axis_size("dp")
    ahead, behind = ring_pairs(n)
    first, second = first_of(1 % n).astype(BF), second_of(n - 1).astype(BF)
    first, second = after((first, second), earlier)
    hops = []
    for step in range(n - 1):
        first, second = lax.ppermute(first, "dp", ahead), lax.ppermute(second, "dp", behind)
        hops.append(first)
        first = first.astype(F32) + first_of((step + 2) % n)
        second = second.astype(F32) + second_of(n - 2 - step)
        if step < n - 2:
            first, second = first.astype(BF), second.astype(BF)
    return jnp.concatenate((first, second), axis=0), hops


def contract_rows(left, right):
    return lax.dot_general(
        left, right, (((0,), (0,)), ((), ())), preferred_element_type=jnp.float32
    )


def times_transposed(left, right):
    return lax.dot_general(
        left, right, (((1,), (1,)), ((), ())), preferred_element_type=jnp.float32
    )


def scatter_rows_of(features, grads, earlier=()):
    block = features.shape[1] // lax.axis_size("dp")
    half = block // 2

    def part(d, start):
        return contract_rows(features[:, d * block + start : d * block + start + half], grads)

    return ring_scatter(lambda d: part(d, 0), lambda d: part(d, half), earlier)


def scatter_columns_of(features, grads, earlier=()):
    block = grads.shape[1] // lax.axis_size("dp")
    half = features.shape[1] // 2

    def part(d, left):
        return contract_rows(left, grads[:, d * block : (d + 1) * block])

    return ring_scatter(
        lambda d: part(d, features[:, :half]), lambda d: part(d, features[:, half:]), earlier
    )


CORES = [(0, 1), (1, 0), (2, 3), (3, 2)]
PAIRS = [(0, 2), (2, 0), (1, 3), (3, 1)]


def spread_rows(block):
    if lax.axis_size("tensor") != 4:
        return lax.all_gather(block, "tensor", axis=0, tiled=True)
    rank = lax.axis_index("tensor")
    rows = block.shape[0]
    far = lax.ppermute(block, "tensor", PAIRS)
    near = lax.ppermute(block, "tensor", CORES)
    far_near = lax.ppermute(far, "tensor", CORES)
    out = jnp.zeros((4 * rows,) + block.shape[1:], block.dtype)
    for part, flip in ((block, 0), (near, 1), (far, 2), (far_near, 3)):
        out = lax.dynamic_update_slice_in_dim(out, part, (rank ^ flip) * rows, 0)
    return out


def sum_rows(product, rows):
    if lax.axis_size("tensor") != 4:
        whole = jnp.concatenate([product(i * rows) for i in range(lax.axis_size("tensor"))], axis=0)
        return lax.psum_scatter(whole, "tensor", scatter_dimension=0, tiled=True)
    rank = lax.axis_index("tensor")
    far_near = lax.ppermute(product((rank ^ 3) * rows).astype(BF), "tensor", CORES)
    far = product((rank ^ 2) * rows) + far_near.astype(F32)
    far = lax.ppermute(far.astype(BF), "tensor", PAIRS)
    near = lax.ppermute(product((rank ^ 1) * rows).astype(BF), "tensor", CORES)
    return product(rank * rows) + near.astype(F32) + far.astype(F32)


def branch_rows(left, right, rows):
    return sum_rows(
        lambda start: jnp.dot(
            lax.dynamic_slice_in_dim(left, start, rows, 0), right, preferred_element_type=F32
        ),
        rows,
    )


def back_rows(pairs, rows):
    def product(start):
        total = None
        for grads, weight in pairs:
            part = times_transposed(lax.dynamic_slice_in_dim(grads, start, rows, 0), weight)
            total = part if total is None else total + part
        return total

    return sum_rows(product, rows)


def sum_over(values, axis):
    n = lax.axis_size(axis)
    if n & (n - 1):
        return lax.psum(values, axis)
    step = 1
    while step < n:
        values = values + lax.ppermute(values, axis, [(i, i ^ step) for i in range(n)])
        step *= 2
    return values


def packed(arrays):
    flat = jnp.concatenate([a.reshape(-1) for a in arrays])
    pad = -flat.shape[0] % 1024
    return jnp.pad(flat, (0, pad)).reshape(-1, 128)


def unpacked(values, shapes):
    flat = values.reshape(-1)
    out, start = [], 0
    for shape in shapes:
        size = 1
        for extent in shape:
            size *= extent
        out.append(flat[start : start + size].reshape(shape))
        start += size
    return out


def norm_back(values, inverse, gain, incoming):
    scaled = incoming * gain
    width = values.shape[1]
    grad_values = (
        inverse * scaled
        - values
        * inverse
        * inverse
        * inverse
        * jnp.sum(scaled * values, axis=1, keepdims=True)
        / width
    )
    grad_gain = jnp.sum(incoming * values * inverse, axis=0)
    return (grad_values, grad_gain)


def place_slice(local, whole, rank, axis):
    return lax.dynamic_update_slice_in_dim(
        jnp.zeros_like(whole), local, rank * local.shape[axis], axis
    )


def columns(array, widths):
    out, start = [], 0
    for width in widths:
        out.append(array[:, start : start + width])
        start += width
    return out


def shards(
    inputs,
    lengths,
    cotangent,
    norm_attn,
    norm_ffn,
    norm_heads,
    w_query,
    w_key,
    w_value,
    w_out_gate,
    w_decay,
    w_beta,
    w_output,
    conv_query,
    conv_key,
    conv_value,
    decay_log,
    decay_bias,
    w_ffn_gate,
    w_ffn_up,
    w_ffn_down,
):
    rows = inputs.shape[0]
    width = inputs.shape[1]
    tensor_rank = lax.axis_index("tensor")
    positions = tensor_rank * rows + jnp.arange(rows, dtype=jnp.int32)
    valid = (positions < lengths[0]).astype(jnp.float32)[:, None]
    heads_here = w_decay.shape[1]
    widths = [w.shape[1] for w in (w_query, w_key, w_value, w_decay, w_beta)]
    fill = -sum(widths) % 128
    mixed_shard = jnp.pad(
        jnp.concatenate((w_query, w_key, w_value, w_decay, w_beta), axis=1), ((0, 0), (0, fill))
    )
    ffn_width = w_ffn_gate.shape[1]
    mixed_ring = ring_gather(mixed_shard)
    gate_ring = ring_gather(w_out_gate, mixed_ring, 6)
    output_ring = ring_gather(w_output, mixed_ring, 7)
    ffn_ring = ring_gather(jnp.concatenate((w_ffn_gate, w_ffn_up), axis=1), gate_ring, 6)
    down_ring = ring_gather(w_ffn_down, ffn_ring, 6)
    mixed_full, gate_full, ffn_full = stacked(mixed_ring), stacked(gate_ring), stacked(ffn_ring)
    output_full, down_full = side_by_side(output_ring), side_by_side(down_ring)

    gain_attn = to_relative(norm_attn)
    gain_ffn = to_relative(norm_ffn)
    stream_in = to_relative(inputs).astype(jnp.float32)
    grad_out = valid * to_relative(cotangent).astype(jnp.float32)
    inverse_in = lax.rsqrt(jnp.mean(stream_in * stream_in, axis=1, keepdims=True) + 1e-06)
    full_in = spread_rows((stream_in * inverse_in * gain_attn).astype(jnp.bfloat16))
    grad_ffn = spread_rows(grad_out.astype(jnp.bfloat16))

    projected = jnp.dot(full_in, mixed_full, preferred_element_type=jnp.float32)
    gate_proj = jnp.dot(full_in, gate_full, preferred_element_type=jnp.float32)

    def here(array):
        size = array.shape[-1] // lax.axis_size("tensor")
        return lax.dynamic_slice_in_dim(array, tensor_rank * size, size, array.ndim - 1)

    taps = jnp.concatenate((here(conv_query), here(conv_key), here(conv_value)), axis=1)
    par = jnp.pad(
        jnp.stack((-jnp.exp(here(decay_log)), here(decay_bias))), ((0, 6), (0, 128 - heads_here))
    )
    gain_heads = norm_heads[None, :]
    heads_out, written, inverse, states = mixer_fwd(projected, taps, par, heads_here)
    mixer = gate_fwd(heads_out, gate_proj, gain_heads)
    branch_attn = branch_rows(mixer, output_full, rows)
    stream = stream_in + branch_attn
    inverse_mid = lax.rsqrt(jnp.mean(stream * stream, axis=1, keepdims=True) + 1e-06)
    full_mid = spread_rows((stream * inverse_mid * gain_ffn).astype(jnp.bfloat16))
    ffn_in = jnp.dot(full_mid, ffn_full, preferred_element_type=jnp.float32)
    ffn_gate, ffn_up = ffn_in[:, :ffn_width], ffn_in[:, ffn_width:]
    sigma = jax.nn.sigmoid(ffn_gate)
    silu_gate = ffn_gate * sigma
    hidden = (silu_gate * ffn_up).astype(jnp.bfloat16)
    branch_ffn = branch_rows(hidden, down_full, rows)
    outputs = to_absolute((valid * (stream + branch_ffn)).astype(jnp.bfloat16))
    stat_sums = jnp.stack(
        [
            jnp.sum(valid * stream_in * stream_in),
            jnp.sum(valid * branch_attn * branch_attn),
            jnp.sum(valid * branch_ffn * branch_ffn),
            jnp.sum(valid),
        ]
    )

    owned_down, down_hops = scatter_columns_of(hidden, grad_ffn)
    grad_hidden = times_transposed(grad_ffn, down_full)
    grad_gate_in = grad_hidden * ffn_up * sigma * (1.0 + ffn_gate * (1.0 - sigma))
    grad_up_in = grad_hidden * silu_gate
    grad_ffn_in = jnp.concatenate((grad_gate_in, grad_up_in), axis=1).astype(jnp.bfloat16)
    grad_mid = back_rows(((grad_ffn_in, ffn_full),), rows)
    owned_ffn, ffn_hops = scatter_rows_of(full_mid, grad_ffn_in, [down_hops[-3]])
    owned_gate, owned_up = columns(owned_ffn, [ffn_width] * 2)
    grad_through, grad_norm_ffn = norm_back(stream, inverse_mid, gain_ffn, grad_mid)
    grad_stream = grad_out + grad_through
    grad_attn = spread_rows(grad_stream.astype(jnp.bfloat16))
    grad_mixer = times_transposed(grad_attn, output_full)
    owned_output, output_hops = scatter_columns_of(mixer, grad_attn, [ffn_hops[-2]])
    grad_heads, grad_gate_proj, heads_gain_grad = gate_bwd(
        heads_out, gate_proj, gain_heads, grad_mixer
    )
    owned_out_gate, gate_hops = scatter_rows_of(full_in, grad_gate_proj, [ffn_hops[-1]])
    grad_projected, grad_taps, grad_par = mixer_bwd(
        projected, taps, par, written, inverse, states, grad_heads, heads_here
    )
    grad_normed = back_rows(((grad_gate_proj, gate_full), (grad_projected, mixed_full)), rows)
    owned_mixed, _ = scatter_rows_of(full_in, grad_projected, [output_hops[-1], gate_hops[-2]])
    owned_query, owned_key, owned_value, owned_decay, owned_beta = columns(owned_mixed, widths)
    grad_through_in, grad_norm_attn = norm_back(stream_in, inverse_in, gain_attn, grad_normed)
    grad_inputs = to_absolute(grad_stream + grad_through_in)

    local = columns(grad_taps, widths[:3]) + [grad_par[0, :heads_here], grad_par[1, :heads_here]]
    whole = [conv_query, conv_key, conv_value, decay_log, decay_bias]
    common = [stat_sums, to_absolute(grad_norm_ffn), heads_gain_grad[0]]
    sums = sum_over(packed(common + local), "dp")
    sums = unpacked(sums, [a.shape for a in common + local])
    spread = [
        place_slice(part, array, tensor_rank, part.ndim - 1)
        for part, array in zip(sums[3:], whole)
    ]
    sums = sum_over(packed(sums[:3] + spread), "tensor")
    (
        stat_sums,
        total_ffn_gain,
        total_heads_gain,
        total_conv_query,
        total_conv_key,
        total_conv_value,
        total_decay_log,
        total_decay_bias,
    ) = unpacked(sums, [a.shape for a in common + whole])
    last = packed([to_absolute(grad_norm_attn)])
    [total_attn_gain] = unpacked(sum_over(sum_over(last, "dp"), "tensor"), [norm_attn.shape])
    statistics = jnp.sqrt(stat_sums[:3] / (stat_sums[3] * width))
    return (
        outputs,
        statistics,
        grad_inputs,
        total_attn_gain,
        total_ffn_gain,
        total_heads_gain,
        owned_query,
        owned_key,
        owned_value,
        owned_out_gate,
        owned_decay,
        owned_beta,
        owned_output,
        total_conv_query,
        total_conv_key,
        total_conv_value,
        total_decay_log,
        total_decay_bias,
        owned_gate,
        owned_up,
        owned_down,
    )


def solution(mesh):
    in_specs = (
        P(("dp", "tensor"), None),
        P("dp"),
        P(("dp", "tensor"), None),
        P(),
        P(),
        P(),
        P("dp", "tensor"),
        P("dp", "tensor"),
        P("dp", "tensor"),
        P("dp", "tensor"),
        P("dp", "tensor"),
        P("dp", "tensor"),
        P("tensor", "dp"),
        P(),
        P(),
        P(),
        P(),
        P(),
        P("dp", "tensor"),
        P("dp", "tensor"),
        P("tensor", "dp"),
    )
    out_specs = (
        P(("dp", "tensor"), None),
        P(),
        P(("dp", "tensor"), None),
        P(),
        P(),
        P(),
        P("dp", "tensor"),
        P("dp", "tensor"),
        P("dp", "tensor"),
        P("dp", "tensor"),
        P("dp", "tensor"),
        P("dp", "tensor"),
        P("tensor", "dp"),
        P(),
        P(),
        P(),
        P(),
        P(),
        P("dp", "tensor"),
        P("dp", "tensor"),
        P("tensor", "dp"),
    )
    return jax.shard_map(shards, mesh=mesh, in_specs=in_specs, out_specs=out_specs, check_vma=False)
```

time: 3660 us -> 1080 us (0.30)
  waiting for transfers between devices: 1980 us -> 369 us
  other arithmetic: 775 us -> 42.2 us
  matrix products: 595 us -> 300 us
  starting transfers between devices: 1.69 us -> 167 us
  local copies, waits for them, and re-layouts: 184 us -> 69.5 us
  Pallas kernels: 0 us -> 114 us
  blocking collectives: 98.8 us -> 0 us
    reduce_scatter x12 -> x0, waiting for transfers between devices: 1390 us -> none  [the longest x1 196 us: shards(): lax.psum_scatter(grad_down, 'dp', scatter_dimension=1, tiled=True)]
    another operation x211 -> x2, other arithmetic: 660 us -> 0.68 us  [shards(): jnp.stack((-jnp.exp(here(decay_log)), here(decay_bias)))]
    all_gather x12 -> x0, waiting for transfers between devices: 464 us -> none  [the longest x1 95.7 us: fetch_ffn(): lax.all_gather(w_ffn_down, 'dp', axis=1, tiled=True)]
    ppermute x0 -> x174, waiting for transfers between devices: none -> 369 us  [the longest x35 159 us: ring_gather(): second.append(lax.ppermute(second[-1], 'dp', behind))]
    dot_general x385 -> x10, matrix products: 425 us -> 64.6 us  [the longest x8 36 us: branch_rows(): jnp.dot(lax.dynamic_slice_in_dim(left, start, rows, 0), right, preferred_...]
    ppermute x0 -> x174, starting transfers between devices: none -> 167 us  [the longest x35 53.8 us: ring_gather(): first.append(lax.ppermute(first[-1], 'dp', ahead))]
    psum x1 -> x0, waiting for transfers between devices: 123 us -> none  [shards(): lax.psum((grad_norm_attn, grad_norm_ffn, heads_gain_grad, conv_query_grad...]
    pallas_call x0 -> x4, Pallas kernels: none -> 114 us  [the longest x1 60.6 us: mixer_bwd(): pl.pallas_call(functools.partial(bwd_kernel, H, DV, n), grid=(n,), in_spe...]
  transfers between devices with their start and end apart: 27 -> 174, of which waited for: 21 -> 74; matrix products, arithmetic and copies ran while one was open for 22% -> 33% of each run, Pallas kernels for 0% -> 11%
where the time goes in v2:
time: 1080 us; the launch traced here: 1070 us
  waiting for transfers between devices  369 us (34%)
  matrix products  300 us (28%)
  starting transfers between devices  167 us (15%)
  Pallas kernels  114 us (11%)
  local copies, waits for them, and re-layouts  69.5 us (6%)
  other arithmetic  42.2 us (4%)
    ppermute x35, waiting for transfers between devices, ring_gather(): second.append(lax.ppermute(second[-1], 'dp', behind))  159 us
    dot_general x80, matrix products, contract_rows(): lax.dot_general(left, right, (((0,), (0,)), ((), ())), preferred_element_...  147 us
    dot_general x14, matrix products, times_transposed(): lax.dot_general(left, right, (((1,), (1,)), ((), ())), preferred_element_...  80.6 us
    ppermute x35, waiting for transfers between devices, ring_scatter(): lax.ppermute(second, 'dp', behind)  61.3 us
    ppermute x35, waiting for transfers between devices, ring_scatter(): lax.ppermute(first, 'dp', ahead)  61.1 us
    pallas_call x1, Pallas kernels, mixer_bwd(): pl.pallas_call(functools.partial(bwd_kernel, H, DV, n), grid=(n,), in_spe...  60.6 us
    ppermute x35, starting transfers between devices, ring_gather(): first.append(lax.ppermute(first[-1], 'dp', ahead))  53.8 us
    ppermute x35, starting transfers between devices, ring_scatter(): lax.ppermute(first, 'dp', ahead)  40 us
  transfers between devices with their start and end apart: 174, of which 74 were waited for; matrix products, arithmetic and copies ran while one was open for 33% of the time, Pallas kernels for 11%

profile of v2, /device:TPU:0, one launch (start us, length us, event | category | flops | bytes accessed | tf_op | source)
XLA Modules:
  0.0 1066.2 jit_solution(11166036586425717084)
XLA Ops:
  11.7 10.1 collective-permute-done.3
  75.9 8.8 collective-permute-done.8
  109.1 11.6 %collective-permute-done.19 = bf16[128,1024]{1,0:T(8,128)(2,1)S(1)} collective-permute-done((bf16[128,1024]{1,0:T(8,128)(2,1)S(1)}, bf16[128,1024]{1,0:T(8,128)(2,1)S(1)}, u32[]{:S(2)}, u32[]{:S(2)}) %collective-permute-start.19) | collective-permute-done | bytes 262176 | tf_op jit(solution)/shard_map/ppermute | solution.py:479
  143.2 13.7 %fusion.272.p_ref.halo_ref = f32[1024,2176]{1,0:T(8,128)} fusion(bf16[1024,2048]{1,0:T(8,128)(2,1)} %constant_dynamic-update-slice_fusion.101, bf16[2048,2176]{1,0:T(8,128)(2,1)S(1)} %constant_dynamic-update-slice_fusion.9), kind=kOutput, calls=%fused_computation.571 | convolution fusion | flops 9126805504 | bytes 22020096 | tf_op jit(solution)/shard_map/dot_general | solution.py:701
  161.5 36.0 %mixer_fwd.1 = (f32[1024,1024]{1,0:T(8,128)}, f32[1024,1024]{1,0:T(8,128)}, f32[1024,512]{1,0:T(8,128)}, f32[8,512,256]{2,1,0:T(8,128)}) custom-call(f32[1024,2176]{1,0:T(8,128)} %fusion.272.p_ref.halo_ref, f32[4,2048]{1,0:T(4,128)} %pad_maximum_fusion.7.taps_ref, f32[8,128]{1,0:T(8,128)} %select_maximum_fusion.par_ref), custom_call_target="tpu_custom_call" | custom-call | flops 35000000512 | bytes 31457280 | tf_op jit(solution)/shard_map/mixer_fwd/pallas_call | solution.py:303
  219.2 8.2 collective-permute-done.36
  227.8 8.3 fusion.273.gate_ref
  238.2 7.5 gate_fwd.1
  278.1 10.0 collective-permute-done.53
  296.4 9.6 collective-permute-done.54
  308.0 9.7 collective-permute-done.47
  330.5 13.9 %collective-permute-done.56 = bf16[128,2816]{1,0:T(8,128)(2,1)S(1)} collective-permute-done((bf16[128,2816]{1,0:T(8,128)(2,1)S(1)}, bf16[128,2816]{1,0:T(8,128)(2,1)S(1)}, u32[]{:S(2)}, u32[]{:S(2)}) %collective-permute-start.56) | collective-permute-done | bytes 720928 | tf_op jit(solution)/shard_map/ppermute | solution.py:479
  352.5 10.9 %collective-permute-done.57 = bf16[128,2816]{1,0:T(8,128)(2,1)S(1)} collective-permute-done((bf16[128,2816]{1,0:T(8,128)(2,1)S(1)}, bf16[128,2816]{1,0:T(8,128)(2,1)S(1)}, u32[]{:S(2)}, u32[]{:S(2)}) %collective-permute-start.57) | collective-permute-done | bytes 720928 | tf_op jit(solution)/shard_map/ppermute | solution.py:479
  364.0 7.2 collective-permute-done.66
  375.8 16.1 %collective-permute-done.67 = bf16[704,256]{1,0:T(8,128)(2,1)S(1)} collective-permute-done((bf16[704,256]{1,0:T(8,128)(2,1)S(1)}, bf16[704,256]{1,0:T(8,128)(2,1)S(1)}, u32[]{:S(2)}, u32[]{:S(2)}) %collective-permute-start.67) | collective-permute-done | bytes 360480 | tf_op jit(solution)/shard_map/ppermute | solution.py:479
  423.3 7.3 collective-permute-done.71
  431.0 14.9 %fusion.274 = f32[1024,2816]{1,0:T(8,128)} fusion(bf16[1024,2048]{1,0:T(8,128)(2,1)S(1)} %constant_dynamic-update-slice_fusion.97, bf16[2048,2816]{1,0:T(8,128)(2,1)S(1)} %constant_dynamic-update-slice_fusion.40), kind=kOutput, calls=%fused_computation.573 | convolution fusion | flops 11811160064 | bytes 27262976 | tf_op jit(solution)/shard_map/dot_general | solution.py:719
  454.7 14.6 %multiply_convert_fusion = (bf16[1024,1408]{1,0:T(8,128)(2,1)S(1)}, bf16[1024,1408]{1,0:T(8,128)(2,1)}, bf16[1024,1408]{1,0:T(8,128)(2,1)}) fusion(f32[1024,2816]{1,0:T(8,128)} %fusion.274, bf16[1024,2048]{1,0:T(8,128)(2,1)S(1)} %constant_dynamic-update-slice_fusion.93, bf16[1408,2048]{1,0:T(8,128)(2,1)} %maximum_dynamic-update-slice_fusion), kind=kOutput, calls=%fused_computation.9 | convolution fusion | flops 5927206912 | bytes 30146560 | tf_op jit(solution)/shard_map/dot_general | solution.py:514
  473.7 7.7 convolution_convert_fusion.5
  481.4 8.7 convolution_convert_fusion.4
  527.0 9.1 fusion.31
  561.5 10.2 multiply_reduce_fusion
  616.5 10.9 %collective-permute-done.111 = bf16[128,2816]{1,0:T(8,128)(2,1)S(1)} collective-permute-done((bf16[128,2816]{1,0:T(8,128)(2,1)S(1)}, bf16[128,2816]{1,0:T(8,128)(2,1)S(1)}, u32[]{:S(2)}, u32[]{:S(2)}) %collective-permute-start.111) | collective-permute-done | bytes 720928 | tf_op jit(solution)/shard_map/ppermute | solution.py:498
  645.1 10.2 gate_bwd.1
  655.3 60.6 %mixer_bwd.1 = (bf16[1024,2176]{1,0:T(8,128)(2,1)}, f32[4,2048]{1,0:T(4,128)}, f32[8,128]{1,0:T(8,128)}) custom-call(f32[1024,2176]{1,0:T(8,128)} %fusion.272.p_ref.halo_ref, f32[1024,2176]{1,0:T(8,128)} %fusion.272.p_ref.halo_ref, f32[4,2048]{1,0:T(4,128)} %pad_maximum_fusion.7.taps_ref, f32[8,128]{1,0:T(8,128)} %select_maximum_fusion.par_ref, ...), custom_call_target="tpu_custom_call" | custom-call | flops 54999998464 | bytes 37748736 | tf_op jit(solution)/shard_map/mixer_bwd/pallas_call | solution.py:334
  722.8 7.8 fusion.102
  759.9 11.2 %collective-permute-done.113 = bf16[128,2816]{1,0:T(8,128)(2,1)S(1)} collective-permute-done((bf16[128,2816]{1,0:T(8,128)(2,1)S(1)}, bf16[128,2816]{1,0:T(8,128)(2,1)S(1)}, u32[]{:S(2)}, u32[]{:S(2)}) %collective-permute-start.113) | collective-permute-done | bytes 720928 | tf_op jit(solution)/shard_map/ppermute | solution.py:498
  782.0 8.6 collective-permute-done.114
  807.4 17.6 %collective-permute-done.81 = bf16[256,2048]{1,0:T(8,128)(2,1)S(1)} collective-permute-done((bf16[256,2048]{1,0:T(8,128)(2,1)S(1)}, bf16[256,2048]{1,0:T(8,128)(2,1)S(1)}, u32[]{:S(2)}, u32[]{:S(2)}) %collective-permute-start.81) | collective-permute-done | bytes 1048608 | tf_op jit(solution)/shard_map/ppermute | solution.py:566
  959.8 9.9 collective-permute-done.136
  992.9 8.6 collective-permute-done.138
  1023.3 9.6 collective-permute-done.140
  (842 shorter events, 652.6 us)
Async XLA Ops:
  27.7 60.7 %collective-permute-start = (bf16[256,2048]{1,0:T(8,128)(2,1)}, bf16[256,2048]{1,0:T(8,128)(2,1)}, u32[]{:S(2)}, u32[]{:S(2)}) collective-permute-start(bf16[256,2048]{1,0:T(8,128)(2,1)} %get-tuple-element.107), channel_id=1, source_target_pairs={{0,1},{1,0},{2,3},{3,2},{4,5},{5,4},{6,7},{7,6},{8,9},{9,8},{10,11... | collective-permute-start | bytes 3145736 | tf_op jit(solution)/shard_map/ppermute | solution.py:551
  27.7 47.1 %collective-permute-start.1 = (bf16[256,2048]{1,0:T(8,128)(2,1)}, bf16[256,2048]{1,0:T(8,128)(2,1)}, u32[]{:S(2)}, u32[]{:S(2)}) collective-permute-start(bf16[256,2048]{1,0:T(8,128)(2,1)} %get-tuple-element.107), channel_id=1, source_target_pairs={{0,2},{2,0},{1,3},{3,1},{4,6},{6,4},{5,7},{7,5},{8,10},{10,8},{9,1... | collective-permute-start | bytes 3145736 | tf_op jit(solution)/shard_map/ppermute | solution.py:550
  74.8 33.1 %collective-permute-start.2 = (bf16[256,2048]{1,0:T(8,128)(2,1)}, bf16[256,2048]{1,0:T(8,128)(2,1)S(1)}, u32[]{:S(2)}, u32[]{:S(2)}) collective-permute-start(bf16[256,2048]{1,0:T(8,128)(2,1)} %collective-permute-done.1), channel_id=1, source_target_pairs={{0,1},{1,0},{2,3},{3,2},{4,5},{5,4},{6,7},{7,6},{8,9},{9,8},{10,11... | collective-permute-start | bytes 3145736 | tf_op jit(solution)/shard_map/ppermute | solution.py:552
  90.7 32.1 %collective-permute-start.16 = (bf16[128,2176]{1,0:T(8,128)(2,1)S(1)}, bf16[128,2176]{1,0:T(8,128)(2,1)S(1)}, u32[]{:S(2)}, u32[]{:S(2)}) collective-permute-start(bf16[128,2176]{1,0:T(8,128)(2,1)S(1)} %collective-permute-done.15), channel_id=1, source_target_pairs={{0,8},{8,16},{16,24},{24,28},{28,20},{20,12},{12,4},{4,0},{1,9},{9... | collective-permute-start | bytes 1671176 | tf_op jit(solution)/shard_map/ppermute | solution.py:478
  157.0 41.5 %collective-permute-start.34 = (bf16[512,256]{1,0:T(8,128)(2,1)}, bf16[512,256]{1,0:T(8,128)(2,1)}, u32[]{:S(2)}, u32[]{:S(2)}) collective-permute-start(bf16[512,256]{1,0:T(8,128)(2,1)} %collective-permute-done.33), channel_id=1, source_target_pairs={{8,0},{16,8},{24,16},{28,24},{20,28},{12,20},{4,12},{0,4},{9,1},{1... | collective-permute-start | bytes 786440 | tf_op jit(solution)/shard_map/ppermute | solution.py:479
  157.5 41.5 %collective-permute-start.40 = (bf16[512,256]{1,0:T(8,128)(2,1)}, bf16[512,256]{1,0:T(8,128)(2,1)}, u32[]{:S(2)}, u32[]{:S(2)}) collective-permute-start(bf16[512,256]{1,0:T(8,128)(2,1)} %collective-permute-done.39), channel_id=1, source_target_pairs={{0,8},{8,16},{16,24},{24,28},{28,20},{20,12},{12,4},{4,0},{1,9},{9... | collective-permute-start | bytes 786440 | tf_op jit(solution)/shard_map/ppermute | solution.py:478
  159.1 41.5 %collective-permute-start.23 = (bf16[128,1024]{1,0:T(8,128)(2,1)}, bf16[128,1024]{1,0:T(8,128)(2,1)}, u32[]{:S(2)}, u32[]{:S(2)}) collective-permute-start(bf16[128,1024]{1,0:T(8,128)(2,1)} %collective-permute-done.22), channel_id=1, source_target_pairs={{8,0},{16,8},{24,16},{28,24},{20,28},{12,20},{4,12},{0,4},{9,1},{1... | collective-permute-start | bytes 786440 | tf_op jit(solution)/shard_map/ppermute | solution.py:479
  159.5 41.0 %collective-permute-start.29 = (bf16[128,1024]{1,0:T(8,128)(2,1)}, bf16[128,1024]{1,0:T(8,128)(2,1)S(1)}, u32[]{:S(2)}, u32[]{:S(2)}) collective-permute-start(bf16[128,1024]{1,0:T(8,128)(2,1)} %collective-permute-done.28), channel_id=1, source_target_pairs={{0,8},{8,16},{16,24},{24,28},{28,20},{20,12},{12,4},{4,0},{1,9},{9... | collective-permute-start | bytes 786440 | tf_op jit(solution)/shard_map/ppermute | solution.py:478
  202.3 45.1 %collective-permute-start.51 = (bf16[128,2816]{1,0:T(8,128)(2,1)}, bf16[128,2816]{1,0:T(8,128)(2,1)}, u32[]{:S(2)}, u32[]{:S(2)}) collective-permute-start(bf16[128,2816]{1,0:T(8,128)(2,1)} %get-tuple-element.119), channel_id=1, source_target_pairs={{0,8},{8,16},{16,24},{24,28},{28,20},{20,12},{12,4},{4,0},{1,9},{9... | collective-permute-start | bytes 2162696 | tf_op jit(solution)/shard_map/ppermute | solution.py:478
  203.8 65.7 %collective-permute-start.52 = (bf16[128,2816]{1,0:T(8,128)(2,1)}, bf16[128,2816]{1,0:T(8,128)(2,1)S(1)}, u32[]{:S(2)}, u32[]{:S(2)}) collective-permute-start(bf16[128,2816]{1,0:T(8,128)(2,1)} %get-tuple-element.118), channel_id=1, source_target_pairs={{8,0},{16,8},{24,16},{28,24},{20,28},{12,20},{4,12},{0,4},{9,1},{1... | collective-permute-start | bytes 2162696 | tf_op jit(solution)/shard_map/ppermute | solution.py:479
  276.1 41.6 %collective-permute-start.47 = (bf16[256,2048]{1,0:T(8,128)(2,1)}, bf16[256,2048]{1,0:T(8,128)(2,1)}, u32[]{:S(2)}, u32[]{:S(2)}) collective-permute-start(bf16[256,2048]{1,0:T(8,128)(2,1)} %fusion.34), channel_id=1, source_target_pairs={{0,2},{2,0},{1,3},{3,1},{4,6},{6,4},{5,7},{7,5},{8,10},{10,8},{9,1... | collective-permute-start | bytes 3145736 | tf_op jit(solution)/shard_map/ppermute | solution.py:566
  295.8 28.9 %collective-permute-start.82 = (bf16[256,2048]{1,0:T(8,128)(2,1)}, bf16[256,2048]{1,0:T(8,128)(2,1)S(1)}, u32[]{:S(2)}, u32[]{:S(2)}) collective-permute-start(bf16[256,2048]{1,0:T(8,128)(2,1)} %get-tuple-element.101), channel_id=1, source_target_pairs={{0,1},{1,0},{2,3},{3,2},{4,5},{5,4},{6,7},{7,6},{8,9},{9,8},{10,11... | collective-permute-start | bytes 3145736 | tf_op jit(solution)/shard_map/ppermute | solution.py:551
  295.8 32.8 %collective-permute-start.84 = (bf16[256,2048]{1,0:T(8,128)(2,1)}, bf16[256,2048]{1,0:T(8,128)(2,1)S(1)}, u32[]{:S(2)}, u32[]{:S(2)}) collective-permute-start(bf16[256,2048]{1,0:T(8,128)(2,1)} %collective-permute-done.83), channel_id=1, source_target_pairs={{0,1},{1,0},{2,3},{3,2},{4,5},{5,4},{6,7},{7,6},{8,9},{9,8},{10,11... | collective-permute-start | bytes 3145736 | tf_op jit(solution)/shard_map/ppermute | solution.py:552
  363.4 30.5 %collective-permute-start.58 = (bf16[128,2816]{1,0:T(8,128)(2,1)S(1)}, bf16[128,2816]{1,0:T(8,128)(2,1)S(1)}, u32[]{:S(2)}, u32[]{:S(2)}) collective-permute-start(bf16[128,2816]{1,0:T(8,128)(2,1)S(1)} %collective-permute-done.57), channel_id=1, source_target_pairs={{8,0},{16,8},{24,16},{28,24},{20,28},{12,20},{4,12},{0,4},{9,1},{1... | collective-permute-start | bytes 2162696 | tf_op jit(solution)/shard_map/ppermute | solution.py:479
  374.1 46.0 %collective-permute-start.64 = (bf16[128,2816]{1,0:T(8,128)(2,1)S(1)}, bf16[128,2816]{1,0:T(8,128)(2,1)S(1)}, u32[]{:S(2)}, u32[]{:S(2)}) collective-permute-start(bf16[128,2816]{1,0:T(8,128)(2,1)S(1)} %collective-permute-done.63), channel_id=1, source_target_pairs={{0,8},{8,16},{16,24},{24,28},{28,20},{20,12},{12,4},{4,0},{1,9},{9... | collective-permute-start | bytes 2162696 | tf_op jit(solution)/shard_map/ppermute | solution.py:478
  519.4 34.6 %collective-permute-start.85 = (bf16[256,2048]{1,0:T(8,128)(2,1)S(1)}, bf16[256,2048]{1,0:T(8,128)(2,1)S(1)}, u32[]{:S(2)}, u32[]{:S(2)}) collective-permute-start(bf16[256,2048]{1,0:T(8,128)(2,1)S(1)} %convolution_convert_fusion.5), channel_id=1, source_target_pairs={{0,1},{1,0},{2,3},{3,2},{4,5},{5,4},{6,7},{7,6},{8,9},{9,8},{10,11... | collective-permute-start | bytes 3145736 | tf_op jit(solution)/shard_map/ppermute | solution.py:567
  519.4 287.9 %collective-permute-start.79 = (bf16[256,2048]{1,0:T(8,128)(2,1)}, bf16[256,2048]{1,0:T(8,128)(2,1)}, u32[]{:S(2)}, u32[]{:S(2)}) collective-permute-start(bf16[256,2048]{1,0:T(8,128)(2,1)} %convolution_convert_fusion.9), channel_id=1, source_target_pairs={{0,1},{1,0},{2,3},{3,2},{4,5},{5,4},{6,7},{7,6},{8,9},{9,8},{10,11... | collective-permute-start | bytes 3145736 | tf_op jit(solution)/shard_map/ppermute | solution.py:567
  554.0 28.2 %collective-permute-start.109 = (bf16[128,2816]{1,0:T(8,128)(2,1)}, bf16[128,2816]{1,0:T(8,128)(2,1)}, u32[]{:S(2)}, u32[]{:S(2)}) collective-permute-start(bf16[128,2816]{1,0:T(8,128)(2,1)} %convolution_convert_fusion.1), channel_id=1, source_target_pairs={{0,8},{8,16},{16,24},{24,28},{28,20},{20,12},{12,4},{4,0},{1,9},{9... | collective-permute-start | bytes 2162696 | tf_op jit(solution)/shard_map/ppermute | solution.py:498
  577.8 38.5 %collective-permute-start.88 = (bf16[256,2048]{1,0:T(8,128)(2,1)S(1)}, bf16[256,2048]{1,0:T(8,128)(2,1)S(1)}, u32[]{:S(2)}, u32[]{:S(2)}) collective-permute-start(bf16[256,2048]{1,0:T(8,128)(2,1)S(1)} %get-tuple-element.98), channel_id=1, source_target_pairs={{0,1},{1,0},{2,3},{3,2},{4,5},{5,4},{6,7},{7,6},{8,9},{9,8},{10,11... | collective-permute-start | bytes 3145736 | tf_op jit(solution)/shard_map/ppermute | solution.py:551
  605.1 31.7 %collective-permute-start.90 = (bf16[256,2048]{1,0:T(8,128)(2,1)S(1)}, bf16[256,2048]{1,0:T(8,128)(2,1)S(1)}, u32[]{:S(2)}, u32[]{:S(2)}) collective-permute-start(bf16[256,2048]{1,0:T(8,128)(2,1)S(1)} %collective-permute-done.89), channel_id=1, source_target_pairs={{0,1},{1,0},{2,3},{3,2},{4,5},{5,4},{6,7},{7,6},{8,9},{9,8},{10,11... | collective-permute-start | bytes 3145736 | tf_op jit(solution)/shard_map/ppermute | solution.py:552
  631.0 117.5 %collective-permute-start.112 = (bf16[128,2816]{1,0:T(8,128)(2,1)}, bf16[128,2816]{1,0:T(8,128)(2,1)}, u32[]{:S(2)}, u32[]{:S(2)}) collective-permute-start(bf16[128,2816]{1,0:T(8,128)(2,1)} %fusion.3), channel_id=1, source_target_pairs={{0,8},{8,16},{16,24},{24,28},{28,20},{20,12},{12,4},{4,0},{1,9},{9... | collective-permute-start | bytes 2162696 | tf_op jit(solution)/shard_map/ppermute | solution.py:498
  636.3 118.0 %collective-permute-start.161 = (bf16[128,2816]{1,0:T(8,128)(2,1)}, bf16[128,2816]{1,0:T(8,128)(2,1)S(1)}, u32[]{:S(2)}, u32[]{:S(2)}) collective-permute-start(bf16[128,2816]{1,0:T(8,128)(2,1)} %fusion.9), channel_id=1, source_target_pairs={{8,0},{16,8},{24,16},{28,24},{20,28},{12,20},{4,12},{0,4},{9,1},{1... | collective-permute-start | bytes 2162696 | tf_op jit(solution)/shard_map/ppermute | solution.py:498
  744.4 58.0 %collective-permute-start.96 = (bf16[256,2048]{1,0:T(8,128)(2,1)S(1)}, bf16[256,2048]{1,0:T(8,128)(2,1)S(1)}, u32[]{:S(2)}, u32[]{:S(2)}) collective-permute-start(bf16[256,2048]{1,0:T(8,128)(2,1)S(1)} %fusion.35), channel_id=1, source_target_pairs={{0,1},{1,0},{2,3},{3,2},{4,5},{5,4},{6,7},{7,6},{8,9},{9,8},{10,11... | collective-permute-start | bytes 3145736 | tf_op jit(solution)/shard_map/ppermute | solution.py:567
  745.9 31.2 %collective-permute-start.97 = (bf16[256,2048]{1,0:T(8,128)(2,1)S(1)}, bf16[256,2048]{1,0:T(8,128)(2,1)S(1)}, u32[]{:S(2)}, u32[]{:S(2)}) collective-permute-start(bf16[256,2048]{1,0:T(8,128)(2,1)S(1)} %fusion.36), channel_id=1, source_target_pairs={{0,1},{1,0},{2,3},{3,2},{4,5},{5,4},{6,7},{7,6},{8,9},{9,8},{10,11... | collective-permute-start | bytes 3145736 | tf_op jit(solution)/shard_map/ppermute | solution.py:564
  790.6 34.4 %collective-permute-start.81 = (bf16[256,2048]{1,0:T(8,128)(2,1)S(1)}, bf16[256,2048]{1,0:T(8,128)(2,1)S(1)}, u32[]{:S(2)}, u32[]{:S(2)}) collective-permute-start(bf16[256,2048]{1,0:T(8,128)(2,1)S(1)} %copy-done.78), channel_id=1, source_target_pairs={{0,2},{2,0},{1,3},{3,1},{4,6},{6,4},{5,7},{7,5},{8,10},{10,8},{9,1... | collective-permute-start | bytes 3145736 | tf_op jit(solution)/shard_map/ppermute | solution.py:566
  796.2 90.0 %collective-permute-start.122 = (bf16[128,2816]{1,0:T(8,128)(2,1)}, bf16[128,2816]{1,0:T(8,128)(2,1)}, u32[]{:S(2)}, u32[]{:S(2)}) collective-permute-start(bf16[128,2816]{1,0:T(8,128)(2,1)} %fusion.6), channel_id=1, source_target_pairs={{0,8},{8,16},{16,24},{24,28},{28,20},{20,12},{12,4},{4,0},{1,9},{9... | collective-permute-start | bytes 2162696 | tf_op jit(solution)/shard_map/ppermute | solution.py:498
  802.5 89.7 %collective-permute-start.164 = (bf16[128,2816]{1,0:T(8,128)(2,1)}, bf16[128,2816]{1,0:T(8,128)(2,1)}, u32[]{:S(2)}, u32[]{:S(2)}) collective-permute-start(bf16[128,2816]{1,0:T(8,128)(2,1)} %fusion.12), channel_id=1, source_target_pairs={{8,0},{16,8},{24,16},{28,24},{20,28},{12,20},{4,12},{0,4},{9,1},{1... | collective-permute-start | bytes 2162696 | tf_op jit(solution)/shard_map/ppermute | solution.py:498
  804.6 58.0 %collective-permute-start.115 = (bf16[512,256]{1,0:T(8,128)(2,1)}, bf16[512,256]{1,0:T(8,128)(2,1)}, u32[]{:S(2)}, u32[]{:S(2)}) collective-permute-start(bf16[512,256]{1,0:T(8,128)(2,1)} %convolution_convert_fusion.15), channel_id=1, source_target_pairs={{0,8},{8,16},{16,24},{24,28},{28,20},{20,12},{12,4},{4,0},{1,9},{9... | collective-permute-start | bytes 786440 | tf_op jit(solution)/shard_map/ppermute | solution.py:498
  957.3 32.4 %collective-permute-start.148 = (bf16[128,1024]{1,0:T(8,128)(2,1)S(1)}, bf16[128,1024]{1,0:T(8,128)(2,1)S(1)}, u32[]{:S(2)}, u32[]{:S(2)}) collective-permute-start(bf16[128,1024]{1,0:T(8,128)(2,1)S(1)} %fusion.95), channel_id=1, source_target_pairs={{8,0},{16,8},{24,16},{28,24},{20,28},{12,20},{4,12},{0,4},{9,1},{1... | collective-permute-start | bytes 786440 | tf_op jit(solution)/shard_map/ppermute | solution.py:498
  991.1 30.0 %collective-permute-start.149 = (bf16[128,1024]{1,0:T(8,128)(2,1)S(1)}, bf16[128,1024]{1,0:T(8,128)(2,1)S(1)}, u32[]{:S(2)}, u32[]{:S(2)}) collective-permute-start(bf16[128,1024]{1,0:T(8,128)(2,1)S(1)} %fusion.96), channel_id=1, source_target_pairs={{8,0},{16,8},{24,16},{28,24},{20,28},{12,20},{4,12},{0,4},{9,1},{1... | collective-permute-start | bytes 786440 | tf_op jit(solution)/shard_map/ppermute | solution.py:498
  1008.5 30.0 %collective-permute-start.143 = (bf16[128,1024]{1,0:T(8,128)(2,1)S(1)}, bf16[128,1024]{1,0:T(8,128)(2,1)S(1)}, u32[]{:S(2)}, u32[]{:S(2)}) collective-permute-start(bf16[128,1024]{1,0:T(8,128)(2,1)S(1)} %fusion.91), channel_id=1, source_target_pairs={{0,8},{8,16},{16,24},{24,28},{28,20},{20,12},{12,4},{4,0},{1,9},{9... | collective-permute-start | bytes 786440 | tf_op jit(solution)/shard_map/ppermute | solution.py:498
  1022.6 29.4 %collective-permute-start.150 = (bf16[128,1024]{1,0:T(8,128)(2,1)S(1)}, bf16[128,1024]{1,0:T(8,128)(2,1)S(1)}, u32[]{:S(2)}, u32[]{:S(2)}) collective-permute-start(bf16[128,1024]{1,0:T(8,128)(2,1)S(1)} %fusion.97), channel_id=1, source_target_pairs={{8,0},{16,8},{24,16},{28,24},{20,28},{12,20},{4,12},{0,4},{9,1},{1... | collective-permute-start | bytes 786440 | tf_op jit(solution)/shard_map/ppermute | solution.py:498
  (244 other events, 3964.4 us)

commit v3 on v2

--- a/solution.py
+++ b/solution.py
@@ -92,19 +92,31 @@
     return exact_sum(ones, log_decay, 1), log_decay, jax.nn.sigmoid(tail), raised
 
 
-def fwd_kernel(H, DV, NC, p_ref, taps_ref, par_ref, o_ref, u_ref, t_ref, s_ref, S, ext):
+def fwd_kernel(H, DV, NC, start, p_ref, halo_ref, taps_ref, par_ref, *refs):
     C = CHUNK
     R = NC * C
     W = H * (2 * DK + DV)
-
-    @pl.when(pl.program_id(0) == 0)
-    def _():
-        S[...] = jnp.zeros_like(S)
-        ext[0:HALO, :] = jnp.zeros((HALO, W), F32)
-
-    @pl.when(pl.program_id(0) > 0)
-    def _():
-        ext[0:HALO, :] = ext[R : R + HALO, :]
+    o_ref, u_ref, t_ref, s_ref, S, ext = refs[-6:]
+    step = pl.program_id(0)
+
+    if start == 0:
+
+        @pl.when(step == 0)
+        def _():
+            S[...] = jnp.zeros_like(S)
+            ext[0:HALO, :] = jnp.zeros((HALO, W), F32)
+
+        @pl.when(step > 0)
+        def _():
+            ext[0:HALO, :] = halo_ref[:, 0:W]
+
+    else:
+
+        @pl.when(step == 0)
+        def _():
+            S[...] = refs[0][...]
+
+        ext[0:HALO, :] = halo_ref[:, 0:W]
 
     ext[HALO : HALO + R, :] = p_ref[:, 0:W]
     i, j = grids(C)
@@ -160,29 +172,35 @@
 
 
 def bwd_kernel(
-    H, DV, steps, p_ref, halo_ref, taps_ref, par_ref, u_ref, t_ref, s_ref, do_ref,
-    dp_ref, dtaps_ref, dpar_ref, dS, ext, dext,
+    H, DV, end, first, p_ref, halo_ref, taps_ref, par_ref, u_ref, t_ref, s_ref, do_ref, *refs
 ):
     C = CHUNK
     W = H * (2 * DK + DV)
+    dp_ref, dtaps_ref, dpar_ref, dS, carry_ref, ext, dext = refs[-7:]
     step = pl.program_id(0)
 
     @pl.when(step == 0)
     def _():
-        dS[...] = jnp.zeros_like(dS)
-        dext[C : C + HALO, :] = jnp.zeros((HALO, W), F32)
-        dtaps_ref[...] = jnp.zeros_like(dtaps_ref)
-        dpar_ref[...] = jnp.zeros_like(dpar_ref)
+        if first:
+            dS[...] = jnp.zeros_like(dS)
+            dext[C : C + HALO, :] = jnp.zeros((HALO, W), F32)
+            dtaps_ref[...] = jnp.zeros_like(dtaps_ref)
+            dpar_ref[...] = jnp.zeros_like(dpar_ref)
+        else:
+            dS[...] = refs[3][...]
+            dext[C : C + HALO, :] = refs[4][...]
+            dtaps_ref[...] = refs[1][...]
+            dpar_ref[...] = refs[2][...]
 
     @pl.when(step > 0)
     def _():
         dext[C : C + HALO, :] = dext[0:HALO, :]
 
-    @pl.when(step == steps - 1)
+    @pl.when(step == end)
     def _():
         ext[0:HALO, :] = jnp.zeros((HALO, W), F32)
 
-    @pl.when(step < steps - 1)
+    @pl.when(step < end)
     def _():
         ext[0:HALO, :] = halo_ref[:, 0:W]
 
@@ -282,9 +300,11 @@
     dp_ref[:, W : W + 128] = d_tail.astype(BF)
     dpar_ref[0:1, :] += jnp.sum(d_log * log_decay, axis=0, keepdims=True)
     dpar_ref[1:2, :] += jnp.sum(d_raised, axis=0, keepdims=True)
-
-
-LIMIT = pltpu.CompilerParams(vmem_limit_bytes=56 * 2**20)
+    carry_ref[...] = dext[0:HALO, :]
+
+
+def room(mebibytes):
+    return pltpu.CompilerParams(vmem_limit_bytes=mebibytes * 2**20)
 
 
 def row_block(rows, width, at=lambda s: s):
@@ -295,45 +315,66 @@
     return pl.BlockSpec(array.shape, lambda s: (0,) * array.ndim)
 
 
-def mixer_fwd(projected, taps, par, heads, NC=2):
+def mixer_fwd(projected, taps, par, heads, start, count, before=None, NC=2):
     L, wide = projected.shape
     H, C = heads, CHUNK
-    DV = taps.shape[1] // H - 2 * DK
+    W = taps.shape[1]
+    DV = W // H - 2 * DK
     f = jax.ShapeDtypeStruct
+    base = start // NC
+    shapes = [f((L, H * DV), F32), f((L, H * DV), F32), f((L, H * C), F32), f((L // C, H * DK, DV), F32)]
+    more, more_specs, aliases = [], [], {}
+    if before is not None:
+        more = [before[4]] + list(before[:4])
+        more_specs = [whole_block(before[4])] + [pl.BlockSpec(memory_space=pl.ANY)] * 4
+        aliases = {5 + n: n for n in range(4)}
     return pl.pallas_call(
-        functools.partial(fwd_kernel, H, DV, NC),
-        grid=(L // C // NC,),
-        in_specs=[row_block(NC * C, wide), whole_block(taps), whole_block(par)],
+        functools.partial(fwd_kernel, H, DV, NC, start),
+        grid=(count // NC,),
+        in_specs=[
+            row_block(NC * C, wide, lambda s: base + s),
+            row_block(HALO, wide, lambda s: jnp.maximum((base + s) * (NC * C // HALO) - 1, 0)),
+            whole_block(taps),
+            whole_block(par),
+        ]
+        + more_specs,
         out_specs=[
-            row_block(NC * C, H * DV),
-            row_block(NC * C, H * DV),
-            row_block(NC * C, H * C),
-            pl.BlockSpec((NC, H * DK, DV), lambda s: (s, 0, 0)),
+            row_block(NC * C, H * DV, lambda s: base + s),
+            row_block(NC * C, H * DV, lambda s: base + s),
+            row_block(NC * C, H * C, lambda s: base + s),
+            pl.BlockSpec((NC, H * DK, DV), lambda s: (base + s, 0, 0)),
+            pl.BlockSpec((H * DK, DV), lambda s: (0, 0)),
         ],
-        out_shape=[
-            f((L, H * DV), F32), f((L, H * DV), F32), f((L, H * C), F32), f((L // C, H * DK, DV), F32),
-        ],
-        scratch_shapes=[pltpu.VMEM((H * DK, DV), F32), pltpu.VMEM((NC * C + HALO, taps.shape[1]), F32)],
-        compiler_params=LIMIT,
-        cost_estimate=pl.CostEstimate(flops=35 * 10**9, bytes_accessed=30 * 2**20, transcendentals=0),
+        out_shape=shapes + [f((H * DK, DV), F32)],
+        scratch_shapes=[pltpu.VMEM((NC * C + HALO, W), F32)],
+        input_output_aliases=aliases,
+        compiler_params=room(22),
+        cost_estimate=pl.CostEstimate(
+            flops=3 * 10**9 * count, bytes_accessed=3 * 2**20 * count, transcendentals=0
+        ),
         name="mixer_fwd",
-    )(projected, taps, par)
-
-
-def mixer_bwd(projected, taps, par, written, inverse, states, grad_heads, heads):
+    )(projected, projected, taps, par, *more)
+
+
+def mixer_bwd(projected, taps, par, written, inverse, states, grad_heads, heads, end, count, before=None):
     L, wide = projected.shape
     H, C = heads, CHUNK
-    DV = taps.shape[1] // H - 2 * DK
     W = taps.shape[1]
-    n = L // C
+    DV = W // H - 2 * DK
     f = jax.ShapeDtypeStruct
 
     def back(s):
-        return n - 1 - s
-
+        return end - s
+
+    more, more_specs, aliases = [], [], {}
+    if before is not None:
+        more = list(before)
+        more_specs = [pl.BlockSpec(memory_space=pl.ANY)] + [whole_block(a) for a in before[1:]]
+        aliases = {8: 0}
+    state, halo = f((H * DK, DV), F32), f((HALO, W), F32)
     return pl.pallas_call(
-        functools.partial(bwd_kernel, H, DV, n),
-        grid=(n,),
+        functools.partial(bwd_kernel, H, DV, end, before is None),
+        grid=(count,),
         in_specs=[
             row_block(C, wide, back),
             row_block(HALO, wide, lambda s: jnp.maximum(back(s) * (C // HALO) - 1, 0)),
@@ -343,18 +384,24 @@
             row_block(C, H * C, back),
             pl.BlockSpec((1, H * DK, DV), lambda s: (back(s), 0, 0)),
             row_block(C, H * DV, back),
+        ]
+        + more_specs,
+        out_specs=[
+            row_block(C, wide, back),
+            whole_block(taps),
+            whole_block(par),
+            whole_block(state),
+            whole_block(halo),
         ],
-        out_specs=[row_block(C, wide, back), whole_block(taps), whole_block(par)],
-        out_shape=[f((L, wide), BF), f(taps.shape, F32), f(par.shape, F32)],
-        scratch_shapes=[
-            pltpu.VMEM((H * DK, DV), F32),
-            pltpu.VMEM((C + HALO, W), F32),
-            pltpu.VMEM((C + HALO, W), F32),
-        ],
-        compiler_params=LIMIT,
-        cost_estimate=pl.CostEstimate(flops=55 * 10**9, bytes_accessed=36 * 2**20, transcendentals=0),
+        out_shape=[f((L, wide), BF), f(taps.shape, F32), f(par.shape, F32), state, halo],
+        scratch_shapes=[pltpu.VMEM((C + HALO, W), F32), pltpu.VMEM((C + HALO, W), F32)],
+        input_output_aliases=aliases,
+        compiler_params=room(22),
+        cost_estimate=pl.CostEstimate(
+            flops=6 * 10**9 * count, bytes_accessed=4 * 2**20 * count, transcendentals=0
+        ),
         name="mixer_bwd",
-    )(projected, projected, taps, par, written, inverse, states, grad_heads)
+    )(projected, projected, taps, par, written, inverse, states, grad_heads, *more)
 
 
 def gate_fwd_kernel(DV, o_ref, gate_ref, gain_ref, out_ref):
@@ -374,6 +421,7 @@
         in_specs=[row_block(rows, width), row_block(rows, width), whole_block(gain)],
         out_specs=row_block(rows, width),
         out_shape=jax.ShapeDtypeStruct((L, width), BF),
+        compiler_params=room(12),
         cost_estimate=pl.CostEstimate(flops=5 * 10**9, bytes_accessed=10 * 2**20, transcendentals=0),
         name="gate_fwd",
     )(heads_out, gate_proj, gain)
@@ -411,6 +459,7 @@
         in_specs=[row_block(rows, width), row_block(rows, width), whole_block(gain), row_block(rows, width)],
         out_specs=[row_block(rows, width), row_block(rows, width), whole_block(gain)],
         out_shape=[f((L, width), F32), f((L, width), BF), f(gain.shape, F32)],
+        compiler_params=room(14),
         cost_estimate=pl.CostEstimate(flops=7 * 10**9, bytes_accessed=18 * 2**20, transcendentals=0),
         name="gate_bwd",
     )(heads_out, gate_proj, gain, grad_mixer)
@@ -430,78 +479,160 @@
     return ahead, [(d, s) for s, d in ahead]
 
 
-def to_relative(array):
+def behind(d):
     n = lax.axis_size("dp")
-    block = array.shape[-1] // n
-    place = place_of(lax.axis_index("dp"), n)
-    return jnp.concatenate(
-        [
-            lax.dynamic_slice_in_dim(
-                array, at_place((place - d + n) % n, n) * block, block, array.ndim - 1
+    return at_place((place_of(lax.axis_index("dp"), n) - d + n) % n, n)
+
+
+def after(values, token):
+    return lax.optimization_barrier((values, token))[0]
+
+
+class GatherRing:
+    def __init__(self, shard):
+        half = shard.shape[0] // 2
+        self.first, self.second = [shard[:half]], [shard[half:]]
+        self.n = lax.axis_size("dp")
+
+    def send(self, token):
+        ahead, back = ring_pairs(self.n)
+        first, second = after((self.first[-1], self.second[-1]), token)
+        self.first.append(lax.ppermute(first, "dp", ahead))
+        self.second.append(lax.ppermute(second, "dp", back))
+
+    def last(self):
+        return self.first[-1], self.second[-1]
+
+    def through(self):
+        return len(self.first) == self.n
+
+    def finish(self, widths):
+        half = self.first[0].shape[0]
+        fulls = [jnp.zeros((self.n * 2 * half, width), BF) for width in widths]
+        for hop in range(self.n):
+            for piece, at in (
+                (self.first[hop], behind(hop) * 2 * half),
+                (self.second[hop], behind(self.n - hop) * 2 * half + half),
+            ):
+                fulls = [
+                    lax.dynamic_update_slice(full, part, (at, 0))
+                    for full, part in zip(fulls, columns(piece, widths))
+                ]
+        return fulls
+
+
+def land_kernel(widths, *refs):
+    count = len(widths)
+    first, second = refs[0], refs[1]
+    terms = refs[2 : 2 + 2 * count]
+    for arrived, mine, out in (
+        (first, terms[:count], refs[-2]),
+        (second, terms[count:], refs[-1]),
+    ):
+        start = 0
+        for width, term in zip(widths, mine):
+            cut = slice(start, start + width)
+            out[:, cut] = (arrived[:, cut].astype(F32) + term[...].astype(F32)).astype(BF)
+            start += width
+
+
+def landed(flying, terms):
+    widths = [term.shape[1] for term in terms[0]]
+    rows, wide = flying[0].shape
+    steps = 2
+    arrays = list(flying) + list(terms[0]) + list(terms[1])
+    return pl.pallas_call(
+        functools.partial(land_kernel, widths),
+        grid=(steps,),
+        in_specs=[row_block(rows // steps, a.shape[1]) for a in arrays],
+        out_specs=[row_block(rows // steps, wide)] * 2,
+        out_shape=[jax.ShapeDtypeStruct((rows, wide), BF)] * 2,
+        compiler_params=room(10),
+        cost_estimate=pl.CostEstimate(flops=10**6, bytes_accessed=10**6, transcendentals=0),
+        name="land",
+    )(*arrays)
+
+
+class ScatterRing:
+    def __init__(self, pairs, token):
+        self.n = lax.axis_size("dp")
+        self.hop = 0
+        self.pairs = pairs
+        self.sums = tuple(
+            jnp.concatenate(terms, axis=1).astype(BF)
+            for terms in (self.terms_of(1, 0, token), self.terms_of(self.n - 1, 1, token))
+        )
+
+    def terms_of(self, place, side, token):
+        terms = []
+        for features, grads in self.pairs:
+            half = features.shape[1] // self.n // 2
+            at = behind(place % self.n) * (2 * half) + side * half
+            left = lax.dynamic_slice_in_dim(features, at, half, 1)
+            terms.append(contract_rows(*after((left, grads), token)))
+        return terms
+
+    def send(self, token):
+        ahead, back = ring_pairs(self.n)
+        first, second = after(self.sums, token)
+        self.flying = lax.ppermute(first, "dp", ahead), lax.ppermute(second, "dp", back)
+
+    def multiply(self, token):
+        kind = F32 if self.hop == self.n - 2 else BF
+        terms = (
+            self.terms_of(self.hop + 2, 0, token),
+            self.terms_of(2 * self.n - 2 - self.hop, 1, token),
+        )
+        self.terms = lax.optimization_barrier([[t.astype(kind) for t in side] for side in terms])
+        return self.terms
+
+    def land(self, token):
+        self.hop += 1
+        flying, terms = after((self.flying, self.terms), token)
+        if self.hop == self.n - 1:
+            self.sums = tuple(
+                [
+                    x.astype(F32) + y
+                    for x, y in zip(columns(arrived, [term.shape[1] for term in mine]), mine)
+                ]
+                for arrived, mine in zip(flying, terms)
             )
-            for d in range(n)
-        ],
-        axis=-1,
-    )
-
-
-def to_absolute(array):
-    n = lax.axis_size("dp")
-    block = array.shape[-1] // n
-    place = place_of(lax.axis_index("dp"), n)
-    return jnp.concatenate(
-        [
-            lax.dynamic_slice_in_dim(
-                array,
-                ((place - place_of(jnp.int32(index), n) + n) % n) * block,
-                block,
-                array.ndim - 1,
-            )
-            for index in range(n)
-        ],
-        axis=-1,
-    )
-
-
-def after(array, other):
-    return lax.optimization_barrier((array, other))[0]
-
-
-def ring_gather(shard, earlier=None, hops=0):
-    n = lax.axis_size("dp")
-    ahead, behind = ring_pairs(n)
-    half = shard.shape[0] // 2
-    if earlier is not None:
-        shard = after(shard, earlier[min(hops, n - 1)][0])
-    first, second = [shard[:half]], [shard[half:]]
-    for _ in range(n - 1):
-        first.append(lax.ppermute(first[-1], "dp", ahead))
-        second.append(lax.ppermute(second[-1], "dp", behind))
-    return [(first[d], second[(n - d) % n]) for d in range(n)]
-
-
-def stacked(pieces):
-    return jnp.concatenate([half for pair in pieces for half in pair], axis=0)
-
-
-def side_by_side(pieces):
-    return jnp.concatenate([jnp.concatenate(pair, axis=0) for pair in pieces], axis=1)
-
-
-def ring_scatter(first_of, second_of, earlier=()):
-    n = lax.axis_size("dp")
-    ahead, behind = ring_pairs(n)
-    first, second = first_of(1 % n).astype(BF), second_of(n - 1).astype(BF)
-    first, second = after((first, second), earlier)
-    hops = []
-    for step in range(n - 1):
-        first, second = lax.ppermute(first, "dp", ahead), lax.ppermute(second, "dp", behind)
-        hops.append(first)
-        first = first.astype(F32) + first_of((step + 2) % n)
-        second = second.astype(F32) + second_of(n - 2 - step)
-        if step < n - 2:
-            first, second = first.astype(BF), second.astype(BF)
-    return jnp.concatenate((first, second), axis=0), hops
+        else:
+            self.sums = tuple(landed(flying, terms))
+        return self.sums
+
+    def done(self):
+        return self.hop == self.n - 1
+
+    def results(self):
+        return [jnp.concatenate(halves, axis=0) for halves in zip(*self.sums)]
+
+
+def slot(token, rings, pieces=(), gathers=()):
+    rings = [ring for ring in rings if not ring.done()]
+    gathers = [ring for ring in gathers if not ring.through()]
+    for ring in rings:
+        ring.send(token)
+    for ring in gathers:
+        ring.send(token)
+    token = [ring.multiply(token) for ring in rings] or token
+    for piece in pieces:
+        token = piece(token)
+    token = [ring.land(token) for ring in rings] or token
+    if gathers:
+        token = token, [ring.last() for ring in gathers]
+    return token
+
+
+def run_out(token, rings, pieces=(), gathers=()):
+    pieces = list(pieces)
+    while (
+        pieces
+        or any(not ring.done() for ring in rings)
+        or any(not ring.through() for ring in gathers)
+    ):
+        token = slot(token, rings, [pieces.pop(0)] if pieces else (), gathers)
+    return token
 
 
 def contract_rows(left, right):
@@ -516,76 +647,103 @@
     )
 
 
-def scatter_rows_of(features, grads, earlier=()):
-    block = features.shape[1] // lax.axis_size("dp")
-    half = block // 2
-
-    def part(d, start):
-        return contract_rows(features[:, d * block + start : d * block + start + half], grads)
-
-    return ring_scatter(lambda d: part(d, 0), lambda d: part(d, half), earlier)
-
-
-def scatter_columns_of(features, grads, earlier=()):
-    block = grads.shape[1] // lax.axis_size("dp")
-    half = features.shape[1] // 2
-
-    def part(d, left):
-        return contract_rows(left, grads[:, d * block : (d + 1) * block])
-
-    return ring_scatter(
-        lambda d: part(d, features[:, :half]), lambda d: part(d, features[:, half:]), earlier
-    )
-
-
 CORES = [(0, 1), (1, 0), (2, 3), (3, 2)]
 PAIRS = [(0, 2), (2, 0), (1, 3), (3, 1)]
 
 
+class Spread:
+    def __init__(self, block):
+        self.block = block
+        self.plain = lax.axis_size("tensor") != 4
+        if not self.plain:
+            self.far = lax.ppermute(block, "tensor", PAIRS)
+            self.near = lax.ppermute(block, "tensor", CORES)
+
+    def turn(self, token):
+        if self.plain:
+            return token
+        far = after(self.far, token)
+        self.far_near = lax.ppermute(far, "tensor", CORES)
+        return far
+
+    def rows(self, token=()):
+        if self.plain:
+            return lax.all_gather(after(self.block, token), "tensor", axis=0, tiled=True)
+        rank = lax.axis_index("tensor")
+        rows, width = self.block.shape
+        out = jnp.zeros((4 * rows, width), self.block.dtype)
+        parts = after((self.block, self.near, self.far, self.far_near), token)
+        for flip, part in enumerate(parts):
+            out = lax.dynamic_update_slice_in_dim(out, part, (rank ^ flip) * rows, 0)
+        return out
+
+
 def spread_rows(block):
-    if lax.axis_size("tensor") != 4:
-        return lax.all_gather(block, "tensor", axis=0, tiled=True)
-    rank = lax.axis_index("tensor")
-    rows = block.shape[0]
-    far = lax.ppermute(block, "tensor", PAIRS)
-    near = lax.ppermute(block, "tensor", CORES)
-    far_near = lax.ppermute(far, "tensor", CORES)
-    out = jnp.zeros((4 * rows,) + block.shape[1:], block.dtype)
-    for part, flip in ((block, 0), (near, 1), (far, 2), (far_near, 3)):
-        out = lax.dynamic_update_slice_in_dim(out, part, (rank ^ flip) * rows, 0)
-    return out
-
-
-def sum_rows(product, rows):
-    if lax.axis_size("tensor") != 4:
-        whole = jnp.concatenate([product(i * rows) for i in range(lax.axis_size("tensor"))], axis=0)
-        return lax.psum_scatter(whole, "tensor", scatter_dimension=0, tiled=True)
-    rank = lax.axis_index("tensor")
-    far_near = lax.ppermute(product((rank ^ 3) * rows).astype(BF), "tensor", CORES)
-    far = product((rank ^ 2) * rows) + far_near.astype(F32)
-    far = lax.ppermute(far.astype(BF), "tensor", PAIRS)
-    near = lax.ppermute(product((rank ^ 1) * rows).astype(BF), "tensor", CORES)
-    return product(rank * rows) + near.astype(F32) + far.astype(F32)
-
-
-def branch_rows(left, right, rows):
-    return sum_rows(
-        lambda start: jnp.dot(
-            lax.dynamic_slice_in_dim(left, start, rows, 0), right, preferred_element_type=F32
-        ),
-        rows,
-    )
-
-
-def back_rows(pairs, rows):
-    def product(start):
+    spread = Spread(block)
+    spread.turn(())
+    return spread.rows()
+
+
+class RowSum:
+    def __init__(self, product, rows):
+        self.product, self.rows = product, rows
+        self.rank = lax.axis_index("tensor")
+        self.plain = lax.axis_size("tensor") != 4
+
+    def term(self, flip, token):
+        return self.product((self.rank ^ flip) * self.rows, token)
+
+    def far(self, token):
+        if self.plain:
+            whole = [self.product(i * self.rows, token) for i in range(lax.axis_size("tensor"))]
+            self.total = lax.psum_scatter(
+                jnp.concatenate(whole, axis=0), "tensor", scatter_dimension=0, tiled=True
+            )
+            return self.total
+        self.sent = self.term(3, token).astype(BF)
+        self.far_near = lax.ppermute(self.sent, "tensor", CORES)
+        return self.sent
+
+    def far_sum(self, token):
+        if self.plain:
+            return token
+        total = (self.term(2, token) + self.far_near.astype(F32)).astype(BF)
+        self.from_far = lax.ppermute(total, "tensor", PAIRS)
+        return total
+
+    def near(self, token):
+        if self.plain:
+            return token
+        sent = self.term(1, token).astype(BF)
+        self.from_near = lax.ppermute(sent, "tensor", CORES)
+        return sent
+
+    def own(self, token):
+        if self.plain:
+            return token
+        self.mine = self.term(0, token)
+        return self.mine
+
+    def result(self, token):
+        if self.plain:
+            return after(self.total, token)
+        mine = after(self.mine, token)
+        return mine + self.from_near.astype(F32) + self.from_far.astype(F32)
+
+    def pieces(self):
+        return [self.far, self.far_sum, self.near, self.own]
+
+
+def summed_rows(pairs, rows):
+    def product(start, token):
         total = None
         for grads, weight in pairs:
-            part = times_transposed(lax.dynamic_slice_in_dim(grads, start, rows, 0), weight)
+            part, other = after((lax.dynamic_slice_in_dim(grads, start, rows, 0), weight), token)
+            part = times_transposed(part, other)
             total = part if total is None else total + part
         return total
 
-    return sum_rows(product, rows)
+    return RowSum(product, rows)
 
 
 def sum_over(values, axis):
@@ -682,24 +840,27 @@
         jnp.concatenate((w_query, w_key, w_value, w_decay, w_beta), axis=1), ((0, 0), (0, fill))
     )
     ffn_width = w_ffn_gate.shape[1]
-    mixed_ring = ring_gather(mixed_shard)
-    gate_ring = ring_gather(w_out_gate, mixed_ring, 6)
-    output_ring = ring_gather(w_output, mixed_ring, 7)
-    ffn_ring = ring_gather(jnp.concatenate((w_ffn_gate, w_ffn_up), axis=1), gate_ring, 6)
-    down_ring = ring_gather(w_ffn_down, ffn_ring, 6)
-    mixed_full, gate_full, ffn_full = stacked(mixed_ring), stacked(gate_ring), stacked(ffn_ring)
-    output_full, down_full = side_by_side(output_ring), side_by_side(down_ring)
-
-    gain_attn = to_relative(norm_attn)
-    gain_ffn = to_relative(norm_ffn)
-    stream_in = to_relative(inputs).astype(jnp.float32)
-    grad_out = valid * to_relative(cotangent).astype(jnp.float32)
+    kept = {}
+    mixed_ring = GatherRing(mixed_shard)
+    mixed_ring.send(())
+    gate_shards, ffn_shards, rows_in = after(
+        ((w_out_gate, w_output), (w_ffn_gate, w_ffn_up, w_ffn_down), (inputs, cotangent)),
+        mixed_ring.last(),
+    )
+    inputs, cotangent = rows_in
+    token = run_out(mixed_ring.last(), (), (), (mixed_ring,))
+    gate_ring = GatherRing(jnp.concatenate((gate_shards[0], gate_shards[1].T), axis=1))
+    ffn_ring = GatherRing(
+        jnp.concatenate((ffn_shards[0], ffn_shards[1], ffn_shards[2].T), axis=1)
+    )
+    [mixed_full] = mixed_ring.finish([mixed_shard.shape[1]])
+
+    gain_attn = norm_attn
+    gain_ffn = norm_ffn
+    stream_in = inputs.astype(jnp.float32)
+    grad_out = valid * cotangent.astype(jnp.float32)
     inverse_in = lax.rsqrt(jnp.mean(stream_in * stream_in, axis=1, keepdims=True) + 1e-06)
     full_in = spread_rows((stream_in * inverse_in * gain_attn).astype(jnp.bfloat16))
-    grad_ffn = spread_rows(grad_out.astype(jnp.bfloat16))
-
-    projected = jnp.dot(full_in, mixed_full, preferred_element_type=jnp.float32)
-    gate_proj = jnp.dot(full_in, gate_full, preferred_element_type=jnp.float32)
 
     def here(array):
         size = array.shape[-1] // lax.axis_size("tensor")
@@ -710,19 +871,179 @@
         jnp.stack((-jnp.exp(here(decay_log)), here(decay_bias))), ((0, 6), (0, 128 - heads_here))
     )
     gain_heads = norm_heads[None, :]
-    heads_out, written, inverse, states = mixer_fwd(projected, taps, par, heads_here)
-    mixer = gate_fwd(heads_out, gate_proj, gain_heads)
-    branch_attn = branch_rows(mixer, output_full, rows)
-    stream = stream_in + branch_attn
-    inverse_mid = lax.rsqrt(jnp.mean(stream * stream, axis=1, keepdims=True) + 1e-06)
-    full_mid = spread_rows((stream * inverse_mid * gain_ffn).astype(jnp.bfloat16))
-    ffn_in = jnp.dot(full_mid, ffn_full, preferred_element_type=jnp.float32)
-    ffn_gate, ffn_up = ffn_in[:, :ffn_width], ffn_in[:, ffn_width:]
+    chunks = full_in.shape[0] // CHUNK
+    parts = 4
+
+    def project(token):
+        kept["projected"] = jnp.dot(
+            *after((full_in, mixed_full), token), preferred_element_type=jnp.float32
+        )
+        kept["forward"] = None
+        return kept["projected"]
+
+    def forward_part(start):
+        def piece(token):
+            kept["forward"] = mixer_fwd(
+                after(kept["projected"], token),
+                taps,
+                par,
+                heads_here,
+                start,
+                chunks // parts,
+                kept["forward"],
+            )
+            return kept["forward"][4]
+
+        return piece
+
+    token = run_out(
+        token,
+        (),
+        [project] + [forward_part(i * (chunks // parts)) for i in range(parts)],
+        (gate_ring,),
+    )
+    projected = kept["projected"]
+    heads_out, written, inverse, states, _ = kept["forward"]
+    gate_full, output_full = gate_ring.finish([w_out_gate.shape[1], w_output.shape[0]])
+
+    def gate(token):
+        kept["gate"] = jnp.dot(
+            *after((full_in, gate_full), token), preferred_element_type=jnp.float32
+        )
+        kept["mixer"] = gate_fwd(heads_out, kept["gate"], gain_heads)
+        return kept["mixer"]
+
+    def attend(token):
+        kept["attn"] = summed_rows(((kept["mixer"], output_full),), rows)
+        return kept["attn"].far_sum(kept["attn"].far(token))
+
+    def attend_own(token):
+        return kept["attn"].own(kept["attn"].near(token))
+
+    def middle(token):
+        kept["branch"] = kept["attn"].result(token)
+        stream = stream_in + kept["branch"]
+        kept["stream"] = stream
+        kept["inverse"] = lax.rsqrt(jnp.mean(stream * stream, axis=1, keepdims=True) + 1e-06)
+        normed = (stream * kept["inverse"] * gain_ffn).astype(jnp.bfloat16)
+        kept["full_mid"] = spread_rows(normed)
+        return normed
+
+    token = run_out(token, (), [gate, attend, attend_own, middle], (ffn_ring,))
+    gate_proj, mixer, branch_attn = kept["gate"], kept["mixer"], kept["branch"]
+    stream, inverse_mid, full_mid = kept["stream"], kept["inverse"], kept["full_mid"]
+    ffn_gate_full, ffn_up_full, down_full = ffn_ring.finish(
+        [ffn_width, ffn_width, w_ffn_down.shape[0]]
+    )
+    grad_ffn = spread_rows(after(grad_out.astype(jnp.bfloat16), full_mid))
+
+    token, full_mid_in = after((token, full_mid), ffn_ring.last())
+    ffn_gate = jnp.dot(full_mid_in, ffn_gate_full, preferred_element_type=jnp.float32)
+    ffn_up = jnp.dot(full_mid_in, ffn_up_full, preferred_element_type=jnp.float32)
     sigma = jax.nn.sigmoid(ffn_gate)
     silu_gate = ffn_gate * sigma
     hidden = (silu_gate * ffn_up).astype(jnp.bfloat16)
-    branch_ffn = branch_rows(hidden, down_full, rows)
-    outputs = to_absolute((valid * (stream + branch_ffn)).astype(jnp.bfloat16))
+    grad_hidden = jnp.dot(grad_ffn, down_full, preferred_element_type=jnp.float32)
+    grad_gate_in = grad_hidden * ffn_up * sigma * (1.0 + ffn_gate * (1.0 - sigma))
+    grad_gate_in = grad_gate_in.astype(jnp.bfloat16)
+    grad_up_in = (grad_hidden * silu_gate).astype(jnp.bfloat16)
+    token = grad_gate_in, grad_up_in, hidden
+    ffn_scatter = ScatterRing(
+        ((full_mid, grad_gate_in), (full_mid, grad_up_in), (grad_ffn, hidden)), token
+    )
+    token = ffn_scatter.sums
+    mid_sum = summed_rows(((grad_gate_in, ffn_gate_full), (grad_up_in, ffn_up_full)), rows)
+
+    def mid_own(token):
+        return mid_sum.own(mid_sum.near(token))
+
+    def middle_back(token):
+        through, kept["norm_ffn"] = norm_back(stream, inverse_mid, gain_ffn, mid_sum.result(token))
+        kept["grad_stream"] = grad_out + through
+        low = kept["grad_stream"].astype(jnp.bfloat16)
+        kept["spread"] = Spread(low)
+        return low
+
+    def turn(token):
+        token = ffn_sum.far_sum(ffn_sum.far(token))
+        return kept["spread"].turn(token)
+
+    def attend_back(token):
+        kept["grad_attn"] = kept["spread"].rows(token)
+        grad_mixer = jnp.dot(
+            *after((kept["grad_attn"], output_full), token), preferred_element_type=jnp.float32
+        )
+        kept["gate_back"] = gate_bwd(heads_out, gate_proj, gain_heads, grad_mixer)
+        kept["backward"] = None
+        return kept["gate_back"][0]
+
+    def backward_part(end):
+        def piece(token):
+            kept["backward"] = mixer_bwd(
+                projected,
+                taps,
+                par,
+                written,
+                inverse,
+                states,
+                after(kept["gate_back"][0], token),
+                heads_here,
+                end,
+                chunks // parts,
+                kept["backward"],
+            )
+            return kept["backward"][3]
+
+        return piece
+
+    ffn_sum = summed_rows(((hidden, down_full),), rows)
+    backward = [backward_part(chunks - 1 - i * (chunks // parts)) for i in range(parts)]
+    token = run_out(
+        token,
+        (ffn_scatter,),
+        [
+            lambda t: mid_sum.far_sum(mid_sum.far(t)),
+            mid_own,
+            middle_back,
+            turn,
+            attend_back,
+        ]
+        + backward[:2],
+    )
+    grad_stream, grad_norm_ffn, grad_attn = kept["grad_stream"], kept["norm_ffn"], kept["grad_attn"]
+    _, grad_gate_proj, heads_gain_grad = kept["gate_back"]
+    gate_scatter = ScatterRing(((full_in, grad_gate_proj), (grad_attn, mixer)), token)
+    token = gate_scatter.sums
+
+    def in_far(token):
+        kept["in_sum"] = summed_rows(
+            ((grad_gate_proj, gate_full), (kept["backward"][0], mixed_full)), rows
+        )
+        return kept["in_sum"].far_sum(kept["in_sum"].far(token))
+
+    def leave(token):
+        kept["branch_ffn"] = ffn_sum.result(ffn_sum.own(ffn_sum.near(token)))
+        kept["outputs"] = (valid * (stream + kept["branch_ffn"])).astype(jnp.bfloat16)
+        return kept["outputs"]
+
+    def in_own(token):
+        return kept["in_sum"].own(kept["in_sum"].near(token))
+
+    def last_back(token):
+        through, kept["norm_attn"] = norm_back(
+            stream_in, inverse_in, gain_attn, kept["in_sum"].result(token)
+        )
+        kept["grad_inputs"] = grad_stream + through
+        return kept["grad_inputs"]
+
+    token = run_out(
+        token,
+        (gate_scatter,),
+        backward[2:] + [in_far, in_own, leave, last_back],
+    )
+    grad_projected, grad_taps, grad_par, _, _ = kept["backward"]
+    mixed_scatter = ScatterRing(((full_in, grad_projected),), token)
+    branch_ffn, outputs = kept["branch_ffn"], kept["outputs"]
     stat_sums = jnp.stack(
         [
             jnp.sum(valid * stream_in * stream_in),
@@ -731,43 +1052,41 @@
             jnp.sum(valid),
         ]
     )
-
-    owned_down, down_hops = scatter_columns_of(hidden, grad_ffn)
-    grad_hidden = times_transposed(grad_ffn, down_full)
-    grad_gate_in = grad_hidden * ffn_up * sigma * (1.0 + ffn_gate * (1.0 - sigma))
-    grad_up_in = grad_hidden * silu_gate
-    grad_ffn_in = jnp.concatenate((grad_gate_in, grad_up_in), axis=1).astype(jnp.bfloat16)
-    grad_mid = back_rows(((grad_ffn_in, ffn_full),), rows)
-    owned_ffn, ffn_hops = scatter_rows_of(full_mid, grad_ffn_in, [down_hops[-3]])
-    owned_gate, owned_up = columns(owned_ffn, [ffn_width] * 2)
-    grad_through, grad_norm_ffn = norm_back(stream, inverse_mid, gain_ffn, grad_mid)
-    grad_stream = grad_out + grad_through
-    grad_attn = spread_rows(grad_stream.astype(jnp.bfloat16))
-    grad_mixer = times_transposed(grad_attn, output_full)
-    owned_output, output_hops = scatter_columns_of(mixer, grad_attn, [ffn_hops[-2]])
-    grad_heads, grad_gate_proj, heads_gain_grad = gate_bwd(
-        heads_out, gate_proj, gain_heads, grad_mixer
-    )
-    owned_out_gate, gate_hops = scatter_rows_of(full_in, grad_gate_proj, [ffn_hops[-1]])
-    grad_projected, grad_taps, grad_par = mixer_bwd(
-        projected, taps, par, written, inverse, states, grad_heads, heads_here
-    )
-    grad_normed = back_rows(((grad_gate_proj, gate_full), (grad_projected, mixed_full)), rows)
-    owned_mixed, _ = scatter_rows_of(full_in, grad_projected, [output_hops[-1], gate_hops[-2]])
-    owned_query, owned_key, owned_value, owned_decay, owned_beta = columns(owned_mixed, widths)
-    grad_through_in, grad_norm_attn = norm_back(stream_in, inverse_in, gain_attn, grad_normed)
-    grad_inputs = to_absolute(grad_stream + grad_through_in)
-
     local = columns(grad_taps, widths[:3]) + [grad_par[0, :heads_here], grad_par[1, :heads_here]]
     whole = [conv_query, conv_key, conv_value, decay_log, decay_bias]
-    common = [stat_sums, to_absolute(grad_norm_ffn), heads_gain_grad[0]]
-    sums = sum_over(packed(common + local), "dp")
-    sums = unpacked(sums, [a.shape for a in common + local])
-    spread = [
-        place_slice(part, array, tensor_rank, part.ndim - 1)
-        for part, array in zip(sums[3:], whole)
-    ]
-    sums = sum_over(packed(sums[:3] + spread), "tensor")
+    common = [stat_sums, grad_norm_ffn, heads_gain_grad[0]]
+    def common_over_dp(token):
+        kept["common"] = sum_over(after(packed(common + local), token), "dp")
+        return kept["common"]
+
+    def common_over_tensor(token):
+        sums = unpacked(kept["common"], [a.shape for a in common + local])
+        spread = [
+            place_slice(part, array, tensor_rank, part.ndim - 1)
+            for part, array in zip(sums[3:], whole)
+        ]
+        kept["common"] = sum_over(after(packed(sums[:3] + spread), token), "tensor")
+        return kept["common"]
+
+    def last_over_dp(token):
+        kept["last"] = sum_over(after(packed([kept["norm_attn"]]), token), "dp")
+        return kept["last"]
+
+    def last_over_tensor(token):
+        kept["last"] = sum_over(after(kept["last"], token), "tensor")
+        return kept["last"]
+
+    token = run_out(
+        mixed_scatter.sums,
+        (mixed_scatter,),
+        [last_over_dp, last_over_tensor, common_over_dp, common_over_tensor],
+    )
+    grad_inputs = kept["grad_inputs"]
+    owned_gate, owned_up, owned_down = ffn_scatter.results()
+    owned_out_gate, owned_output = gate_scatter.results()
+    owned_query, owned_key, owned_value, owned_decay, owned_beta = columns(
+        mixed_scatter.results()[0], widths
+    )
     (
         stat_sums,
         total_ffn_gain,
@@ -777,9 +1096,8 @@
         total_conv_value,
         total_decay_log,
         total_decay_bias,
-    ) = unpacked(sums, [a.shape for a in common + whole])
-    last = packed([to_absolute(grad_norm_attn)])
-    [total_attn_gain] = unpacked(sum_over(sum_over(last, "dp"), "tensor"), [norm_attn.shape])
+    ) = unpacked(kept["common"], [a.shape for a in common + whole])
+    [total_attn_gain] = unpacked(kept["last"], [norm_attn.shape])
     statistics = jnp.sqrt(stat_sums[:3] / (stat_sums[3] * width))
     return (
         outputs,
@@ -794,7 +1112,7 @@
         owned_out_gate,
         owned_decay,
         owned_beta,
-        owned_output,
+        owned_output.T,
         total_conv_query,
         total_conv_key,
         total_conv_value,
@@ -802,7 +1120,7 @@
         total_decay_bias,
         owned_gate,
         owned_up,
-        owned_down,
+        owned_down.T,
     )
 
 

time: 1080 us -> 977 us (0.905)
  matrix products: 300 us -> 227 us
  local copies, waits for them, and re-layouts: 69.5 us -> 142 us
  starting transfers between devices: 167 us -> 110 us
  waiting for transfers between devices: 369 us -> 343 us
    dot_general x80 -> x96, matrix products: 147 us -> 75.5 us  [contract_rows(): lax.dot_general(left, right, (((0,), (0,)), ((), ())), preferred_element_...]
    ppermute x164 -> x108, starting transfers between devices: 156 us -> 99 us  [the longest x21 26.6 us: send(): lax.ppermute(second, 'dp', back)]
    dynamic_update_slice x12 -> x70, local copies, waits for them, and re-layouts: 7.79 us -> 50.8 us  [the longest x54 46.5 us: finish(): lax.dynamic_update_slice(full, part, (at, 0))]
    ppermute x164 -> x108, waiting for transfers between devices: 356 us -> 323 us  [the longest x21 155 us: send(): self.first.append(lax.ppermute(first, 'dp', ahead))]
    unnamed x17 -> x5, other arithmetic: 17.1 us -> 0.01 us
    dynamic_slice x1 -> x9, local copies, waits for them, and re-layouts: 0.67 us -> 15.6 us  [the longest x3 11.9 us: terms_of(): left = lax.dynamic_slice_in_dim(features, at, half, 1)]
    dot_general x11 -> x6, matrix products: 72.9 us -> 59 us  [the longest x1 14.7 us: shards(): jnp.dot(grad_ffn, down_full, preferred_element_type=jnp.float32)]
    dot_general x14 -> x24, matrix products: 80.6 us -> 92.7 us  [times_transposed(): lax.dot_general(left, right, (((1,), (1,)), ((), ())), preferred_element_...]
  transfers between devices with their start and end apart: 174 -> 118, of which waited for: 74 -> 73; matrix products, arithmetic and copies ran while one was open for 33% -> 28% of each run, Pallas kernels for 11% -> 10%
where the time goes in v3:
time: 977 us; the launch traced here: 968 us
  waiting for transfers between devices  343 us (35%)
  matrix products  227 us (23%)
  local copies, waits for them, and re-layouts  142 us (15%)
  starting transfers between devices  110 us (11%)
  Pallas kernels  105 us (11%)
  other arithmetic  34.3 us (4%)
    ppermute x21, waiting for transfers between devices, send(): self.first.append(lax.ppermute(first, 'dp', ahead))  155 us
    ppermute x21, waiting for transfers between devices, send(): lax.ppermute(first, 'dp', ahead)  102 us
    dot_general x24, matrix products, times_transposed(): lax.dot_general(left, right, (((1,), (1,)), ((), ())), preferred_element_...  92.7 us
    dot_general x96, matrix products, contract_rows(): lax.dot_general(left, right, (((0,), (0,)), ((), ())), preferred_element_...  75.5 us
    pallas_call x4, Pallas kernels, mixer_bwd(): pl.pallas_call(functools.partial(bwd_kernel, H, DV, end, before is None),...  58.7 us
    dynamic_update_slice x54, local copies, waits for them, and re-layouts, finish(): lax.dynamic_update_slice(full, part, (at, 0))  46.5 us
    ppermute x4, waiting for transfers between devices, __init__(): self.far = lax.ppermute(block, 'tensor', PAIRS)  37.1 us
    pallas_call x4, Pallas kernels, mixer_fwd(): pl.pallas_call(functools.partial(fwd_kernel, H, DV, NC, start), grid=(cou...  33.7 us
  transfers between devices with their start and end apart: 118, of which 73 were waited for; matrix products, arithmetic and copies ran while one was open for 28% of the time, Pallas kernels for 10%

profile of v3, /device:TPU:0, one launch (start us, length us, event | category | flops | bytes accessed | tf_op | source)
XLA Modules:
  0.0 968.1 jit_solution(16720062358763245002)
XLA Ops:
  15.6 10.3 %collective-permute-done = bf16[128,2176]{1,0:T(8,128)(2,1)S(1)} collective-permute-done((bf16[128,2176]{1,0:T(8,128)(2,1)}, bf16[128,2176]{1,0:T(8,128)(2,1)S(1)}, u32[]{:S(2)}, u32[]{:S(2)}) %collective-permute-start) | collective-permute-done | bytes 557088 | tf_op jit(solution)/shard_map/ppermute | solution.py:500
  75.4 8.5 collective-permute-done.7
  89.0 9.2 collective-permute-done.9
  141.4 13.1 %fusion.38.p_ref.halo_ref = f32[1024,2176]{1,0:T(8,128)S(1)} fusion(bf16[1024,2048]{1,0:T(8,128)(2,1)S(1)} %constant_dynamic-update-slice_fusion.37, bf16[2048,2176]{1,0:T(8,128)(2,1)} %constant_dynamic-update-slice_fusion.21), kind=kOutput, calls=%fused_computation.423 | convolution fusion | flops 9126805504 | bytes 22020096 | tf_op jit(solution)/shard_map/dot_general | solution.py:878
  159.0 8.2 mixer_fwd.4
  171.5 8.3 mixer_fwd.5
  185.0 8.2 mixer_fwd.6
  198.0 9.1 mixer_fwd.7
  216.3 8.4 collective-permute-done.27
  230.3 10.1 %collective-permute-done.29 = bf16[128,2048]{0,1:T(8,128)(2,1)S(1)} collective-permute-done((bf16[128,2048]{0,1:T(8,128)(2,1)S(1)}, bf16[128,2048]{0,1:T(8,128)(2,1)S(1)}, u32[]{:S(2)}, u32[]{:S(2)}) %collective-permute-start.29) | collective-permute-done | bytes 524320 | tf_op jit(solution)/shard_map/ppermute | solution.py:500
  273.9 18.7 %collective-permute-done.34 = bf16[128,4224]{0,1:T(8,128)(2,1)S(1)} collective-permute-done((bf16[128,4224]{0,1:T(8,128)(2,1)S(1)}, bf16[128,4224]{0,1:T(8,128)(2,1)S(1)}, u32[]{:S(2)}, u32[]{:S(2)}) %collective-permute-start.34) | collective-permute-done | bytes 1081376 | tf_op jit(solution)/shard_map/ppermute | solution.py:500
  304.5 15.1 %collective-permute-done.36 = bf16[128,4224]{0,1:T(8,128)(2,1)S(1)} collective-permute-done((bf16[128,4224]{0,1:T(8,128)(2,1)S(1)}, bf16[128,4224]{0,1:T(8,128)(2,1)S(1)}, u32[]{:S(2)}, u32[]{:S(2)}) %collective-permute-start.36) | collective-permute-done | bytes 1081376 | tf_op jit(solution)/shard_map/ppermute | solution.py:500
  326.8 18.1 %collective-permute-done.49 = bf16[256,2048]{1,0:T(8,128)(2,1)S(1)} collective-permute-done((bf16[256,2048]{1,0:T(8,128)(2,1)S(1)}, bf16[256,2048]{1,0:T(8,128)(2,1)S(1)}, u32[]{:S(2)}, u32[]{:S(2)}) %collective-permute-start.49) | collective-permute-done | bytes 1048608 | tf_op jit(solution)/shard_map/ppermute | solution.py:659
  357.3 15.5 %collective-permute-done.42 = bf16[128,4224]{0,1:T(8,128)(2,1)S(1)} collective-permute-done((bf16[128,4224]{0,1:T(8,128)(2,1)S(1)}, bf16[128,4224]{0,1:T(8,128)(2,1)S(1)}, u32[]{:S(2)}, u32[]{:S(2)}) %collective-permute-start.42) | collective-permute-done | bytes 1081376 | tf_op jit(solution)/shard_map/ppermute | solution.py:500
  379.1 17.9 %collective-permute-done.44 = bf16[128,4224]{0,1:T(8,128)(2,1)S(1)} collective-permute-done((bf16[128,4224]{0,1:T(8,128)(2,1)S(1)}, bf16[128,4224]{0,1:T(8,128)(2,1)S(1)}, u32[]{:S(2)}, u32[]{:S(2)}) %collective-permute-start.44) | collective-permute-done | bytes 1081376 | tf_op jit(solution)/shard_map/ppermute | solution.py:500
  406.9 13.2 %collective-permute-done.46 = bf16[128,4224]{0,1:T(8,128)(2,1)S(1)} collective-permute-done((bf16[128,4224]{0,1:T(8,128)(2,1)S(1)}, bf16[128,4224]{0,1:T(8,128)(2,1)S(1)}, u32[]{:S(2)}, u32[]{:S(2)}) %collective-permute-start.46) | collective-permute-done | bytes 1081376 | tf_op jit(solution)/shard_map/ppermute | solution.py:500
  422.4 8.5 fusion.42
  430.9 8.5 fusion.43
  439.4 14.7 %multiply_convert_fusion = (bf16[1024,1408]{1,0:T(8,128)(2,1)S(1)}, bf16[1024,1408]{1,0:T(8,128)(2,1)S(1)}, bf16[1024,1408]{1,0:T(8,128)(2,1)S(1)}) fusion(f32[1024,1408]{1,0:T(8,128)} %fusion.42, f32[1024,1408]{1,0:T(8,128)} %fusion.43, bf16[1024,2048]{1,0:T(8,128)(2,1)} %copy-done.37, bf16[2048,1408]{0,1:T(8,128)(2,1)} %get-tuple-element.1176), kind=kOutput, calls=%fused_computation | convolution fusion | flops 5927206912 | bytes 30146560 | tf_op jit(solution)/shard_map/dot_general | solution.py:946
  475.0 18.8 %collective-permute-done.54.refs_0_ = bf16[128,4224]{1,0:T(8,128)(2,1)S(1)} collective-permute-done((bf16[128,4224]{1,0:T(8,128)(2,1)S(1)}, bf16[128,4224]{1,0:T(8,128)(2,1)S(1)}, u32[]{:S(2)}, u32[]{:S(2)}) %collective-permute-start.54) | collective-permute-done | bytes 1081376 | tf_op jit(solution)/shard_map/ppermute | solution.py:578
  508.4 11.7 %collective-permute-done.57.refs_0_ = bf16[128,4224]{1,0:T(8,128)(2,1)S(1)} collective-permute-done((bf16[128,4224]{1,0:T(8,128)(2,1)S(1)}, bf16[128,4224]{1,0:T(8,128)(2,1)S(1)}, u32[]{:S(2)}, u32[]{:S(2)}) %collective-permute-start.57) | collective-permute-done | bytes 1081376 | tf_op jit(solution)/shard_map/ppermute | solution.py:578
  532.6 13.7 %collective-permute-done.63.refs_0_ = bf16[128,4224]{1,0:T(8,128)(2,1)S(1)} collective-permute-done((bf16[128,4224]{1,0:T(8,128)(2,1)S(1)}, bf16[128,4224]{1,0:T(8,128)(2,1)S(1)}, u32[]{:S(2)}, u32[]{:S(2)}) %collective-permute-start.63) | collective-permute-done | bytes 1081376 | tf_op jit(solution)/shard_map/ppermute | solution.py:578
  564.6 19.1 %collective-permute-done.62 = bf16[256,2048]{1,0:T(8,128)(2,1)S(1)} collective-permute-done((bf16[256,2048]{1,0:T(8,128)(2,1)S(1)}, bf16[256,2048]{1,0:T(8,128)(2,1)S(1)}, u32[]{:S(2)}, u32[]{:S(2)}) %collective-permute-start.62) | collective-permute-done | bytes 1048608 | tf_op jit(solution)/shard_map/ppermute | solution.py:659
  591.7 7.9 fusion.48.in_ref
  628.9 14.5 %mixer_bwd.4 = (bf16[1024,2176]{1,0:T(8,128)(2,1)S(1)}, f32[4,2048]{1,0:T(4,128)S(1)}, f32[8,128]{1,0:T(8,128)S(1)}, f32[512,256]{1,0:T(8,128)S(1)}, f32[8,2048]{1,0:T(8,128)S(1)}) custom-call(f32[1024,2176]{1,0:T(8,128)S(1)} %bitcast.304, f32[1024,2176]{1,0:T(8,128)S(1)} %bitcast.304, f32[4,2048]{1,0:T(4,128)S(1)} %copy-done.16, f32[8,128]{1,0:T(8,128)S(1)} %copy-done.18, ...), custom_call_target="tpu_custom_call" | custom-call | flops 12000000000 | bytes 8388608 | tf_op jit(solution)/shard_map/mixer_bwd/pallas_call | solution.py:375
  652.0 14.5 %mixer_bwd.5 = (bf16[1024,2176]{1,0:T(8,128)(2,1)S(1)}, f32[4,2048]{1,0:T(4,128)S(1)}, f32[8,128]{1,0:T(8,128)S(1)}, f32[512,256]{1,0:T(8,128)S(1)}, f32[8,2048]{1,0:T(8,128)S(1)}) custom-call(f32[1024,2176]{1,0:T(8,128)S(1)} %bitcast.304, f32[1024,2176]{1,0:T(8,128)S(1)} %bitcast.304, f32[4,2048]{1,0:T(4,128)S(1)} %copy-done.16, ...), custom_call_target="tpu_custom_call", output_to_operand_aliasing={{0}: (8, {})} | custom-call | flops 12000000000 | bytes 8388608 | tf_op jit(solution)/shard_map/mixer_bwd/pallas_call | solution.py:375
  680.0 14.5 %mixer_bwd.6 = (bf16[1024,2176]{1,0:T(8,128)(2,1)S(1)}, f32[4,2048]{1,0:T(4,128)S(1)}, f32[8,128]{1,0:T(8,128)S(1)}, f32[512,256]{1,0:T(8,128)S(1)}, f32[8,2048]{1,0:T(8,128)S(1)}) custom-call(f32[1024,2176]{1,0:T(8,128)S(1)} %bitcast.306, f32[1024,2176]{1,0:T(8,128)S(1)} %bitcast.306, f32[4,2048]{1,0:T(4,128)S(1)} %copy-done.16, ...), custom_call_target="tpu_custom_call", output_to_operand_aliasing={{0}: (8, {})} | custom-call | flops 12000000000 | bytes 8388608 | tf_op jit(solution)/shard_map/mixer_bwd/pallas_call | solution.py:375
  698.9 15.2 %mixer_bwd.7 = (bf16[1024,2176]{1,0:T(8,128)(2,1)S(1)}, f32[4,2048]{1,0:T(4,128)S(1)}, f32[8,128]{1,0:T(8,128)S(1)}, f32[512,256]{1,0:T(8,128)}, f32[8,2048]{1,0:T(8,128)}) custom-call(f32[1024,2176]{1,0:T(8,128)S(1)} %bitcast.306, f32[1024,2176]{1,0:T(8,128)S(1)} %bitcast.306, f32[4,2048]{1,0:T(4,128)S(1)} %copy-done.16, ...), custom_call_target="tpu_custom_call", output_to_operand_aliasing={{0}: (8, {})} | custom-call | flops 12000000000 | bytes 8388608 | tf_op jit(solution)/shard_map/mixer_bwd/pallas_call | solution.py:375
  722.0 9.9 %fusion.4 = bf16[256,2048]{1,0:T(8,128)(2,1)S(1)} fusion(f32[256,2048]{1,0:T(8,128)} %fusion.55, bf16[256,2176]{1,0:T(8,128)(2,1)S(1)} %get-tuple-element.1117, bf16[2048,2176]{1,0:T(8,128)(2,1)} %constant_dynamic-update-slice_fusion.21), kind=kOutput, calls=%fused_computation.47 | convolution fusion | flops 2282749952 | bytes 13172736 | tf_op jit(solution)/shard_map/dot_general | solution.py:645
  788.8 10.2 %collective-permute-done.86.refs_0_ = bf16[128,2048]{1,0:T(8,128)(2,1)S(1)} collective-permute-done((bf16[128,2048]{1,0:T(8,128)(2,1)S(1)}, bf16[128,2048]{1,0:T(8,128)(2,1)S(1)}, u32[]{:S(2)}, u32[]{:S(2)}) %collective-permute-start.86) | collective-permute-done | bytes 524320 | tf_op jit(solution)/shard_map/ppermute | solution.py:578
  819.7 7.9 collective-permute-done.92
  942.7 8.8 collective-permute-done.114.refs_0_
  (928 shorter events, 571.9 us)
Async XLA Ops:
  28.2 75.1 %collective-permute-start.2 = (bf16[256,2048]{1,0:T(8,128)(2,1)S(1)}, bf16[256,2048]{1,0:T(8,128)(2,1)}, u32[]{:S(2)}, u32[]{:S(2)}) collective-permute-start(bf16[256,2048]{1,0:T(8,128)(2,1)S(1)} %fusion.9), channel_id=1, source_target_pairs={{0,1},{1,0},{2,3},{3,2},{4,5},{5,4},{6,7},{7,6},{8,9},{9,8},{10,11... | collective-permute-start | bytes 3145736 | tf_op jit(solution)/shard_map/ppermute | solution.py:660
  28.3 47.1 %collective-permute-start.3 = (bf16[256,2048]{1,0:T(8,128)(2,1)S(1)}, bf16[256,2048]{1,0:T(8,128)(2,1)}, u32[]{:S(2)}, u32[]{:S(2)}) collective-permute-start(bf16[256,2048]{1,0:T(8,128)(2,1)S(1)} %fusion.9), channel_id=1, source_target_pairs={{0,2},{2,0},{1,3},{3,1},{4,6},{6,4},{5,7},{7,5},{8,10},{10,8},{9,1... | collective-permute-start | bytes 3145736 | tf_op jit(solution)/shard_map/ppermute | solution.py:659
  38.1 31.5 %collective-permute-start.5 = (bf16[128,2176]{1,0:T(8,128)(2,1)}, bf16[128,2176]{1,0:T(8,128)(2,1)}, u32[]{:S(2)}, u32[]{:S(2)}) collective-permute-start(bf16[128,2176]{1,0:T(8,128)(2,1)} %copy-done.150), channel_id=1, source_target_pairs={{0,8},{8,16},{16,24},{24,28},{28,20},{20,12},{12,4},{4,0},{1,9},{9... | collective-permute-start | bytes 1671176 | tf_op jit(solution)/shard_map/ppermute | solution.py:500
  39.6 29.9 %collective-permute-start.6 = (bf16[128,2176]{1,0:T(8,128)(2,1)}, bf16[128,2176]{1,0:T(8,128)(2,1)}, u32[]{:S(2)}, u32[]{:S(2)}) collective-permute-start(bf16[128,2176]{1,0:T(8,128)(2,1)} %collective-permute-done.1), channel_id=1, source_target_pairs={{8,0},{16,8},{24,16},{28,24},{20,28},{12,20},{4,12},{0,4},{9,1},{1... | collective-permute-start | bytes 1671176 | tf_op jit(solution)/shard_map/ppermute | solution.py:501
  75.4 27.9 %collective-permute-start.4 = (bf16[256,2048]{1,0:T(8,128)(2,1)}, bf16[256,2048]{1,0:T(8,128)(2,1)S(1)}, u32[]{:S(2)}, u32[]{:S(2)}) collective-permute-start(bf16[256,2048]{1,0:T(8,128)(2,1)} %collective-permute-done.3), channel_id=1, source_target_pairs={{0,1},{1,0},{2,3},{3,2},{4,5},{5,4},{6,7},{7,6},{8,9},{9,8},{10,11... | collective-permute-start | bytes 3145736 | tf_op jit(solution)/shard_map/ppermute | solution.py:666
  266.4 26.3 %collective-permute-start.34 = (bf16[128,4224]{0,1:T(8,128)(2,1)S(1)}, bf16[128,4224]{0,1:T(8,128)(2,1)S(1)}, u32[]{:S(2)}, u32[]{:S(2)}) collective-permute-start(bf16[128,4224]{0,1:T(8,128)(2,1)S(1)} %collective-permute-done.31), channel_id=1, source_target_pairs={{0,8},{8,16},{16,24},{24,28},{28,20},{20,12},{12,4},{4,0},{1,9},{9... | collective-permute-start | bytes 3244040 | tf_op jit(solution)/shard_map/ppermute | solution.py:500
  268.3 26.2 %collective-permute-start.35 = (bf16[128,4224]{0,1:T(8,128)(2,1)S(1)}, bf16[128,4224]{0,1:T(8,128)(2,1)S(1)}, u32[]{:S(2)}, u32[]{:S(2)}) collective-permute-start(bf16[128,4224]{0,1:T(8,128)(2,1)S(1)} %collective-permute-done.32), channel_id=1, source_target_pairs={{8,0},{16,8},{24,16},{28,24},{20,28},{12,20},{4,12},{0,4},{9,1},{1... | collective-permute-start | bytes 3244040 | tf_op jit(solution)/shard_map/ppermute | solution.py:501
  273.3 46.7 %collective-permute-start.39 = (bf16[256,2048]{1,0:T(8,128)(2,1)S(1)}, bf16[256,2048]{1,0:T(8,128)(2,1)S(1)}, u32[]{:S(2)}, u32[]{:S(2)}) collective-permute-start(bf16[256,2048]{1,0:T(8,128)(2,1)S(1)} %add_convert_fusion.2), channel_id=1, source_target_pairs={{0,2},{2,0},{1,3},{3,1},{4,6},{6,4},{5,7},{7,5},{8,10},{10,8},{9,1... | collective-permute-start | bytes 3145736 | tf_op jit(solution)/shard_map/ppermute | solution.py:711
  294.5 25.2 %collective-permute-start.36 = (bf16[128,4224]{0,1:T(8,128)(2,1)S(1)}, bf16[128,4224]{0,1:T(8,128)(2,1)S(1)}, u32[]{:S(2)}, u32[]{:S(2)}) collective-permute-start(bf16[128,4224]{0,1:T(8,128)(2,1)S(1)} %collective-permute-done.34), channel_id=1, source_target_pairs={{0,8},{8,16},{16,24},{24,28},{28,20},{20,12},{12,4},{4,0},{1,9},{9... | collective-permute-start | bytes 3244040 | tf_op jit(solution)/shard_map/ppermute | solution.py:500
  295.0 24.9 %collective-permute-start.37 = (bf16[128,4224]{0,1:T(8,128)(2,1)S(1)}, bf16[128,4224]{0,1:T(8,128)(2,1)S(1)}, u32[]{:S(2)}, u32[]{:S(2)}) collective-permute-start(bf16[128,4224]{0,1:T(8,128)(2,1)S(1)} %collective-permute-done.35), channel_id=1, source_target_pairs={{8,0},{16,8},{24,16},{28,24},{20,28},{12,20},{4,12},{0,4},{9,1},{1... | collective-permute-start | bytes 3244040 | tf_op jit(solution)/shard_map/ppermute | solution.py:501
  347.9 24.9 %collective-permute-start.42 = (bf16[128,4224]{0,1:T(8,128)(2,1)S(1)}, bf16[128,4224]{0,1:T(8,128)(2,1)S(1)}, u32[]{:S(2)}, u32[]{:S(2)}) collective-permute-start(bf16[128,4224]{0,1:T(8,128)(2,1)S(1)} %collective-permute-done.40), channel_id=1, source_target_pairs={{0,8},{8,16},{16,24},{24,28},{28,20},{20,12},{12,4},{4,0},{1,9},{9... | collective-permute-start | bytes 3244040 | tf_op jit(solution)/shard_map/ppermute | solution.py:500
  348.4 24.7 %collective-permute-start.43 = (bf16[128,4224]{0,1:T(8,128)(2,1)S(1)}, bf16[128,4224]{0,1:T(8,128)(2,1)S(1)}, u32[]{:S(2)}, u32[]{:S(2)}) collective-permute-start(bf16[128,4224]{0,1:T(8,128)(2,1)S(1)} %collective-permute-done.41), channel_id=1, source_target_pairs={{8,0},{16,8},{24,16},{28,24},{20,28},{12,20},{4,12},{0,4},{9,1},{1... | collective-permute-start | bytes 3244040 | tf_op jit(solution)/shard_map/ppermute | solution.py:501
  354.2 24.0 %collective-permute-start.52 = (bf16[256,2048]{1,0:T(8,128)(2,1)S(1)}, bf16[256,2048]{1,0:T(8,128)(2,1)S(1)}, u32[]{:S(2)}, u32[]{:S(2)}) collective-permute-start(bf16[256,2048]{1,0:T(8,128)(2,1)S(1)} %fusion.22), channel_id=1, source_target_pairs={{0,2},{2,0},{1,3},{3,1},{4,6},{6,4},{5,7},{7,5},{8,10},{10,8},{9,1... | collective-permute-start | bytes 3145736 | tf_op jit(solution)/shard_map/ppermute | solution.py:659
  357.3 44.1 %collective-permute-start.51 = (bf16[256,2048]{1,0:T(8,128)(2,1)S(1)}, bf16[256,2048]{1,0:T(8,128)(2,1)S(1)}, u32[]{:S(2)}, u32[]{:S(2)}) collective-permute-start(bf16[256,2048]{1,0:T(8,128)(2,1)S(1)} %fusion.22), channel_id=1, source_target_pairs={{0,1},{1,0},{2,3},{3,2},{4,5},{5,4},{6,7},{7,6},{8,9},{9,8},{10,11... | collective-permute-start | bytes 3145736 | tf_op jit(solution)/shard_map/ppermute | solution.py:660
  467.6 26.3 %collective-permute-start.54 = (bf16[128,4224]{1,0:T(8,128)(2,1)S(1)}, bf16[128,4224]{1,0:T(8,128)(2,1)S(1)}, u32[]{:S(2)}, u32[]{:S(2)}) collective-permute-start(bf16[128,4224]{1,0:T(8,128)(2,1)S(1)} %pad_maximum_fusion.3), channel_id=1, source_target_pairs={{0,8},{8,16},{16,24},{24,28},{28,20},{20,12},{12,4},{4,0},{1,9},{9... | collective-permute-start | bytes 3244040 | tf_op jit(solution)/shard_map/ppermute | solution.py:578
  468.2 26.1 %collective-permute-start.55 = (bf16[128,4224]{1,0:T(8,128)(2,1)S(1)}, bf16[128,4224]{1,0:T(8,128)(2,1)S(1)}, u32[]{:S(2)}, u32[]{:S(2)}) collective-permute-start(bf16[128,4224]{1,0:T(8,128)(2,1)S(1)} %pad_maximum_fusion.4), channel_id=1, source_target_pairs={{8,0},{16,8},{24,16},{28,24},{20,28},{12,20},{4,12},{0,4},{9,1},{1... | collective-permute-start | bytes 3244040 | tf_op jit(solution)/shard_map/ppermute | solution.py:578
  474.9 53.4 %collective-permute-start.60 = (bf16[256,2048]{1,0:T(8,128)(2,1)S(1)}, bf16[256,2048]{1,0:T(8,128)(2,1)S(1)}, u32[]{:S(2)}, u32[]{:S(2)}) collective-permute-start(bf16[256,2048]{1,0:T(8,128)(2,1)S(1)} %add_convert_fusion.1), channel_id=1, source_target_pairs={{0,2},{2,0},{1,3},{3,1},{4,6},{6,4},{5,7},{7,5},{8,10},{10,8},{9,1... | collective-permute-start | bytes 3145736 | tf_op jit(solution)/shard_map/ppermute | solution.py:711
  494.9 25.2 %collective-permute-start.57 = (bf16[128,4224]{1,0:T(8,128)(2,1)S(1)}, bf16[128,4224]{1,0:T(8,128)(2,1)S(1)}, u32[]{:S(2)}, u32[]{:S(2)}) collective-permute-start(bf16[128,4224]{1,0:T(8,128)(2,1)S(1)} %get-tuple-element.852), channel_id=1, source_target_pairs={{0,8},{8,16},{16,24},{24,28},{28,20},{20,12},{12,4},{4,0},{1,9},{9... | collective-permute-start | bytes 3244040 | tf_op jit(solution)/shard_map/ppermute | solution.py:578
  496.4 25.1 %collective-permute-start.58 = (bf16[128,4224]{1,0:T(8,128)(2,1)S(1)}, bf16[128,4224]{1,0:T(8,128)(2,1)S(1)}, u32[]{:S(2)}, u32[]{:S(2)}) collective-permute-start(bf16[128,4224]{1,0:T(8,128)(2,1)S(1)} %get-tuple-element.853), channel_id=1, source_target_pairs={{8,0},{16,8},{24,16},{28,24},{20,28},{12,20},{4,12},{0,4},{9,1},{1... | collective-permute-start | bytes 3244040 | tf_op jit(solution)/shard_map/ppermute | solution.py:578
  522.1 24.3 %collective-permute-start.63 = (bf16[128,4224]{1,0:T(8,128)(2,1)S(1)}, bf16[128,4224]{1,0:T(8,128)(2,1)S(1)}, u32[]{:S(2)}, u32[]{:S(2)}) collective-permute-start(bf16[128,4224]{1,0:T(8,128)(2,1)S(1)} %get-tuple-element.883), channel_id=1, source_target_pairs={{0,8},{8,16},{16,24},{24,28},{28,20},{20,12},{12,4},{4,0},{1,9},{9... | collective-permute-start | bytes 3244040 | tf_op jit(solution)/shard_map/ppermute | solution.py:578
  556.4 27.2 %collective-permute-start.67 = (bf16[128,4224]{1,0:T(8,128)(2,1)S(1)}, bf16[128,4224]{1,0:T(8,128)(2,1)S(1)}, u32[]{:S(2)}, u32[]{:S(2)}) collective-permute-start(bf16[128,4224]{1,0:T(8,128)(2,1)S(1)} %get-tuple-element.918), channel_id=1, source_target_pairs={{0,8},{8,16},{16,24},{24,28},{28,20},{20,12},{12,4},{4,0},{1,9},{9... | collective-permute-start | bytes 3244040 | tf_op jit(solution)/shard_map/ppermute | solution.py:578
  558.2 26.1 %collective-permute-start.68 = (bf16[128,4224]{1,0:T(8,128)(2,1)S(1)}, bf16[128,4224]{1,0:T(8,128)(2,1)S(1)}, u32[]{:S(2)}, u32[]{:S(2)}) collective-permute-start(bf16[128,4224]{1,0:T(8,128)(2,1)S(1)} %get-tuple-element.919), channel_id=1, source_target_pairs={{8,0},{16,8},{24,16},{28,24},{20,28},{12,20},{4,12},{0,4},{9,1},{1... | collective-permute-start | bytes 3244040 | tf_op jit(solution)/shard_map/ppermute | solution.py:578
  558.7 25.0 %collective-permute-start.62 = (bf16[256,2048]{1,0:T(8,128)(2,1)S(1)}, bf16[256,2048]{1,0:T(8,128)(2,1)S(1)}, u32[]{:S(2)}, u32[]{:S(2)}) collective-permute-start(bf16[256,2048]{1,0:T(8,128)(2,1)S(1)} %get-tuple-element.948), channel_id=1, source_target_pairs={{0,2},{2,0},{1,3},{3,1},{4,6},{6,4},{5,7},{7,5},{8,10},{10,8},{9,1... | collective-permute-start | bytes 3145736 | tf_op jit(solution)/shard_map/ppermute | solution.py:659
  558.7 32.0 %collective-permute-start.61 = (bf16[256,2048]{1,0:T(8,128)(2,1)S(1)}, bf16[256,2048]{1,0:T(8,128)(2,1)S(1)}, u32[]{:S(2)}, u32[]{:S(2)}) collective-permute-start(bf16[256,2048]{1,0:T(8,128)(2,1)S(1)} %get-tuple-element.948), channel_id=1, source_target_pairs={{0,1},{1,0},{2,3},{3,2},{4,5},{5,4},{6,7},{7,6},{8,9},{9,8},{10,11... | collective-permute-start | bytes 3145736 | tf_op jit(solution)/shard_map/ppermute | solution.py:660
  588.6 25.7 %collective-permute-start.69 = (bf16[128,4224]{1,0:T(8,128)(2,1)S(1)}, bf16[128,4224]{1,0:T(8,128)(2,1)S(1)}, u32[]{:S(2)}, u32[]{:S(2)}) collective-permute-start(bf16[128,4224]{1,0:T(8,128)(2,1)S(1)} %get-tuple-element.955), channel_id=1, source_target_pairs={{0,8},{8,16},{16,24},{24,28},{28,20},{20,12},{12,4},{4,0},{1,9},{9... | collective-permute-start | bytes 3244040 | tf_op jit(solution)/shard_map/ppermute | solution.py:578
  589.7 26.0 %collective-permute-start.70 = (bf16[128,4224]{1,0:T(8,128)(2,1)S(1)}, bf16[128,4224]{1,0:T(8,128)(2,1)S(1)}, u32[]{:S(2)}, u32[]{:S(2)}) collective-permute-start(bf16[128,4224]{1,0:T(8,128)(2,1)S(1)} %get-tuple-element.956), channel_id=1, source_target_pairs={{8,0},{16,8},{24,16},{28,24},{20,28},{12,20},{4,12},{0,4},{9,1},{1... | collective-permute-start | bytes 3244040 | tf_op jit(solution)/shard_map/ppermute | solution.py:578
  616.2 27.2 %collective-permute-start.71 = (bf16[128,4224]{1,0:T(8,128)(2,1)S(1)}, bf16[128,4224]{1,0:T(8,128)(2,1)S(1)}, u32[]{:S(2)}, u32[]{:S(2)}) collective-permute-start(bf16[128,4224]{1,0:T(8,128)(2,1)S(1)} %get-tuple-element.968), channel_id=1, source_target_pairs={{0,8},{8,16},{16,24},{24,28},{28,20},{20,12},{12,4},{4,0},{1,9},{9... | collective-permute-start | bytes 3244040 | tf_op jit(solution)/shard_map/ppermute | solution.py:578
  616.8 26.5 %collective-permute-start.72 = (bf16[128,4224]{1,0:T(8,128)(2,1)S(1)}, bf16[128,4224]{1,0:T(8,128)(2,1)S(1)}, u32[]{:S(2)}, u32[]{:S(2)}) collective-permute-start(bf16[128,4224]{1,0:T(8,128)(2,1)S(1)} %get-tuple-element.969), channel_id=1, source_target_pairs={{8,0},{16,8},{24,16},{28,24},{20,28},{12,20},{4,12},{0,4},{9,1},{1... | collective-permute-start | bytes 3244040 | tf_op jit(solution)/shard_map/ppermute | solution.py:578
  644.0 24.6 %collective-permute-start.73 = (bf16[128,4224]{1,0:T(8,128)(2,1)S(1)}, bf16[128,4224]{1,0:T(8,128)(2,1)S(1)}, u32[]{:S(2)}, u32[]{:S(2)}) collective-permute-start(bf16[128,4224]{1,0:T(8,128)(2,1)S(1)} %get-tuple-element.1003), channel_id=1, source_target_pairs={{0,8},{8,16},{16,24},{24,28},{28,20},{20,12},{12,4},{4,0},{1,9},{9... | collective-permute-start | bytes 3244040 | tf_op jit(solution)/shard_map/ppermute | solution.py:578
  644.6 24.8 %collective-permute-start.74 = (bf16[128,4224]{1,0:T(8,128)(2,1)S(1)}, bf16[128,4224]{1,0:T(8,128)(2,1)}, u32[]{:S(2)}, u32[]{:S(2)}) collective-permute-start(bf16[128,4224]{1,0:T(8,128)(2,1)S(1)} %get-tuple-element.1004), channel_id=1, source_target_pairs={{8,0},{16,8},{24,16},{28,24},{20,28},{12,20},{4,12},{0,4},{9,1},{1... | collective-permute-start | bytes 3244040 | tf_op jit(solution)/shard_map/ppermute | solution.py:578
  732.0 53.5 %collective-permute-start.85 = (bf16[256,2048]{1,0:T(8,128)(2,1)}, bf16[256,2048]{1,0:T(8,128)(2,1)S(1)}, u32[]{:S(2)}, u32[]{:S(2)}) collective-permute-start(bf16[256,2048]{1,0:T(8,128)(2,1)} %add_convert_fusion), channel_id=1, source_target_pairs={{0,2},{2,0},{1,3},{3,1},{4,6},{6,4},{5,7},{7,5},{8,10},{10,8},{9,1... | collective-permute-start | bytes 3145736 | tf_op jit(solution)/shard_map/ppermute | solution.py:711
  778.2 25.7 %collective-permute-start.91 = (bf16[256,2048]{1,0:T(8,128)(2,1)S(1)}, bf16[256,2048]{1,0:T(8,128)(2,1)S(1)}, u32[]{:S(2)}, u32[]{:S(2)}) collective-permute-start(bf16[256,2048]{1,0:T(8,128)(2,1)S(1)} %copy-done.167), channel_id=1, source_target_pairs={{0,2},{2,0},{1,3},{3,1},{4,6},{6,4},{5,7},{7,5},{8,10},{10,8},{9,1... | collective-permute-start | bytes 3145736 | tf_op jit(solution)/shard_map/ppermute | solution.py:711
  (269 other events, 3579.8 us)

commit v4 on v3

--- a/solution.py
+++ b/solution.py
@@ -422,7 +422,7 @@
         out_specs=row_block(rows, width),
         out_shape=jax.ShapeDtypeStruct((L, width), BF),
         compiler_params=room(12),
-        cost_estimate=pl.CostEstimate(flops=5 * 10**9, bytes_accessed=10 * 2**20, transcendentals=0),
+        cost_estimate=pl.CostEstimate(flops=10**6, bytes_accessed=10**5, transcendentals=0),
         name="gate_fwd",
     )(heads_out, gate_proj, gain)
 
@@ -460,7 +460,7 @@
         out_specs=[row_block(rows, width), row_block(rows, width), whole_block(gain)],
         out_shape=[f((L, width), F32), f((L, width), BF), f(gain.shape, F32)],
         compiler_params=room(14),
-        cost_estimate=pl.CostEstimate(flops=7 * 10**9, bytes_accessed=18 * 2**20, transcendentals=0),
+        cost_estimate=pl.CostEstimate(flops=10**6, bytes_accessed=10**5, transcendentals=0),
         name="gate_bwd",
     )(heads_out, gate_proj, gain, grad_mixer)
 
@@ -521,13 +521,11 @@
         return fulls
 
 
-def land_kernel(widths, *refs):
+def land_kernel(widths, at_ref, first, second, *refs):
     count = len(widths)
-    first, second = refs[0], refs[1]
-    terms = refs[2 : 2 + 2 * count]
     for arrived, mine, out in (
-        (first, terms[:count], refs[-2]),
-        (second, terms[count:], refs[-1]),
+        (first, refs[:count], refs[-2]),
+        (second, refs[count : 2 * count], refs[-1]),
     ):
         start = 0
         for width, term in zip(widths, mine):
@@ -536,69 +534,82 @@
             start += width
 
 
-def landed(flying, terms):
-    widths = [term.shape[1] for term in terms[0]]
+def landed(flying, partials, places):
+    widths = [partial.shape[1] for partial in partials]
     rows, wide = flying[0].shape
     steps = 2
-    arrays = list(flying) + list(terms[0]) + list(terms[1])
+    block = rows // steps
+    sent = pl.BlockSpec((block, wide), lambda s, at: (s, 0))
+
+    def term(width, side):
+        return pl.BlockSpec(
+            (block, width), lambda s, at: (at[side] * (2 * steps) + side * steps + s, 0)
+        )
+
+    terms = [term(width, side) for side in (0, 1) for width in widths]
     return pl.pallas_call(
         functools.partial(land_kernel, widths),
-        grid=(steps,),
-        in_specs=[row_block(rows // steps, a.shape[1]) for a in arrays],
-        out_specs=[row_block(rows // steps, wide)] * 2,
+        grid_spec=pltpu.PrefetchScalarGridSpec(
+            num_scalar_prefetch=1, grid=(steps,), in_specs=[sent, sent] + terms, out_specs=[sent, sent]
+        ),
         out_shape=[jax.ShapeDtypeStruct((rows, wide), BF)] * 2,
         compiler_params=room(10),
         cost_estimate=pl.CostEstimate(flops=10**6, bytes_accessed=10**6, transcendentals=0),
         name="land",
-    )(*arrays)
+    )(jnp.stack(places).astype(jnp.int32), *flying, *partials, *partials)
 
 
 class ScatterRing:
-    def __init__(self, pairs, token):
+    def __init__(self, pairs, token, partials=None):
         self.n = lax.axis_size("dp")
         self.hop = 0
-        self.pairs = pairs
+        self.pairs, self.partials = pairs, partials
         self.sums = tuple(
-            jnp.concatenate(terms, axis=1).astype(BF)
-            for terms in (self.terms_of(1, 0, token), self.terms_of(self.n - 1, 1, token))
+            jnp.concatenate(self.terms_of(place, side, token), axis=1).astype(BF)
+            for place, side in ((1, 0), (self.n - 1, 1))
         )
 
     def terms_of(self, place, side, token):
         terms = []
-        for features, grads in self.pairs:
+        for number, (features, grads) in enumerate(self.pairs):
             half = features.shape[1] // self.n // 2
             at = behind(place % self.n) * (2 * half) + side * half
+            if self.partials is not None:
+                terms.append(lax.dynamic_slice_in_dim(self.partials[number], at, half, 0))
+                continue
             left = lax.dynamic_slice_in_dim(features, at, half, 1)
             terms.append(contract_rows(*after((left, grads), token)))
         return terms
+
+    def prepare(self, token):
+        self.partials = [
+            contract_rows(*after((features, grads), token)).astype(BF)
+            for features, grads in self.pairs
+        ]
+        return self.partials
 
     def send(self, token):
         ahead, back = ring_pairs(self.n)
         first, second = after(self.sums, token)
         self.flying = lax.ppermute(first, "dp", ahead), lax.ppermute(second, "dp", back)
 
-    def multiply(self, token):
-        kind = F32 if self.hop == self.n - 2 else BF
-        terms = (
-            self.terms_of(self.hop + 2, 0, token),
-            self.terms_of(2 * self.n - 2 - self.hop, 1, token),
-        )
-        self.terms = lax.optimization_barrier([[t.astype(kind) for t in side] for side in terms])
-        return self.terms
-
     def land(self, token):
         self.hop += 1
-        flying, terms = after((self.flying, self.terms), token)
-        if self.hop == self.n - 1:
-            self.sums = tuple(
-                [
-                    x.astype(F32) + y
-                    for x, y in zip(columns(arrived, [term.shape[1] for term in mine]), mine)
-                ]
-                for arrived, mine in zip(flying, terms)
-            )
-        else:
-            self.sums = tuple(landed(flying, terms))
+        flying = after(self.flying, token)
+        if self.hop < self.n - 1:
+            places = behind((self.hop + 1) % self.n), behind((self.n - 1 - self.hop) % self.n)
+            self.sums = tuple(landed(flying, self.partials, places))
+            return self.sums
+        self.sums = tuple(
+            [
+                x.astype(F32) + y.astype(F32)
+                for x, y in zip(
+                    columns(arrived, [part.shape[1] for part in self.partials]),
+                    self.terms_of(0, side, ()),
+                )
+            ]
+            for side, arrived in enumerate(flying)
+        )
         return self.sums
 
     def done(self):
@@ -615,7 +626,6 @@
         ring.send(token)
     for ring in gathers:
         ring.send(token)
-    token = [ring.multiply(token) for ring in rings] or token
     for piece in pieces:
         token = piece(token)
     token = [ring.land(token) for ring in rings] or token
@@ -843,12 +853,15 @@
     kept = {}
     mixed_ring = GatherRing(mixed_shard)
     mixed_ring.send(())
-    gate_shards, ffn_shards, rows_in = after(
-        ((w_out_gate, w_output), (w_ffn_gate, w_ffn_up, w_ffn_down), (inputs, cotangent)),
-        mixed_ring.last(),
-    )
-    inputs, cotangent = rows_in
+    inputs, cotangent = after((inputs, cotangent), mixed_ring.last())
     token = run_out(mixed_ring.last(), (), (), (mixed_ring,))
+
+    def arrived(hop):
+        at = min(hop, mixed_ring.n - 1)
+        return mixed_ring.first[at], mixed_ring.second[at]
+
+    gate_shards = after((w_out_gate, w_output), arrived(3))
+    ffn_shards = after((w_ffn_gate, w_ffn_up, w_ffn_down), arrived(4))
     gate_ring = GatherRing(jnp.concatenate((gate_shards[0], gate_shards[1].T), axis=1))
     ffn_ring = GatherRing(
         jnp.concatenate((ffn_shards[0], ffn_shards[1], ffn_shards[2].T), axis=1)
@@ -965,11 +978,11 @@
         return low
 
     def turn(token):
-        token = ffn_sum.far_sum(ffn_sum.far(token))
-        return kept["spread"].turn(token)
+        token = ffn_sum.far_sum(ffn_sum.far(kept["spread"].turn(token)))
+        kept["grad_attn"] = kept["spread"].rows(token)
+        return kept["grad_attn"]
 
     def attend_back(token):
-        kept["grad_attn"] = kept["spread"].rows(token)
         grad_mixer = jnp.dot(
             *after((kept["grad_attn"], output_full), token), preferred_element_type=jnp.float32
         )
@@ -1002,32 +1015,41 @@
         token,
         (ffn_scatter,),
         [
+            ffn_scatter.prepare,
             lambda t: mid_sum.far_sum(mid_sum.far(t)),
             mid_own,
             middle_back,
             turn,
             attend_back,
         ]
-        + backward[:2],
+        + backward[:1],
     )
     grad_stream, grad_norm_ffn, grad_attn = kept["grad_stream"], kept["norm_ffn"], kept["grad_attn"]
     _, grad_gate_proj, heads_gain_grad = kept["gate_back"]
-    gate_scatter = ScatterRing(((full_in, grad_gate_proj), (grad_attn, mixer)), token)
-    token = gate_scatter.sums
+    gate_scatter = ScatterRing(
+        ((full_in, grad_gate_proj), (grad_attn, mixer)), token
+    )
+    token = token, gate_scatter.sums
 
     def in_far(token):
         kept["in_sum"] = summed_rows(
             ((grad_gate_proj, gate_full), (kept["backward"][0], mixed_full)), rows
         )
-        return kept["in_sum"].far_sum(kept["in_sum"].far(token))
+        return kept["in_sum"].far(token)
 
     def leave(token):
-        kept["branch_ffn"] = ffn_sum.result(ffn_sum.own(ffn_sum.near(token)))
+        kept["branch_ffn"] = ffn_sum.result(token)
         kept["outputs"] = (valid * (stream + kept["branch_ffn"])).astype(jnp.bfloat16)
         return kept["outputs"]
 
+    def in_far_sum(token):
+        return kept["in_sum"].far_sum(token)
+
+    def in_near(token):
+        return kept["in_sum"].near(token)
+
     def in_own(token):
-        return kept["in_sum"].own(kept["in_sum"].near(token))
+        return kept["in_sum"].own(token)
 
     def last_back(token):
         through, kept["norm_attn"] = norm_back(
@@ -1039,10 +1061,15 @@
     token = run_out(
         token,
         (gate_scatter,),
-        backward[2:] + [in_far, in_own, leave, last_back],
+        [gate_scatter.prepare]
+        + backward[1:]
+        + [in_far, in_far_sum, lambda t: in_near(ffn_sum.near(t))],
     )
     grad_projected, grad_taps, grad_par, _, _ = kept["backward"]
     mixed_scatter = ScatterRing(((full_in, grad_projected),), token)
+    token = token, mixed_scatter.sums
+    token = slot(token, (mixed_scatter,), [ffn_sum.own, mixed_scatter.prepare])
+    token = slot(token, (mixed_scatter,), [leave, in_own])
     branch_ffn, outputs = kept["branch_ffn"], kept["outputs"]
     stat_sums = jnp.stack(
         [
@@ -1077,9 +1104,9 @@
         return kept["last"]
 
     token = run_out(
-        mixed_scatter.sums,
+        token,
         (mixed_scatter,),
-        [last_over_dp, last_over_tensor, common_over_dp, common_over_tensor],
+        [last_back, common_over_dp, last_over_dp, common_over_tensor, last_over_tensor],
     )
     grad_inputs = kept["grad_inputs"]
     owned_gate, owned_up, owned_down = ffn_scatter.results()

time: 977 us -> 935 us (0.957)
  waiting for transfers between devices: 343 us -> 295 us
  matrix products: 227 us -> 213 us
  other arithmetic: 34.3 us -> 47 us
  Pallas kernels: 105 us -> 116 us
    ppermute x21, waiting for transfers between devices: 102 us -> 59.1 us  [send(): lax.ppermute(first, 'dp', ahead)]
    dot_general x96 -> x18, matrix products: 75.5 us -> 49.3 us  [contract_rows(): lax.dot_general(left, right, (((0,), (0,)), ((), ())), preferred_element_...]
    unnamed x380 -> x314, local copies, waits for them, and re-layouts: 31.2 us -> 49.3 us
    pallas_call x18, Pallas kernels: 7.25 us -> 18.2 us  [landed(): pl.pallas_call(functools.partial(land_kernel, widths), grid_spec=pltpu.Pr...]
    ppermute x21, starting transfers between devices: 25.1 us -> 14.6 us  [send(): self.second.append(lax.ppermute(second, 'dp', back))]
    ppermute x21, starting transfers between devices: 20.4 us -> 30.6 us  [send(): self.first.append(lax.ppermute(first, 'dp', ahead))]
    dynamic_update_slice x54 -> x52, local copies, waits for them, and re-layouts: 46.5 us -> 43 us  [finish(): lax.dynamic_update_slice(full, part, (at, 0))]
  transfers between devices with their start and end apart: 118 -> 118, of which waited for: 73 -> 60; matrix products, arithmetic and copies ran while one was open for 28% -> 32% of each run, Pallas kernels for 10% -> 12%
where the time goes in v4:
time: 935 us; the launch traced here: 927 us
  waiting for transfers between devices  295 us (32%)
  matrix products  213 us (23%)
  local copies, waits for them, and re-layouts  147 us (16%)
  Pallas kernels  116 us (12%)
  starting transfers between devices  104 us (11%)
  other arithmetic  47 us (5%)
    ppermute x21, waiting for transfers between devices, send(): self.first.append(lax.ppermute(first, 'dp', ahead))  157 us
    dot_general x24, matrix products, times_transposed(): lax.dot_general(left, right, (((1,), (1,)), ((), ())), preferred_element_...  102 us
    ppermute x21, waiting for transfers between devices, send(): lax.ppermute(first, 'dp', ahead)  59.1 us
    pallas_call x4, Pallas kernels, mixer_bwd(): pl.pallas_call(functools.partial(bwd_kernel, H, DV, end, before is None),...  58.3 us
    unnamed x314, local copies, waits for them, and re-layouts  49.3 us
    dot_general x18, matrix products, contract_rows(): lax.dot_general(left, right, (((0,), (0,)), ((), ())), preferred_element_...  49.3 us
    dynamic_update_slice x52, local copies, waits for them, and re-layouts, finish(): lax.dynamic_update_slice(full, part, (at, 0))  43 us
    pallas_call x4, Pallas kernels, mixer_fwd(): pl.pallas_call(functools.partial(fwd_kernel, H, DV, NC, start), grid=(cou...  33.7 us
  transfers between devices with their start and end apart: 118, of which 60 were waited for; matrix products, arithmetic and copies ran while one was open for 32% of the time, Pallas kernels for 12%

profile of v4, /device:TPU:0, one launch (start us, length us, event | category | flops | bytes accessed | tf_op | source)
XLA Modules:
  0.0 927.1 jit_solution(17578917533424133761)
XLA Ops:
  15.6 11.0 %collective-permute-done = bf16[128,2176]{1,0:T(8,128)(2,1)S(1)} collective-permute-done((bf16[128,2176]{1,0:T(8,128)(2,1)}, bf16[128,2176]{1,0:T(8,128)(2,1)S(1)}, u32[]{:S(2)}, u32[]{:S(2)}) %collective-permute-start) | collective-permute-done | bytes 557088 | tf_op jit(solution)/shard_map/ppermute | solution.py:500
  37.7 9.1 collective-permute-done.5
  54.1 8.1 collective-permute-done.7
  120.3 8.6 collective-permute-done.15
  133.2 13.1 %fusion.38.p_ref.halo_ref = f32[1024,2176]{1,0:T(8,128)S(1)} fusion(bf16[1024,2048]{1,0:T(8,128)(2,1)S(1)} %constant_dynamic-update-slice_fusion.37, bf16[2048,2176]{1,0:T(8,128)(2,1)} %constant_dynamic-update-slice_fusion.21), kind=kOutput, calls=%fused_computation.307 | convolution fusion | flops 9126805504 | bytes 22020096 | tf_op jit(solution)/shard_map/dot_general | solution.py:891
  150.8 8.2 mixer_fwd.4
  163.3 8.3 mixer_fwd.5
  177.0 8.3 mixer_fwd.6
  188.5 9.0 mixer_fwd.7
  205.6 9.5 %collective-permute-done.27 = bf16[128,2048]{0,1:T(8,128)(2,1)S(1)} collective-permute-done((bf16[128,2048]{0,1:T(8,128)(2,1)S(1)}, bf16[128,2048]{0,1:T(8,128)(2,1)S(1)}, u32[]{:S(2)}, u32[]{:S(2)}) %collective-permute-start.27) | collective-permute-done | bytes 524320 | tf_op jit(solution)/shard_map/ppermute | solution.py:500
  221.1 10.2 %collective-permute-done.29 = bf16[128,2048]{0,1:T(8,128)(2,1)S(1)} collective-permute-done((bf16[128,2048]{0,1:T(8,128)(2,1)S(1)}, bf16[128,2048]{0,1:T(8,128)(2,1)S(1)}, u32[]{:S(2)}, u32[]{:S(2)}) %collective-permute-start.29) | collective-permute-done | bytes 524320 | tf_op jit(solution)/shard_map/ppermute | solution.py:500
  258.8 19.0 %collective-permute-done.34 = bf16[128,4224]{0,1:T(8,128)(2,1)S(1)} collective-permute-done((bf16[128,4224]{0,1:T(8,128)(2,1)}, bf16[128,4224]{0,1:T(8,128)(2,1)S(1)}, u32[]{:S(2)}, u32[]{:S(2)}) %collective-permute-start.34) | collective-permute-done | bytes 1081376 | tf_op jit(solution)/shard_map/ppermute | solution.py:500
  290.0 14.6 %collective-permute-done.36 = bf16[128,4224]{0,1:T(8,128)(2,1)S(1)} collective-permute-done((bf16[128,4224]{0,1:T(8,128)(2,1)S(1)}, bf16[128,4224]{0,1:T(8,128)(2,1)S(1)}, u32[]{:S(2)}, u32[]{:S(2)}) %collective-permute-start.36) | collective-permute-done | bytes 1081376 | tf_op jit(solution)/shard_map/ppermute | solution.py:500
  310.9 19.4 %collective-permute-done.49 = bf16[256,2048]{1,0:T(8,128)(2,1)S(1)} collective-permute-done((bf16[256,2048]{1,0:T(8,128)(2,1)S(1)}, bf16[256,2048]{1,0:T(8,128)(2,1)S(1)}, u32[]{:S(2)}, u32[]{:S(2)}) %collective-permute-start.49) | collective-permute-done | bytes 1048608 | tf_op jit(solution)/shard_map/ppermute | solution.py:669
  339.6 17.8 %collective-permute-done.42 = bf16[128,4224]{0,1:T(8,128)(2,1)S(1)} collective-permute-done((bf16[128,4224]{0,1:T(8,128)(2,1)S(1)}, bf16[128,4224]{0,1:T(8,128)(2,1)S(1)}, u32[]{:S(2)}, u32[]{:S(2)}) %collective-permute-start.42) | collective-permute-done | bytes 1081376 | tf_op jit(solution)/shard_map/ppermute | solution.py:500
  361.9 20.7 %collective-permute-done.44 = bf16[128,4224]{0,1:T(8,128)(2,1)S(1)} collective-permute-done((bf16[128,4224]{0,1:T(8,128)(2,1)S(1)}, bf16[128,4224]{0,1:T(8,128)(2,1)S(1)}, u32[]{:S(2)}, u32[]{:S(2)}) %collective-permute-start.44) | collective-permute-done | bytes 1081376 | tf_op jit(solution)/shard_map/ppermute | solution.py:500
  388.3 17.4 %collective-permute-done.46 = bf16[128,4224]{0,1:T(8,128)(2,1)S(1)} collective-permute-done((bf16[128,4224]{0,1:T(8,128)(2,1)S(1)}, bf16[128,4224]{0,1:T(8,128)(2,1)S(1)}, u32[]{:S(2)}, u32[]{:S(2)}) %collective-permute-start.46) | collective-permute-done | bytes 1081376 | tf_op jit(solution)/shard_map/ppermute | solution.py:500
  407.2 8.5 fusion.43
  415.7 8.5 fusion.42
  424.2 14.7 %multiply_convert_fusion = (bf16[1024,1408]{1,0:T(8,128)(2,1)S(1)}, bf16[1024,1408]{1,0:T(8,128)(2,1)S(1)}, bf16[1024,1408]{1,0:T(8,128)(2,1)S(1)}) fusion(f32[1024,1408]{1,0:T(8,128)} %fusion.42, f32[1024,1408]{1,0:T(8,128)} %fusion.43, bf16[1024,2048]{1,0:T(8,128)(2,1)} %copy-done.65, bf16[2048,1408]{0,1:T(8,128)(2,1)} %copy-done.56), kind=kOutput, calls=%fused_computation.4 | convolution fusion | flops 5927206912 | bytes 30146560 | tf_op jit(solution)/shard_map/dot_general | solution.py:959
  490.4 16.4 %collective-permute-done.56.first = bf16[128,4224]{1,0:T(8,128)(2,1)S(1)} collective-permute-done((bf16[128,4224]{1,0:T(8,128)(2,1)S(1)}, bf16[128,4224]{1,0:T(8,128)(2,1)S(1)}, u32[]{:S(2)}, u32[]{:S(2)}) %collective-permute-start.56) | collective-permute-done | bytes 1081376 | tf_op jit(solution)/shard_map/ppermute | solution.py:594
  524.9 8.6 collective-permute-done.59.first
  546.1 13.4 %collective-permute-done.65.first = bf16[128,4224]{1,0:T(8,128)(2,1)S(1)} collective-permute-done((bf16[128,4224]{1,0:T(8,128)(2,1)S(1)}, bf16[128,4224]{1,0:T(8,128)(2,1)S(1)}, u32[]{:S(2)}, u32[]{:S(2)}) %collective-permute-start.65) | collective-permute-done | bytes 1081376 | tf_op jit(solution)/shard_map/ppermute | solution.py:594
  588.8 11.1 %collective-permute-done.69.first = bf16[128,4224]{1,0:T(8,128)(2,1)S(1)} collective-permute-done((bf16[128,4224]{1,0:T(8,128)(2,1)S(1)}, bf16[128,4224]{1,0:T(8,128)(2,1)S(1)}, u32[]{:S(2)}, u32[]{:S(2)}) %collective-permute-start.69) | collective-permute-done | bytes 1081376 | tf_op jit(solution)/shard_map/ppermute | solution.py:594
  603.6 10.4 %fusion.48.in_ref = f32[1024,1024]{1,0:T(8,128)} fusion(bf16[1024,2048]{1,0:T(8,128)(2,1)} %copy-done.57, bf16[2048,1024]{0,1:T(8,128)(2,1)} %get-tuple-element.528), kind=kOutput, calls=%fused_computation.317 | convolution fusion | flops 4294967296 | bytes 12582912 | tf_op jit(solution)/shard_map/dot_general | solution.py:986
  636.9 14.5 %mixer_bwd.4 = (bf16[1024,2176]{1,0:T(8,128)(2,1)S(1)}, f32[4,2048]{1,0:T(4,128)S(1)}, f32[8,128]{1,0:T(8,128)S(1)}, f32[512,256]{1,0:T(8,128)S(1)}, f32[8,2048]{1,0:T(8,128)S(1)}) custom-call(f32[1024,2176]{1,0:T(8,128)S(1)} %copy-done.11, f32[1024,2176]{1,0:T(8,128)S(1)} %copy-done.11, f32[4,2048]{1,0:T(4,128)S(1)} %copy-done.33, f32[8,128]{1,0:T(8,128)S(1)} %copy-done.35, ...), custom_call_target="tpu_custom_call" | custom-call | flops 12000000000 | bytes 8388608 | tf_op jit(solution)/shard_map/mixer_bwd/pallas_call | solution.py:375
  682.6 14.4 %mixer_bwd.5 = (bf16[1024,2176]{1,0:T(8,128)(2,1)S(1)}, f32[4,2048]{1,0:T(4,128)S(1)}, f32[8,128]{1,0:T(8,128)S(1)}, f32[512,256]{1,0:T(8,128)S(1)}, f32[8,2048]{1,0:T(8,128)S(1)}) custom-call(f32[1024,2176]{1,0:T(8,128)S(1)} %copy-done.12, f32[1024,2176]{1,0:T(8,128)S(1)} %copy-done.12, f32[4,2048]{1,0:T(4,128)S(1)} %copy-done.33, ...), custom_call_target="tpu_custom_call", output_to_operand_aliasing={{0}: (8, {})} | custom-call | flops 12000000000 | bytes 8388608 | tf_op jit(solution)/shard_map/mixer_bwd/pallas_call | solution.py:375
  700.1 14.4 %mixer_bwd.6 = (bf16[1024,2176]{1,0:T(8,128)(2,1)S(1)}, f32[4,2048]{1,0:T(4,128)S(1)}, f32[8,128]{1,0:T(8,128)S(1)}, f32[512,256]{1,0:T(8,128)S(1)}, f32[8,2048]{1,0:T(8,128)S(1)}) custom-call(f32[1024,2176]{1,0:T(8,128)S(1)} %copy-done.12, f32[1024,2176]{1,0:T(8,128)S(1)} %copy-done.12, f32[4,2048]{1,0:T(4,128)S(1)} %copy-done.33, ...), custom_call_target="tpu_custom_call", output_to_operand_aliasing={{0}: (8, {})} | custom-call | flops 12000000000 | bytes 8388608 | tf_op jit(solution)/shard_map/mixer_bwd/pallas_call | solution.py:375
  717.7 14.9 %mixer_bwd.7 = (bf16[1024,2176]{1,0:T(8,128)(2,1)S(1)}, f32[4,2048]{1,0:T(4,128)S(1)}, f32[8,128]{1,0:T(8,128)S(1)}, f32[512,256]{1,0:T(8,128)}, f32[8,2048]{1,0:T(8,128)}) custom-call(f32[1024,2176]{1,0:T(8,128)S(1)} %copy-done.12, f32[1024,2176]{1,0:T(8,128)S(1)} %copy-done.12, f32[4,2048]{1,0:T(4,128)S(1)} %copy-done.33, ...), custom_call_target="tpu_custom_call", output_to_operand_aliasing={{0}: (8, {})} | custom-call | flops 12000000000 | bytes 8388608 | tf_op jit(solution)/shard_map/mixer_bwd/pallas_call | solution.py:375
  756.4 8.4 fusion.6
  775.6 8.0 fusion.5
  791.6 10.9 %convolution_convert_fusion.refs_0_.refs_1_ = bf16[2048,2176]{1,0:T(8,128)(2,1)S(1)} fusion(bf16[1024,2048]{1,0:T(8,128)(2,1)S(1)} %copy-done.62, bf16[1024,2176]{1,0:T(8,128)(2,1)S(1)} %get-tuple-element.639), kind=kOutput, calls=%fused_computation | convolution fusion | flops 9131261952 | bytes 17563648 | tf_op jit(solution)/shard_map/dot_general | solution.py:649
  (786 shorter events, 532.5 us)
Async XLA Ops:
  30.0 24.0 %collective-permute-start.3 = (bf16[256,2048]{1,0:T(8,128)(2,1)}, bf16[256,2048]{1,0:T(8,128)(2,1)}, u32[]{:S(2)}, u32[]{:S(2)}) collective-permute-start(bf16[256,2048]{1,0:T(8,128)(2,1)} %fusion.9), channel_id=1, source_target_pairs={{0,2},{2,0},{1,3},{3,1},{4,6},{6,4},{5,7},{7,5},{8,10},{10,8},{9,1... | collective-permute-start | bytes 3145736 | tf_op jit(solution)/shard_map/ppermute | solution.py:669
  31.6 65.7 %collective-permute-start.2 = (bf16[256,2048]{1,0:T(8,128)(2,1)}, bf16[256,2048]{1,0:T(8,128)(2,1)}, u32[]{:S(2)}, u32[]{:S(2)}) collective-permute-start(bf16[256,2048]{1,0:T(8,128)(2,1)} %fusion.9), channel_id=1, source_target_pairs={{0,1},{1,0},{2,3},{3,2},{4,5},{5,4},{6,7},{7,6},{8,9},{9,8},{10,11... | collective-permute-start | bytes 3145736 | tf_op jit(solution)/shard_map/ppermute | solution.py:670
  54.1 43.3 %collective-permute-start.4 = (bf16[256,2048]{1,0:T(8,128)(2,1)}, bf16[256,2048]{1,0:T(8,128)(2,1)}, u32[]{:S(2)}, u32[]{:S(2)}) collective-permute-start(bf16[256,2048]{1,0:T(8,128)(2,1)} %collective-permute-done.3), channel_id=1, source_target_pairs={{0,1},{1,0},{2,3},{3,2},{4,5},{5,4},{6,7},{7,6},{8,9},{9,8},{10,11... | collective-permute-start | bytes 3145736 | tf_op jit(solution)/shard_map/ppermute | solution.py:676
  251.3 26.5 %collective-permute-start.34 = (bf16[128,4224]{0,1:T(8,128)(2,1)}, bf16[128,4224]{0,1:T(8,128)(2,1)S(1)}, u32[]{:S(2)}, u32[]{:S(2)}) collective-permute-start(bf16[128,4224]{0,1:T(8,128)(2,1)} %collective-permute-done.31), channel_id=1, source_target_pairs={{0,8},{8,16},{16,24},{24,28},{28,20},{20,12},{12,4},{4,0},{1,9},{9... | collective-permute-start | bytes 3244040 | tf_op jit(solution)/shard_map/ppermute | solution.py:500
  252.7 26.4 %collective-permute-start.35 = (bf16[128,4224]{0,1:T(8,128)(2,1)S(1)}, bf16[128,4224]{0,1:T(8,128)(2,1)S(1)}, u32[]{:S(2)}, u32[]{:S(2)}) collective-permute-start(bf16[128,4224]{0,1:T(8,128)(2,1)S(1)} %collective-permute-done.32), channel_id=1, source_target_pairs={{8,0},{16,8},{24,16},{28,24},{20,28},{12,20},{4,12},{0,4},{9,1},{1... | collective-permute-start | bytes 3244040 | tf_op jit(solution)/shard_map/ppermute | solution.py:501
  258.2 47.5 %collective-permute-start.39 = (bf16[256,2048]{1,0:T(8,128)(2,1)S(1)}, bf16[256,2048]{1,0:T(8,128)(2,1)S(1)}, u32[]{:S(2)}, u32[]{:S(2)}) collective-permute-start(bf16[256,2048]{1,0:T(8,128)(2,1)S(1)} %add_convert_fusion.2), channel_id=1, source_target_pairs={{0,2},{2,0},{1,3},{3,1},{4,6},{6,4},{5,7},{7,5},{8,10},{10,8},{9,1... | collective-permute-start | bytes 3145736 | tf_op jit(solution)/shard_map/ppermute | solution.py:721
  279.1 25.4 %collective-permute-start.36 = (bf16[128,4224]{0,1:T(8,128)(2,1)S(1)}, bf16[128,4224]{0,1:T(8,128)(2,1)S(1)}, u32[]{:S(2)}, u32[]{:S(2)}) collective-permute-start(bf16[128,4224]{0,1:T(8,128)(2,1)S(1)} %collective-permute-done.34), channel_id=1, source_target_pairs={{0,8},{8,16},{16,24},{24,28},{28,20},{20,12},{12,4},{4,0},{1,9},{9... | collective-permute-start | bytes 3244040 | tf_op jit(solution)/shard_map/ppermute | solution.py:500
  280.9 24.9 %collective-permute-start.37 = (bf16[128,4224]{0,1:T(8,128)(2,1)S(1)}, bf16[128,4224]{0,1:T(8,128)(2,1)S(1)}, u32[]{:S(2)}, u32[]{:S(2)}) collective-permute-start(bf16[128,4224]{0,1:T(8,128)(2,1)S(1)} %collective-permute-done.35), channel_id=1, source_target_pairs={{8,0},{16,8},{24,16},{28,24},{20,28},{12,20},{4,12},{0,4},{9,1},{1... | collective-permute-start | bytes 3244040 | tf_op jit(solution)/shard_map/ppermute | solution.py:501
  310.8 25.1 %collective-permute-start.48 = (bf16[256,2048]{1,0:T(8,128)(2,1)S(1)}, bf16[256,2048]{1,0:T(8,128)(2,1)S(1)}, u32[]{:S(2)}, u32[]{:S(2)}) collective-permute-start(bf16[256,2048]{1,0:T(8,128)(2,1)S(1)} %multiply_convert_fusion.4), channel_id=1, source_target_pairs={{0,1},{1,0},{2,3},{3,2},{4,5},{5,4},{6,7},{7,6},{8,9},{9,8},{10,11... | collective-permute-start | bytes 3145736 | tf_op jit(solution)/shard_map/ppermute | solution.py:670
  333.4 24.0 %collective-permute-start.42 = (bf16[128,4224]{0,1:T(8,128)(2,1)S(1)}, bf16[128,4224]{0,1:T(8,128)(2,1)S(1)}, u32[]{:S(2)}, u32[]{:S(2)}) collective-permute-start(bf16[128,4224]{0,1:T(8,128)(2,1)S(1)} %collective-permute-done.40), channel_id=1, source_target_pairs={{0,8},{8,16},{16,24},{24,28},{28,20},{20,12},{12,4},{4,0},{1,9},{9... | collective-permute-start | bytes 3244040 | tf_op jit(solution)/shard_map/ppermute | solution.py:500
  334.2 24.6 %collective-permute-start.43 = (bf16[128,4224]{0,1:T(8,128)(2,1)S(1)}, bf16[128,4224]{0,1:T(8,128)(2,1)S(1)}, u32[]{:S(2)}, u32[]{:S(2)}) collective-permute-start(bf16[128,4224]{0,1:T(8,128)(2,1)S(1)} %collective-permute-done.41), channel_id=1, source_target_pairs={{8,0},{16,8},{24,16},{28,24},{20,28},{12,20},{4,12},{0,4},{9,1},{1... | collective-permute-start | bytes 3244040 | tf_op jit(solution)/shard_map/ppermute | solution.py:501
  339.6 46.7 %collective-permute-start.51 = (bf16[256,2048]{1,0:T(8,128)(2,1)S(1)}, bf16[256,2048]{1,0:T(8,128)(2,1)S(1)}, u32[]{:S(2)}, u32[]{:S(2)}) collective-permute-start(bf16[256,2048]{1,0:T(8,128)(2,1)S(1)} %copy-done.72), channel_id=1, source_target_pairs={{0,1},{1,0},{2,3},{3,2},{4,5},{5,4},{6,7},{7,6},{8,9},{9,8},{10,11... | collective-permute-start | bytes 3145736 | tf_op jit(solution)/shard_map/ppermute | solution.py:670
  361.4 24.8 %collective-permute-start.53 = (bf16[256,2048]{1,0:T(8,128)(2,1)S(1)}, bf16[256,2048]{1,0:T(8,128)(2,1)S(1)}, u32[]{:S(2)}, u32[]{:S(2)}) collective-permute-start(bf16[256,2048]{1,0:T(8,128)(2,1)S(1)} %collective-permute-done.52), channel_id=1, source_target_pairs={{0,1},{1,0},{2,3},{3,2},{4,5},{5,4},{6,7},{7,6},{8,9},{9,8},{10,11... | collective-permute-start | bytes 3145736 | tf_op jit(solution)/shard_map/ppermute | solution.py:676
  443.8 26.2 %collective-permute-start.54 = (bf16[128,4224]{1,0:T(8,128)(2,1)}, bf16[128,4224]{1,0:T(8,128)(2,1)S(1)}, u32[]{:S(2)}, u32[]{:S(2)}) collective-permute-start(bf16[128,4224]{1,0:T(8,128)(2,1)} %pad_maximum_fusion.3), channel_id=1, source_target_pairs={{0,8},{8,16},{16,24},{24,28},{28,20},{20,12},{12,4},{4,0},{1,9},{9... | collective-permute-start | bytes 3244040 | tf_op jit(solution)/shard_map/ppermute | solution.py:594
  444.4 25.7 %collective-permute-start.55 = (bf16[128,4224]{1,0:T(8,128)(2,1)S(1)}, bf16[128,4224]{1,0:T(8,128)(2,1)S(1)}, u32[]{:S(2)}, u32[]{:S(2)}) collective-permute-start(bf16[128,4224]{1,0:T(8,128)(2,1)S(1)} %pad_maximum_fusion.4), channel_id=1, source_target_pairs={{8,0},{16,8},{24,16},{28,24},{20,28},{12,20},{4,12},{0,4},{9,1},{1... | collective-permute-start | bytes 3244040 | tf_op jit(solution)/shard_map/ppermute | solution.py:594
  480.5 26.3 %collective-permute-start.56 = (bf16[128,4224]{1,0:T(8,128)(2,1)S(1)}, bf16[128,4224]{1,0:T(8,128)(2,1)S(1)}, u32[]{:S(2)}, u32[]{:S(2)}) collective-permute-start(bf16[128,4224]{1,0:T(8,128)(2,1)S(1)} %get-tuple-element.477), channel_id=1, source_target_pairs={{0,8},{8,16},{16,24},{24,28},{28,20},{20,12},{12,4},{4,0},{1,9},{9... | collective-permute-start | bytes 3244040 | tf_op jit(solution)/shard_map/ppermute | solution.py:594
  481.1 26.0 %collective-permute-start.57 = (bf16[128,4224]{1,0:T(8,128)(2,1)S(1)}, bf16[128,4224]{1,0:T(8,128)(2,1)S(1)}, u32[]{:S(2)}, u32[]{:S(2)}) collective-permute-start(bf16[128,4224]{1,0:T(8,128)(2,1)S(1)} %get-tuple-element.478), channel_id=1, source_target_pairs={{8,0},{16,8},{24,16},{28,24},{20,28},{12,20},{4,12},{0,4},{9,1},{1... | collective-permute-start | bytes 3244040 | tf_op jit(solution)/shard_map/ppermute | solution.py:594
  490.4 47.4 %collective-permute-start.62 = (bf16[256,2048]{1,0:T(8,128)(2,1)}, bf16[256,2048]{1,0:T(8,128)(2,1)S(1)}, u32[]{:S(2)}, u32[]{:S(2)}) collective-permute-start(bf16[256,2048]{1,0:T(8,128)(2,1)} %add_convert_fusion.1), channel_id=1, source_target_pairs={{0,2},{2,0},{1,3},{3,1},{4,6},{6,4},{5,7},{7,5},{8,10},{10,8},{9,1... | collective-permute-start | bytes 3145736 | tf_op jit(solution)/shard_map/ppermute | solution.py:721
  508.2 25.3 %collective-permute-start.59 = (bf16[128,4224]{1,0:T(8,128)(2,1)S(1)}, bf16[128,4224]{1,0:T(8,128)(2,1)S(1)}, u32[]{:S(2)}, u32[]{:S(2)}) collective-permute-start(bf16[128,4224]{1,0:T(8,128)(2,1)S(1)} %get-tuple-element.499), channel_id=1, source_target_pairs={{0,8},{8,16},{16,24},{24,28},{28,20},{20,12},{12,4},{4,0},{1,9},{9... | collective-permute-start | bytes 3244040 | tf_op jit(solution)/shard_map/ppermute | solution.py:594
  509.5 24.9 %collective-permute-start.60 = (bf16[128,4224]{1,0:T(8,128)(2,1)S(1)}, bf16[128,4224]{1,0:T(8,128)(2,1)S(1)}, u32[]{:S(2)}, u32[]{:S(2)}) collective-permute-start(bf16[128,4224]{1,0:T(8,128)(2,1)S(1)} %get-tuple-element.500), channel_id=1, source_target_pairs={{8,0},{16,8},{24,16},{28,24},{20,28},{12,20},{4,12},{0,4},{9,1},{1... | collective-permute-start | bytes 3244040 | tf_op jit(solution)/shard_map/ppermute | solution.py:594
  535.6 24.0 %collective-permute-start.65 = (bf16[128,4224]{1,0:T(8,128)(2,1)S(1)}, bf16[128,4224]{1,0:T(8,128)(2,1)S(1)}, u32[]{:S(2)}, u32[]{:S(2)}) collective-permute-start(bf16[128,4224]{1,0:T(8,128)(2,1)S(1)} %get-tuple-element.506), channel_id=1, source_target_pairs={{0,8},{8,16},{16,24},{24,28},{28,20},{20,12},{12,4},{4,0},{1,9},{9... | collective-permute-start | bytes 3244040 | tf_op jit(solution)/shard_map/ppermute | solution.py:594
  536.2 23.9 %collective-permute-start.66 = (bf16[128,4224]{1,0:T(8,128)(2,1)S(1)}, bf16[128,4224]{1,0:T(8,128)(2,1)S(1)}, u32[]{:S(2)}, u32[]{:S(2)}) collective-permute-start(bf16[128,4224]{1,0:T(8,128)(2,1)S(1)} %get-tuple-element.507), channel_id=1, source_target_pairs={{8,0},{16,8},{24,16},{28,24},{20,28},{12,20},{4,12},{0,4},{9,1},{1... | collective-permute-start | bytes 3244040 | tf_op jit(solution)/shard_map/ppermute | solution.py:594
  573.6 26.3 %collective-permute-start.69 = (bf16[128,4224]{1,0:T(8,128)(2,1)S(1)}, bf16[128,4224]{1,0:T(8,128)(2,1)S(1)}, u32[]{:S(2)}, u32[]{:S(2)}) collective-permute-start(bf16[128,4224]{1,0:T(8,128)(2,1)S(1)} %get-tuple-element.521), channel_id=1, source_target_pairs={{0,8},{8,16},{16,24},{24,28},{28,20},{20,12},{12,4},{4,0},{1,9},{9... | collective-permute-start | bytes 3244040 | tf_op jit(solution)/shard_map/ppermute | solution.py:594
  574.3 26.0 %collective-permute-start.70 = (bf16[128,4224]{1,0:T(8,128)(2,1)S(1)}, bf16[128,4224]{1,0:T(8,128)(2,1)S(1)}, u32[]{:S(2)}, u32[]{:S(2)}) collective-permute-start(bf16[128,4224]{1,0:T(8,128)(2,1)S(1)} %get-tuple-element.522), channel_id=1, source_target_pairs={{8,0},{16,8},{24,16},{28,24},{20,28},{12,20},{4,12},{0,4},{9,1},{1... | collective-permute-start | bytes 3244040 | tf_op jit(solution)/shard_map/ppermute | solution.py:594
  581.5 225.5 %collective-permute-start.93 = (bf16[256,2048]{1,0:T(8,128)(2,1)}, bf16[256,2048]{1,0:T(8,128)(2,1)}, u32[]{:S(2)}, u32[]{:S(2)}) collective-permute-start(bf16[256,2048]{1,0:T(8,128)(2,1)} %add_convert_fusion), channel_id=1, source_target_pairs={{0,2},{2,0},{1,3},{3,1},{4,6},{6,4},{5,7},{7,5},{8,10},{10,8},{9,1... | collective-permute-start | bytes 3145736 | tf_op jit(solution)/shard_map/ppermute | solution.py:721
  601.5 25.3 %collective-permute-start.71 = (bf16[128,4224]{1,0:T(8,128)(2,1)S(1)}, bf16[128,4224]{1,0:T(8,128)(2,1)S(1)}, u32[]{:S(2)}, u32[]{:S(2)}) collective-permute-start(bf16[128,4224]{1,0:T(8,128)(2,1)S(1)} %get-tuple-element.530), channel_id=1, source_target_pairs={{0,8},{8,16},{16,24},{24,28},{28,20},{20,12},{12,4},{4,0},{1,9},{9... | collective-permute-start | bytes 3244040 | tf_op jit(solution)/shard_map/ppermute | solution.py:594
  602.2 25.0 %collective-permute-start.72 = (bf16[128,4224]{1,0:T(8,128)(2,1)S(1)}, bf16[128,4224]{1,0:T(8,128)(2,1)S(1)}, u32[]{:S(2)}, u32[]{:S(2)}) collective-permute-start(bf16[128,4224]{1,0:T(8,128)(2,1)S(1)} %get-tuple-element.531), channel_id=1, source_target_pairs={{8,0},{16,8},{24,16},{28,24},{20,28},{12,20},{4,12},{0,4},{9,1},{1... | collective-permute-start | bytes 3244040 | tf_op jit(solution)/shard_map/ppermute | solution.py:594
  629.3 24.4 %collective-permute-start.73 = (bf16[128,4224]{1,0:T(8,128)(2,1)}, bf16[128,4224]{1,0:T(8,128)(2,1)}, u32[]{:S(2)}, u32[]{:S(2)}) collective-permute-start(bf16[128,4224]{1,0:T(8,128)(2,1)} %get-tuple-element.537), channel_id=1, source_target_pairs={{0,8},{8,16},{16,24},{24,28},{28,20},{20,12},{12,4},{4,0},{1,9},{9... | collective-permute-start | bytes 3244040 | tf_op jit(solution)/shard_map/ppermute | solution.py:594
  631.0 24.3 %collective-permute-start.74 = (bf16[128,4224]{1,0:T(8,128)(2,1)}, bf16[128,4224]{1,0:T(8,128)(2,1)}, u32[]{:S(2)}, u32[]{:S(2)}) collective-permute-start(bf16[128,4224]{1,0:T(8,128)(2,1)} %get-tuple-element.538), channel_id=1, source_target_pairs={{8,0},{16,8},{24,16},{28,24},{20,28},{12,20},{4,12},{0,4},{9,1},{1... | collective-permute-start | bytes 3244040 | tf_op jit(solution)/shard_map/ppermute | solution.py:594
  768.7 39.4 %collective-permute-start.92 = (bf16[256,2048]{1,0:T(8,128)(2,1)}, bf16[256,2048]{1,0:T(8,128)(2,1)}, u32[]{:S(2)}, u32[]{:S(2)}) collective-permute-start(bf16[256,2048]{1,0:T(8,128)(2,1)} %convolution_convert_fusion.10), channel_id=1, source_target_pairs={{0,1},{1,0},{2,3},{3,2},{4,5},{5,4},{6,7},{7,6},{8,9},{9,8},{10,11... | collective-permute-start | bytes 3145736 | tf_op jit(solution)/shard_map/ppermute | solution.py:728
  783.7 40.0 %collective-permute-start.98 = (bf16[256,2048]{1,0:T(8,128)(2,1)}, bf16[256,2048]{1,0:T(8,128)(2,1)}, u32[]{:S(2)}, u32[]{:S(2)}) collective-permute-start(bf16[256,2048]{1,0:T(8,128)(2,1)} %fusion.5), channel_id=1, source_target_pairs={{0,1},{1,0},{2,3},{3,2},{4,5},{5,4},{6,7},{7,6},{8,9},{9,8},{10,11... | collective-permute-start | bytes 3145736 | tf_op jit(solution)/shard_map/ppermute | solution.py:728
  803.7 24.2 %collective-permute-start.99 = (bf16[256,2048]{1,0:T(8,128)(2,1)}, bf16[256,2048]{1,0:T(8,128)(2,1)S(1)}, u32[]{:S(2)}, u32[]{:S(2)}) collective-permute-start(bf16[256,2048]{1,0:T(8,128)(2,1)} %fusion.6), channel_id=1, source_target_pairs={{0,2},{2,0},{1,3},{3,1},{4,6},{6,4},{5,7},{7,5},{8,10},{10,8},{9,1... | collective-permute-start | bytes 3145736 | tf_op jit(solution)/shard_map/ppermute | solution.py:721
  (236 other events, 3762.1 us)

commit v5 on v4

--- a/solution.py
+++ b/solution.py
@@ -506,9 +506,12 @@
     def through(self):
         return len(self.first) == self.n
 
-    def finish(self, widths):
+    def finish(self, widths, token=None):
         half = self.first[0].shape[0]
-        fulls = [jnp.zeros((self.n * 2 * half, width), BF) for width in widths]
+        if token is None:
+            token = self.first[1 % self.n], self.second[1 % self.n]
+        nothing = after(jnp.zeros((), BF), token)
+        fulls = [jnp.broadcast_to(nothing, (self.n * 2 * half, width)) for width in widths]
         for hop in range(self.n):
             for piece, at in (
                 (self.first[hop], behind(hop) * 2 * half),
@@ -861,11 +864,7 @@
         return mixed_ring.first[at], mixed_ring.second[at]
 
     gate_shards = after((w_out_gate, w_output), arrived(3))
-    ffn_shards = after((w_ffn_gate, w_ffn_up, w_ffn_down), arrived(4))
     gate_ring = GatherRing(jnp.concatenate((gate_shards[0], gate_shards[1].T), axis=1))
-    ffn_ring = GatherRing(
-        jnp.concatenate((ffn_shards[0], ffn_shards[1], ffn_shards[2].T), axis=1)
-    )
     [mixed_full] = mixed_ring.finish([mixed_shard.shape[1]])
 
     gain_attn = norm_attn
@@ -917,7 +916,13 @@
     )
     projected = kept["projected"]
     heads_out, written, inverse, states, _ = kept["forward"]
-    gate_full, output_full = gate_ring.finish([w_out_gate.shape[1], w_output.shape[0]])
+    ffn_shards = after((w_ffn_gate, w_ffn_up, w_ffn_down), arrived(4))
+    ffn_ring = GatherRing(
+        jnp.concatenate((ffn_shards[0], ffn_shards[1], ffn_shards[2].T), axis=1)
+    )
+    gate_full, output_full = gate_ring.finish(
+        [w_out_gate.shape[1], w_output.shape[0]], arrived(5)
+    )
 
     def gate(token):
         kept["gate"] = jnp.dot(
@@ -1081,32 +1086,25 @@
     )
     local = columns(grad_taps, widths[:3]) + [grad_par[0, :heads_here], grad_par[1, :heads_here]]
     whole = [conv_query, conv_key, conv_value, decay_log, decay_bias]
-    common = [stat_sums, grad_norm_ffn, heads_gain_grad[0]]
+    common = [stat_sums, grad_norm_ffn, heads_gain_grad[0], norm_attn]
     def common_over_dp(token):
-        kept["common"] = sum_over(after(packed(common + local), token), "dp")
+        parts = common[:3] + [kept["norm_attn"]] + local
+        kept["common"] = sum_over(after(packed(parts), token), "dp")
         return kept["common"]
 
     def common_over_tensor(token):
         sums = unpacked(kept["common"], [a.shape for a in common + local])
         spread = [
             place_slice(part, array, tensor_rank, part.ndim - 1)
-            for part, array in zip(sums[3:], whole)
+            for part, array in zip(sums[4:], whole)
         ]
-        kept["common"] = sum_over(after(packed(sums[:3] + spread), token), "tensor")
+        kept["common"] = sum_over(after(packed(sums[:4] + spread), token), "tensor")
         return kept["common"]
-
-    def last_over_dp(token):
-        kept["last"] = sum_over(after(packed([kept["norm_attn"]]), token), "dp")
-        return kept["last"]
-
-    def last_over_tensor(token):
-        kept["last"] = sum_over(after(kept["last"], token), "tensor")
-        return kept["last"]
 
     token = run_out(
         token,
         (mixed_scatter,),
-        [last_back, common_over_dp, last_over_dp, common_over_tensor, last_over_tensor],
+        [last_back, common_over_dp, common_over_tensor],
     )
     grad_inputs = kept["grad_inputs"]
     owned_gate, owned_up, owned_down = ffn_scatter.results()
@@ -1118,13 +1116,13 @@
         stat_sums,
         total_ffn_gain,
         total_heads_gain,
+        total_attn_gain,
         total_conv_query,
         total_conv_key,
         total_conv_value,
         total_decay_log,
         total_decay_bias,
     ) = unpacked(kept["common"], [a.shape for a in common + whole])
-    [total_attn_gain] = unpacked(kept["last"], [norm_attn.shape])
     statistics = jnp.sqrt(stat_sums[:3] / (stat_sums[3] * width))
     return (
         outputs,

time: 935 us -> 912 us (0.975)
  waiting for transfers between devices: 295 us -> 282 us
    ppermute x21, waiting for transfers between devices: 157 us -> 135 us  [send(): self.first.append(lax.ppermute(first, 'dp', ahead))]
    ppermute x21, waiting for transfers between devices: 14.7 us -> 27.8 us  [send(): self.second.append(lax.ppermute(second, 'dp', back))]
    ppermute x10 -> x5, waiting for transfers between devices: 24.7 us -> 11.8 us  [sum_over(): lax.ppermute(values, axis, [(i, i ^ step) for i in range(n)])]
    dynamic_update_slice x52 -> x53, local copies, waits for them, and re-layouts: 43 us -> 42.9 us  [finish(): lax.dynamic_update_slice(full, part, (at, 0))]
  transfers between devices with their start and end apart: 118 -> 113, of which waited for: 60 -> 71; matrix products, arithmetic and copies ran while one was open for 32% -> 33% of each run, Pallas kernels for 12% -> 12%
where the time goes in v5:
time: 912 us; the launch traced here: 904 us
  waiting for transfers between devices  282 us (31%)
  matrix products  206 us (23%)
  local copies, waits for them, and re-layouts  142 us (16%)
  Pallas kernels  116 us (13%)
  starting transfers between devices  107 us (12%)
  other arithmetic  47.1 us (5%)
    ppermute x21, waiting for transfers between devices, send(): self.first.append(lax.ppermute(first, 'dp', ahead))  135 us
    dot_general x24, matrix products, times_transposed(): lax.dot_general(left, right, (((1,), (1,)), ((), ())), preferred_element_...  97.1 us
    ppermute x21, waiting for transfers between devices, send(): lax.ppermute(first, 'dp', ahead)  65.7 us
    pallas_call x4, Pallas kernels, mixer_bwd(): pl.pallas_call(functools.partial(bwd_kernel, H, DV, end, before is None),...  58.3 us
    dot_general x18, matrix products, contract_rows(): lax.dot_general(left, right, (((0,), (0,)), ((), ())), preferred_element_...  49.3 us
    dynamic_update_slice x53, local copies, waits for them, and re-layouts, finish(): lax.dynamic_update_slice(full, part, (at, 0))  42.9 us
    unnamed x314, local copies, waits for them, and re-layouts  41.8 us
    pallas_call x4, Pallas kernels, mixer_fwd(): pl.pallas_call(functools.partial(fwd_kernel, H, DV, NC, start), grid=(cou...  33.8 us
  transfers between devices with their start and end apart: 113, of which 71 were waited for; matrix products, arithmetic and copies ran while one was open for 33% of the time, Pallas kernels for 12%

profile of v5, /device:TPU:0, one launch (start us, length us, event | category | flops | bytes accessed | tf_op | source)
XLA Modules:
  0.0 904.0 jit_solution(5953626894356900663)
XLA Ops:
  10.5 11.1 %collective-permute-done = bf16[128,2176]{1,0:T(8,128)(2,1)} collective-permute-done((bf16[128,2176]{1,0:T(8,128)(2,1)}, bf16[128,2176]{1,0:T(8,128)(2,1)}, u32[]{:S(2)}, u32[]{:S(2)}) %collective-permute-start) | collective-permute-done | bytes 557088 | tf_op jit(solution)/shard_map/ppermute | solution.py:500
  48.6 8.1 collective-permute-done.7
  109.7 8.6 collective-permute-done.15
  123.0 13.1 %fusion.39.p_ref.halo_ref = f32[1024,2176]{1,0:T(8,128)S(1)} fusion(bf16[1024,2048]{1,0:T(8,128)(2,1)S(1)} %constant_dynamic-update-slice_fusion.37, bf16[2048,2176]{1,0:T(8,128)(2,1)} %constant_dynamic-update-slice_fusion.21), kind=kOutput, calls=%fused_computation.308 | convolution fusion | flops 9126805504 | bytes 22020096 | tf_op jit(solution)/shard_map/dot_general | solution.py:890
  140.5 8.2 mixer_fwd.4
  153.5 8.3 mixer_fwd.5
  168.9 8.3 mixer_fwd.6
  182.7 9.1 %mixer_fwd.7 = (f32[1024,1024]{1,0:T(8,128)S(1)}, f32[1024,1024]{1,0:T(8,128)S(1)}, f32[1024,512]{1,0:T(8,128)S(1)}, f32[8,512,256]{2,1,0:T(8,128)S(1)}, f32[512,256]{1,0:T(8,128)}) custom-call(f32[1024,2176]{1,0:T(8,128)S(1)} %fusion.39.p_ref.halo_ref, ...), custom_call_target="tpu_custom_call", output_to_operand_aliasing={{0}: (5, {}), {1}: (6, {}), {2}: (7, {}), {3}: (8, {})} | custom-call | flops 6000000000 | bytes 6291456 | tf_op jit(solution)/shard_map/mixer_fwd/pallas_call | solution.py:331
  200.0 8.4 collective-permute-done.27
  214.0 10.5 %collective-permute-done.29 = bf16[128,2048]{0,1:T(8,128)(2,1)S(1)} collective-permute-done((bf16[128,2048]{0,1:T(8,128)(2,1)S(1)}, bf16[128,2048]{0,1:T(8,128)(2,1)S(1)}, u32[]{:S(2)}, u32[]{:S(2)}) %collective-permute-start.29) | collective-permute-done | bytes 524320 | tf_op jit(solution)/shard_map/ppermute | solution.py:500
  235.4 12.7 %collective-permute-done.31 = bf16[128,4224]{0,1:T(8,128)(2,1)} collective-permute-done((bf16[128,4224]{0,1:T(8,128)(2,1)S(1)}, bf16[128,4224]{0,1:T(8,128)(2,1)}, u32[]{:S(2)}, u32[]{:S(2)}) %collective-permute-start.31) | collective-permute-done | bytes 1081376 | tf_op jit(solution)/shard_map/ppermute | solution.py:500
  276.9 11.4 %collective-permute-done.36 = bf16[128,4224]{0,1:T(8,128)(2,1)S(1)} collective-permute-done((bf16[128,4224]{0,1:T(8,128)(2,1)S(1)}, bf16[128,4224]{0,1:T(8,128)(2,1)S(1)}, u32[]{:S(2)}, u32[]{:S(2)}) %collective-permute-start.36) | collective-permute-done | bytes 1081376 | tf_op jit(solution)/shard_map/ppermute | solution.py:500
  296.2 16.9 %collective-permute-done.49 = bf16[256,2048]{1,0:T(8,128)(2,1)S(1)} collective-permute-done((bf16[256,2048]{1,0:T(8,128)(2,1)S(1)}, bf16[256,2048]{1,0:T(8,128)(2,1)S(1)}, u32[]{:S(2)}, u32[]{:S(2)}) %collective-permute-start.49) | collective-permute-done | bytes 1048608 | tf_op jit(solution)/shard_map/ppermute | solution.py:672
  323.6 17.1 %collective-permute-done.42 = bf16[128,4224]{0,1:T(8,128)(2,1)S(1)} collective-permute-done((bf16[128,4224]{0,1:T(8,128)(2,1)S(1)}, bf16[128,4224]{0,1:T(8,128)(2,1)S(1)}, u32[]{:S(2)}, u32[]{:S(2)}) %collective-permute-start.42) | collective-permute-done | bytes 1081376 | tf_op jit(solution)/shard_map/ppermute | solution.py:500
  345.8 18.9 %collective-permute-done.44 = bf16[128,4224]{0,1:T(8,128)(2,1)S(1)} collective-permute-done((bf16[128,4224]{0,1:T(8,128)(2,1)S(1)}, bf16[128,4224]{0,1:T(8,128)(2,1)S(1)}, u32[]{:S(2)}, u32[]{:S(2)}) %collective-permute-start.44) | collective-permute-done | bytes 1081376 | tf_op jit(solution)/shard_map/ppermute | solution.py:500
  372.7 16.8 %collective-permute-done.46 = bf16[128,4224]{0,1:T(8,128)(2,1)S(1)} collective-permute-done((bf16[128,4224]{0,1:T(8,128)(2,1)S(1)}, bf16[128,4224]{0,1:T(8,128)(2,1)S(1)}, u32[]{:S(2)}, u32[]{:S(2)}) %collective-permute-start.46) | collective-permute-done | bytes 1081376 | tf_op jit(solution)/shard_map/ppermute | solution.py:500
  392.6 8.5 fusion.44
  401.1 8.5 fusion.43
  409.6 14.7 %multiply_convert_fusion = (bf16[1024,1408]{1,0:T(8,128)(2,1)S(1)}, bf16[1024,1408]{1,0:T(8,128)(2,1)S(1)}, bf16[1024,1408]{1,0:T(8,128)(2,1)S(1)}) fusion(f32[1024,1408]{1,0:T(8,128)} %fusion.43, f32[1024,1408]{1,0:T(8,128)} %fusion.44, bf16[1024,2048]{1,0:T(8,128)(2,1)} %copy-done.63, bf16[2048,1408]{0,1:T(8,128)(2,1)} %copy-done.55), kind=kOutput, calls=%fused_computation.4 | convolution fusion | flops 5927206912 | bytes 30146560 | tf_op jit(solution)/shard_map/dot_general | solution.py:964
  476.1 15.8 %collective-permute-done.56.first = bf16[128,4224]{1,0:T(8,128)(2,1)S(1)} collective-permute-done((bf16[128,4224]{1,0:T(8,128)(2,1)S(1)}, bf16[128,4224]{1,0:T(8,128)(2,1)S(1)}, u32[]{:S(2)}, u32[]{:S(2)}) %collective-permute-start.56) | collective-permute-done | bytes 1081376 | tf_op jit(solution)/shard_map/ppermute | solution.py:597
  509.9 8.8 collective-permute-done.59.first
  531.8 12.4 %collective-permute-done.65.first = bf16[128,4224]{1,0:T(8,128)(2,1)S(1)} collective-permute-done((bf16[128,4224]{1,0:T(8,128)(2,1)S(1)}, bf16[128,4224]{1,0:T(8,128)(2,1)S(1)}, u32[]{:S(2)}, u32[]{:S(2)}) %collective-permute-start.65) | collective-permute-done | bytes 1081376 | tf_op jit(solution)/shard_map/ppermute | solution.py:597
  574.2 10.4 %collective-permute-done.69.first = bf16[128,4224]{1,0:T(8,128)(2,1)S(1)} collective-permute-done((bf16[128,4224]{1,0:T(8,128)(2,1)S(1)}, bf16[128,4224]{1,0:T(8,128)(2,1)S(1)}, u32[]{:S(2)}, u32[]{:S(2)}) %collective-permute-start.69) | collective-permute-done | bytes 1081376 | tf_op jit(solution)/shard_map/ppermute | solution.py:597
  588.3 10.4 %fusion.49.in_ref = f32[1024,1024]{1,0:T(8,128)} fusion(bf16[1024,2048]{1,0:T(8,128)(2,1)} %copy-done.56, bf16[2048,1024]{0,1:T(8,128)(2,1)} %get-tuple-element.532), kind=kOutput, calls=%fused_computation.318 | convolution fusion | flops 4294967296 | bytes 12582912 | tf_op jit(solution)/shard_map/dot_general | solution.py:991
  621.7 14.5 %mixer_bwd.4 = (bf16[1024,2176]{1,0:T(8,128)(2,1)S(1)}, f32[4,2048]{1,0:T(4,128)S(1)}, f32[8,128]{1,0:T(8,128)S(1)}, f32[512,256]{1,0:T(8,128)S(1)}, f32[8,2048]{1,0:T(8,128)S(1)}) custom-call(f32[1024,2176]{1,0:T(8,128)S(1)} %copy-done.11, f32[1024,2176]{1,0:T(8,128)S(1)} %copy-done.11, f32[4,2048]{1,0:T(4,128)S(1)} %copy-done.33, f32[8,128]{1,0:T(8,128)S(1)} %copy-done.35, ...), custom_call_target="tpu_custom_call" | custom-call | flops 12000000000 | bytes 8388608 | tf_op jit(solution)/shard_map/mixer_bwd/pallas_call | solution.py:375
  666.5 14.4 %mixer_bwd.5 = (bf16[1024,2176]{1,0:T(8,128)(2,1)S(1)}, f32[4,2048]{1,0:T(4,128)S(1)}, f32[8,128]{1,0:T(8,128)S(1)}, f32[512,256]{1,0:T(8,128)S(1)}, f32[8,2048]{1,0:T(8,128)S(1)}) custom-call(f32[1024,2176]{1,0:T(8,128)S(1)} %copy-done.12, f32[1024,2176]{1,0:T(8,128)S(1)} %copy-done.12, f32[4,2048]{1,0:T(4,128)S(1)} %copy-done.33, ...), custom_call_target="tpu_custom_call", output_to_operand_aliasing={{0}: (8, {})} | custom-call | flops 12000000000 | bytes 8388608 | tf_op jit(solution)/shard_map/mixer_bwd/pallas_call | solution.py:375
  684.0 14.4 %mixer_bwd.6 = (bf16[1024,2176]{1,0:T(8,128)(2,1)S(1)}, f32[4,2048]{1,0:T(4,128)S(1)}, f32[8,128]{1,0:T(8,128)S(1)}, f32[512,256]{1,0:T(8,128)S(1)}, f32[8,2048]{1,0:T(8,128)S(1)}) custom-call(f32[1024,2176]{1,0:T(8,128)S(1)} %copy-done.12, f32[1024,2176]{1,0:T(8,128)S(1)} %copy-done.12, f32[4,2048]{1,0:T(4,128)S(1)} %copy-done.33, ...), custom_call_target="tpu_custom_call", output_to_operand_aliasing={{0}: (8, {})} | custom-call | flops 12000000000 | bytes 8388608 | tf_op jit(solution)/shard_map/mixer_bwd/pallas_call | solution.py:375
  701.6 14.9 %mixer_bwd.7 = (bf16[1024,2176]{1,0:T(8,128)(2,1)S(1)}, f32[4,2048]{1,0:T(4,128)S(1)}, f32[8,128]{1,0:T(8,128)S(1)}, f32[512,256]{1,0:T(8,128)}, f32[8,2048]{1,0:T(8,128)}) custom-call(f32[1024,2176]{1,0:T(8,128)S(1)} %copy-done.12, f32[1024,2176]{1,0:T(8,128)S(1)} %copy-done.12, f32[4,2048]{1,0:T(4,128)S(1)} %copy-done.33, ...), custom_call_target="tpu_custom_call", output_to_operand_aliasing={{0}: (8, {})} | custom-call | flops 12000000000 | bytes 8388608 | tf_op jit(solution)/shard_map/mixer_bwd/pallas_call | solution.py:375
  724.4 10.6 %fusion.4 = bf16[256,2048]{1,0:T(8,128)(2,1)} fusion(f32[256,2048]{1,0:T(8,128)} %fusion.50, bf16[256,2176]{1,0:T(8,128)(2,1)S(1)} %copy-done.99, bf16[2048,2176]{1,0:T(8,128)(2,1)} %constant_dynamic-update-slice_fusion.21), kind=kOutput, calls=%fused_computation.41 | convolution fusion | flops 2282749952 | bytes 13172736 | tf_op jit(solution)/shard_map/dot_general | solution.py:658
  741.0 8.4 fusion.6
  760.5 8.0 fusion.5
  778.2 11.0 %convolution_convert_fusion.refs_0_.refs_1_ = bf16[2048,2176]{1,0:T(8,128)(2,1)S(1)} fusion(bf16[1024,2048]{1,0:T(8,128)(2,1)S(1)} %copy-done.60, bf16[1024,2176]{1,0:T(8,128)(2,1)S(1)} %get-tuple-element.643), kind=kOutput, calls=%fused_computation | convolution fusion | flops 9131261952 | bytes 17563648 | tf_op jit(solution)/shard_map/dot_general | solution.py:652
  (771 shorter events, 526.1 us)
Async XLA Ops:
  24.5 24.0 %collective-permute-start.3 = (bf16[256,2048]{1,0:T(8,128)(2,1)}, bf16[256,2048]{1,0:T(8,128)(2,1)}, u32[]{:S(2)}, u32[]{:S(2)}) collective-permute-start(bf16[256,2048]{1,0:T(8,128)(2,1)} %fusion.9), channel_id=1, source_target_pairs={{0,2},{2,0},{1,3},{3,1},{4,6},{6,4},{5,7},{7,5},{8,10},{10,8},{9,1... | collective-permute-start | bytes 3145736 | tf_op jit(solution)/shard_map/ppermute | solution.py:672
  26.1 61.0 %collective-permute-start.2 = (bf16[256,2048]{1,0:T(8,128)(2,1)}, bf16[256,2048]{1,0:T(8,128)(2,1)}, u32[]{:S(2)}, u32[]{:S(2)}) collective-permute-start(bf16[256,2048]{1,0:T(8,128)(2,1)} %fusion.9), channel_id=1, source_target_pairs={{0,1},{1,0},{2,3},{3,2},{4,5},{5,4},{6,7},{7,6},{8,9},{9,8},{10,11... | collective-permute-start | bytes 3145736 | tf_op jit(solution)/shard_map/ppermute | solution.py:673
  48.6 38.6 %collective-permute-start.4 = (bf16[256,2048]{1,0:T(8,128)(2,1)}, bf16[256,2048]{1,0:T(8,128)(2,1)}, u32[]{:S(2)}, u32[]{:S(2)}) collective-permute-start(bf16[256,2048]{1,0:T(8,128)(2,1)} %collective-permute-done.3), channel_id=1, source_target_pairs={{0,1},{1,0},{2,3},{3,2},{4,5},{5,4},{6,7},{7,6},{8,9},{9,8},{10,11... | collective-permute-start | bytes 3145736 | tf_op jit(solution)/shard_map/ppermute | solution.py:679
  224.8 23.3 %collective-permute-start.31 = (bf16[128,4224]{0,1:T(8,128)(2,1)S(1)}, bf16[128,4224]{0,1:T(8,128)(2,1)}, u32[]{:S(2)}, u32[]{:S(2)}) collective-permute-start(bf16[128,4224]{0,1:T(8,128)(2,1)S(1)} %get-tuple-element.422), channel_id=1, source_target_pairs={{0,8},{8,16},{16,24},{24,28},{28,20},{20,12},{12,4},{4,0},{1,9},{9... | collective-permute-start | bytes 3244040 | tf_op jit(solution)/shard_map/ppermute | solution.py:500
  225.1 23.4 %collective-permute-start.32 = (bf16[128,4224]{0,1:T(8,128)(2,1)S(1)}, bf16[128,4224]{0,1:T(8,128)(2,1)S(1)}, u32[]{:S(2)}, u32[]{:S(2)}) collective-permute-start(bf16[128,4224]{0,1:T(8,128)(2,1)S(1)} %get-tuple-element.423), channel_id=1, source_target_pairs={{8,0},{16,8},{24,16},{28,24},{20,28},{12,20},{4,12},{0,4},{9,1},{1... | collective-permute-start | bytes 3244040 | tf_op jit(solution)/shard_map/ppermute | solution.py:501
  261.4 28.7 %collective-permute-start.39 = (bf16[256,2048]{1,0:T(8,128)(2,1)S(1)}, bf16[256,2048]{1,0:T(8,128)(2,1)S(1)}, u32[]{:S(2)}, u32[]{:S(2)}) collective-permute-start(bf16[256,2048]{1,0:T(8,128)(2,1)S(1)} %add_convert_fusion.2), channel_id=1, source_target_pairs={{0,2},{2,0},{1,3},{3,1},{4,6},{6,4},{5,7},{7,5},{8,10},{10,8},{9,1... | collective-permute-start | bytes 3145736 | tf_op jit(solution)/shard_map/ppermute | solution.py:724
  264.8 23.5 %collective-permute-start.36 = (bf16[128,4224]{0,1:T(8,128)(2,1)S(1)}, bf16[128,4224]{0,1:T(8,128)(2,1)S(1)}, u32[]{:S(2)}, u32[]{:S(2)}) collective-permute-start(bf16[128,4224]{0,1:T(8,128)(2,1)S(1)} %collective-permute-done.34), channel_id=1, source_target_pairs={{0,8},{8,16},{16,24},{24,28},{28,20},{20,12},{12,4},{4,0},{1,9},{9... | collective-permute-start | bytes 3244040 | tf_op jit(solution)/shard_map/ppermute | solution.py:500
  295.7 22.9 %collective-permute-start.41 = (bf16[128,4224]{0,1:T(8,128)(2,1)S(1)}, bf16[128,4224]{0,1:T(8,128)(2,1)S(1)}, u32[]{:S(2)}, u32[]{:S(2)}) collective-permute-start(bf16[128,4224]{0,1:T(8,128)(2,1)S(1)} %collective-permute-done.37), channel_id=1, source_target_pairs={{8,0},{16,8},{24,16},{28,24},{20,28},{12,20},{4,12},{0,4},{9,1},{1... | collective-permute-start | bytes 3244040 | tf_op jit(solution)/shard_map/ppermute | solution.py:501
  296.1 24.9 %collective-permute-start.48 = (bf16[256,2048]{1,0:T(8,128)(2,1)S(1)}, bf16[256,2048]{1,0:T(8,128)(2,1)S(1)}, u32[]{:S(2)}, u32[]{:S(2)}) collective-permute-start(bf16[256,2048]{1,0:T(8,128)(2,1)S(1)} %multiply_convert_fusion.4), channel_id=1, source_target_pairs={{0,1},{1,0},{2,3},{3,2},{4,5},{5,4},{6,7},{7,6},{8,9},{9,8},{10,11... | collective-permute-start | bytes 3145736 | tf_op jit(solution)/shard_map/ppermute | solution.py:673
  323.5 47.2 %collective-permute-start.51 = (bf16[256,2048]{1,0:T(8,128)(2,1)S(1)}, bf16[256,2048]{1,0:T(8,128)(2,1)S(1)}, u32[]{:S(2)}, u32[]{:S(2)}) collective-permute-start(bf16[256,2048]{1,0:T(8,128)(2,1)S(1)} %copy-done.75), channel_id=1, source_target_pairs={{0,1},{1,0},{2,3},{3,2},{4,5},{5,4},{6,7},{7,6},{8,9},{9,8},{10,11... | collective-permute-start | bytes 3145736 | tf_op jit(solution)/shard_map/ppermute | solution.py:673
  344.5 23.0 %collective-permute-start.45 = (bf16[128,4224]{0,1:T(8,128)(2,1)S(1)}, bf16[128,4224]{0,1:T(8,128)(2,1)S(1)}, u32[]{:S(2)}, u32[]{:S(2)}) collective-permute-start(bf16[128,4224]{0,1:T(8,128)(2,1)S(1)} %collective-permute-done.43), channel_id=1, source_target_pairs={{8,0},{16,8},{24,16},{28,24},{20,28},{12,20},{4,12},{0,4},{9,1},{1... | collective-permute-start | bytes 3244040 | tf_op jit(solution)/shard_map/ppermute | solution.py:501
  345.4 25.3 %collective-permute-start.53 = (bf16[256,2048]{1,0:T(8,128)(2,1)S(1)}, bf16[256,2048]{1,0:T(8,128)(2,1)S(1)}, u32[]{:S(2)}, u32[]{:S(2)}) collective-permute-start(bf16[256,2048]{1,0:T(8,128)(2,1)S(1)} %collective-permute-done.52), channel_id=1, source_target_pairs={{0,1},{1,0},{2,3},{3,2},{4,5},{5,4},{6,7},{7,6},{8,9},{9,8},{10,11... | collective-permute-start | bytes 3145736 | tf_op jit(solution)/shard_map/ppermute | solution.py:679
  429.1 26.2 %collective-permute-start.54 = (bf16[128,4224]{1,0:T(8,128)(2,1)}, bf16[128,4224]{1,0:T(8,128)(2,1)S(1)}, u32[]{:S(2)}, u32[]{:S(2)}) collective-permute-start(bf16[128,4224]{1,0:T(8,128)(2,1)} %pad_maximum_fusion.3), channel_id=1, source_target_pairs={{0,8},{8,16},{16,24},{24,28},{28,20},{20,12},{12,4},{4,0},{1,9},{9... | collective-permute-start | bytes 3244040 | tf_op jit(solution)/shard_map/ppermute | solution.py:597
  429.8 25.5 %collective-permute-start.55 = (bf16[128,4224]{1,0:T(8,128)(2,1)S(1)}, bf16[128,4224]{1,0:T(8,128)(2,1)S(1)}, u32[]{:S(2)}, u32[]{:S(2)}) collective-permute-start(bf16[128,4224]{1,0:T(8,128)(2,1)S(1)} %pad_maximum_fusion.4), channel_id=1, source_target_pairs={{8,0},{16,8},{24,16},{28,24},{20,28},{12,20},{4,12},{0,4},{9,1},{1... | collective-permute-start | bytes 3244040 | tf_op jit(solution)/shard_map/ppermute | solution.py:597
  465.7 26.3 %collective-permute-start.56 = (bf16[128,4224]{1,0:T(8,128)(2,1)S(1)}, bf16[128,4224]{1,0:T(8,128)(2,1)S(1)}, u32[]{:S(2)}, u32[]{:S(2)}) collective-permute-start(bf16[128,4224]{1,0:T(8,128)(2,1)S(1)} %get-tuple-element.481), channel_id=1, source_target_pairs={{0,8},{8,16},{16,24},{24,28},{28,20},{20,12},{12,4},{4,0},{1,9},{9... | collective-permute-start | bytes 3244040 | tf_op jit(solution)/shard_map/ppermute | solution.py:597
  466.3 26.0 %collective-permute-start.57 = (bf16[128,4224]{1,0:T(8,128)(2,1)S(1)}, bf16[128,4224]{1,0:T(8,128)(2,1)S(1)}, u32[]{:S(2)}, u32[]{:S(2)}) collective-permute-start(bf16[128,4224]{1,0:T(8,128)(2,1)S(1)} %get-tuple-element.482), channel_id=1, source_target_pairs={{8,0},{16,8},{24,16},{28,24},{20,28},{12,20},{4,12},{0,4},{9,1},{1... | collective-permute-start | bytes 3244040 | tf_op jit(solution)/shard_map/ppermute | solution.py:597
  475.4 47.1 %collective-permute-start.62 = (bf16[256,2048]{1,0:T(8,128)(2,1)}, bf16[256,2048]{1,0:T(8,128)(2,1)S(1)}, u32[]{:S(2)}, u32[]{:S(2)}) collective-permute-start(bf16[256,2048]{1,0:T(8,128)(2,1)} %add_convert_fusion.1), channel_id=1, source_target_pairs={{0,2},{2,0},{1,3},{3,1},{4,6},{6,4},{5,7},{7,5},{8,10},{10,8},{9,1... | collective-permute-start | bytes 3145736 | tf_op jit(solution)/shard_map/ppermute | solution.py:724
  493.5 25.2 %collective-permute-start.59 = (bf16[128,4224]{1,0:T(8,128)(2,1)S(1)}, bf16[128,4224]{1,0:T(8,128)(2,1)S(1)}, u32[]{:S(2)}, u32[]{:S(2)}) collective-permute-start(bf16[128,4224]{1,0:T(8,128)(2,1)S(1)} %get-tuple-element.503), channel_id=1, source_target_pairs={{0,8},{8,16},{16,24},{24,28},{28,20},{20,12},{12,4},{4,0},{1,9},{9... | collective-permute-start | bytes 3244040 | tf_op jit(solution)/shard_map/ppermute | solution.py:597
  494.1 24.9 %collective-permute-start.60 = (bf16[128,4224]{1,0:T(8,128)(2,1)S(1)}, bf16[128,4224]{1,0:T(8,128)(2,1)S(1)}, u32[]{:S(2)}, u32[]{:S(2)}) collective-permute-start(bf16[128,4224]{1,0:T(8,128)(2,1)S(1)} %get-tuple-element.504), channel_id=1, source_target_pairs={{8,0},{16,8},{24,16},{28,24},{20,28},{12,20},{4,12},{0,4},{9,1},{1... | collective-permute-start | bytes 3244040 | tf_op jit(solution)/shard_map/ppermute | solution.py:597
  520.2 24.0 %collective-permute-start.65 = (bf16[128,4224]{1,0:T(8,128)(2,1)S(1)}, bf16[128,4224]{1,0:T(8,128)(2,1)S(1)}, u32[]{:S(2)}, u32[]{:S(2)}) collective-permute-start(bf16[128,4224]{1,0:T(8,128)(2,1)S(1)} %get-tuple-element.510), channel_id=1, source_target_pairs={{0,8},{8,16},{16,24},{24,28},{28,20},{20,12},{12,4},{4,0},{1,9},{9... | collective-permute-start | bytes 3244040 | tf_op jit(solution)/shard_map/ppermute | solution.py:597
  520.8 23.9 %collective-permute-start.66 = (bf16[128,4224]{1,0:T(8,128)(2,1)S(1)}, bf16[128,4224]{1,0:T(8,128)(2,1)S(1)}, u32[]{:S(2)}, u32[]{:S(2)}) collective-permute-start(bf16[128,4224]{1,0:T(8,128)(2,1)S(1)} %get-tuple-element.511), channel_id=1, source_target_pairs={{8,0},{16,8},{24,16},{28,24},{20,28},{12,20},{4,12},{0,4},{9,1},{1... | collective-permute-start | bytes 3244040 | tf_op jit(solution)/shard_map/ppermute | solution.py:597
  529.4 23.0 %collective-permute-start.64 = (bf16[256,2048]{1,0:T(8,128)(2,1)}, bf16[256,2048]{1,0:T(8,128)(2,1)}, u32[]{:S(2)}, u32[]{:S(2)}) collective-permute-start(bf16[256,2048]{1,0:T(8,128)(2,1)} %get-tuple-element.521), channel_id=1, source_target_pairs={{0,2},{2,0},{1,3},{3,1},{4,6},{6,4},{5,7},{7,5},{8,10},{10,8},{9,1... | collective-permute-start | bytes 3145736 | tf_op jit(solution)/shard_map/ppermute | solution.py:672
  558.3 26.3 %collective-permute-start.69 = (bf16[128,4224]{1,0:T(8,128)(2,1)S(1)}, bf16[128,4224]{1,0:T(8,128)(2,1)S(1)}, u32[]{:S(2)}, u32[]{:S(2)}) collective-permute-start(bf16[128,4224]{1,0:T(8,128)(2,1)S(1)} %get-tuple-element.525), channel_id=1, source_target_pairs={{0,8},{8,16},{16,24},{24,28},{28,20},{20,12},{12,4},{4,0},{1,9},{9... | collective-permute-start | bytes 3244040 | tf_op jit(solution)/shard_map/ppermute | solution.py:597
  559.0 26.0 %collective-permute-start.70 = (bf16[128,4224]{1,0:T(8,128)(2,1)S(1)}, bf16[128,4224]{1,0:T(8,128)(2,1)S(1)}, u32[]{:S(2)}, u32[]{:S(2)}) collective-permute-start(bf16[128,4224]{1,0:T(8,128)(2,1)S(1)} %get-tuple-element.526), channel_id=1, source_target_pairs={{8,0},{16,8},{24,16},{28,24},{20,28},{12,20},{4,12},{0,4},{9,1},{1... | collective-permute-start | bytes 3244040 | tf_op jit(solution)/shard_map/ppermute | solution.py:597
  566.2 227.2 %collective-permute-start.93 = (bf16[256,2048]{1,0:T(8,128)(2,1)}, bf16[256,2048]{1,0:T(8,128)(2,1)}, u32[]{:S(2)}, u32[]{:S(2)}) collective-permute-start(bf16[256,2048]{1,0:T(8,128)(2,1)} %add_convert_fusion), channel_id=1, source_target_pairs={{0,2},{2,0},{1,3},{3,1},{4,6},{6,4},{5,7},{7,5},{8,10},{10,8},{9,1... | collective-permute-start | bytes 3145736 | tf_op jit(solution)/shard_map/ppermute | solution.py:724
  586.3 25.3 %collective-permute-start.71 = (bf16[128,4224]{1,0:T(8,128)(2,1)S(1)}, bf16[128,4224]{1,0:T(8,128)(2,1)S(1)}, u32[]{:S(2)}, u32[]{:S(2)}) collective-permute-start(bf16[128,4224]{1,0:T(8,128)(2,1)S(1)} %get-tuple-element.534), channel_id=1, source_target_pairs={{0,8},{8,16},{16,24},{24,28},{28,20},{20,12},{12,4},{4,0},{1,9},{9... | collective-permute-start | bytes 3244040 | tf_op jit(solution)/shard_map/ppermute | solution.py:597
  587.1 25.0 %collective-permute-start.72 = (bf16[128,4224]{1,0:T(8,128)(2,1)S(1)}, bf16[128,4224]{1,0:T(8,128)(2,1)S(1)}, u32[]{:S(2)}, u32[]{:S(2)}) collective-permute-start(bf16[128,4224]{1,0:T(8,128)(2,1)S(1)} %get-tuple-element.535), channel_id=1, source_target_pairs={{8,0},{16,8},{24,16},{28,24},{20,28},{12,20},{4,12},{0,4},{9,1},{1... | collective-permute-start | bytes 3244040 | tf_op jit(solution)/shard_map/ppermute | solution.py:597
  614.2 24.4 %collective-permute-start.73 = (bf16[128,4224]{1,0:T(8,128)(2,1)}, bf16[128,4224]{1,0:T(8,128)(2,1)}, u32[]{:S(2)}, u32[]{:S(2)}) collective-permute-start(bf16[128,4224]{1,0:T(8,128)(2,1)} %get-tuple-element.541), channel_id=1, source_target_pairs={{0,8},{8,16},{16,24},{24,28},{28,20},{20,12},{12,4},{4,0},{1,9},{9... | collective-permute-start | bytes 3244040 | tf_op jit(solution)/shard_map/ppermute | solution.py:597
  614.9 24.3 %collective-permute-start.74 = (bf16[128,4224]{1,0:T(8,128)(2,1)}, bf16[128,4224]{1,0:T(8,128)(2,1)}, u32[]{:S(2)}, u32[]{:S(2)}) collective-permute-start(bf16[128,4224]{1,0:T(8,128)(2,1)} %get-tuple-element.542), channel_id=1, source_target_pairs={{8,0},{16,8},{24,16},{28,24},{20,28},{12,20},{4,12},{0,4},{9,1},{1... | collective-permute-start | bytes 3244040 | tf_op jit(solution)/shard_map/ppermute | solution.py:597
  755.8 38.7 %collective-permute-start.92 = (bf16[256,2048]{1,0:T(8,128)(2,1)}, bf16[256,2048]{1,0:T(8,128)(2,1)}, u32[]{:S(2)}, u32[]{:S(2)}) collective-permute-start(bf16[256,2048]{1,0:T(8,128)(2,1)} %convolution_convert_fusion.10), channel_id=1, source_target_pairs={{0,1},{1,0},{2,3},{3,2},{4,5},{5,4},{6,7},{7,6},{8,9},{9,8},{10,11... | collective-permute-start | bytes 3145736 | tf_op jit(solution)/shard_map/ppermute | solution.py:731
  768.5 40.3 %collective-permute-start.96 = (bf16[256,2048]{1,0:T(8,128)(2,1)}, bf16[256,2048]{1,0:T(8,128)(2,1)}, u32[]{:S(2)}, u32[]{:S(2)}) collective-permute-start(bf16[256,2048]{1,0:T(8,128)(2,1)} %fusion.5), channel_id=1, source_target_pairs={{0,1},{1,0},{2,3},{3,2},{4,5},{5,4},{6,7},{7,6},{8,9},{9,8},{10,11... | collective-permute-start | bytes 3145736 | tf_op jit(solution)/shard_map/ppermute | solution.py:731
  790.0 23.8 %collective-permute-start.97 = (bf16[256,2048]{1,0:T(8,128)(2,1)}, bf16[256,2048]{1,0:T(8,128)(2,1)S(1)}, u32[]{:S(2)}, u32[]{:S(2)}) collective-permute-start(bf16[256,2048]{1,0:T(8,128)(2,1)} %fusion.6), channel_id=1, source_target_pairs={{0,2},{2,0},{1,3},{3,1},{4,6},{6,4},{5,7},{7,5},{8,10},{10,8},{9,1... | collective-permute-start | bytes 3145736 | tf_op jit(solution)/shard_map/ppermute | solution.py:724
  (231 other events, 3730.1 us)

commit v6 on v5

--- a/solution.py
+++ b/solution.py
@@ -348,7 +348,7 @@
         out_shape=shapes + [f((H * DK, DV), F32)],
         scratch_shapes=[pltpu.VMEM((NC * C + HALO, W), F32)],
         input_output_aliases=aliases,
-        compiler_params=room(22),
+        compiler_params=room(18),
         cost_estimate=pl.CostEstimate(
             flops=3 * 10**9 * count, bytes_accessed=3 * 2**20 * count, transcendentals=0
         ),
@@ -396,7 +396,7 @@
         out_shape=[f((L, wide), BF), f(taps.shape, F32), f(par.shape, F32), state, halo],
         scratch_shapes=[pltpu.VMEM((C + HALO, W), F32), pltpu.VMEM((C + HALO, W), F32)],
         input_output_aliases=aliases,
-        compiler_params=room(22),
+        compiler_params=room(16),
         cost_estimate=pl.CostEstimate(
             flops=6 * 10**9 * count, bytes_accessed=4 * 2**20 * count, transcendentals=0
         ),
@@ -421,7 +421,7 @@
         in_specs=[row_block(rows, width), row_block(rows, width), whole_block(gain)],
         out_specs=row_block(rows, width),
         out_shape=jax.ShapeDtypeStruct((L, width), BF),
-        compiler_params=room(12),
+        compiler_params=room(8),
         cost_estimate=pl.CostEstimate(flops=10**6, bytes_accessed=10**5, transcendentals=0),
         name="gate_fwd",
     )(heads_out, gate_proj, gain)
@@ -459,7 +459,7 @@
         in_specs=[row_block(rows, width), row_block(rows, width), whole_block(gain), row_block(rows, width)],
         out_specs=[row_block(rows, width), row_block(rows, width), whole_block(gain)],
         out_shape=[f((L, width), F32), f((L, width), BF), f(gain.shape, F32)],
-        compiler_params=room(14),
+        compiler_params=room(8),
         cost_estimate=pl.CostEstimate(flops=10**6, bytes_accessed=10**5, transcendentals=0),
         name="gate_bwd",
     )(heads_out, gate_proj, gain, grad_mixer)
@@ -556,7 +556,7 @@
             num_scalar_prefetch=1, grid=(steps,), in_specs=[sent, sent] + terms, out_specs=[sent, sent]
         ),
         out_shape=[jax.ShapeDtypeStruct((rows, wide), BF)] * 2,
-        compiler_params=room(10),
+        compiler_params=room(8),
         cost_estimate=pl.CostEstimate(flops=10**6, bytes_accessed=10**6, transcendentals=0),
         name="land",
     )(jnp.stack(places).astype(jnp.int32), *flying, *partials, *partials)

time: 912 us -> 901 us (0.988)
  waiting for transfers between devices: 282 us -> 309 us
  local copies, waits for them, and re-layouts: 142 us -> 124 us
  matrix products: 206 us -> 194 us
    ppermute x21, waiting for transfers between devices: 135 us -> 161 us  [send(): self.first.append(lax.ppermute(first, 'dp', ahead))]
    ppermute x21, waiting for transfers between devices: 65.7 us -> 82.8 us  [send(): lax.ppermute(first, 'dp', ahead)]
    dot_general x24, matrix products: 97.1 us -> 84.7 us  [times_transposed(): lax.dot_general(left, right, (((1,), (1,)), ((), ())), preferred_element_...]
    ppermute x21, waiting for transfers between devices: 27.8 us -> 16.3 us  [send(): self.second.append(lax.ppermute(second, 'dp', back))]
    dynamic_update_slice x53, local copies, waits for them, and re-layouts: 42.9 us -> 33.4 us  [finish(): lax.dynamic_update_slice(full, part, (at, 0))]
    unnamed x314 -> x296, local copies, waits for them, and re-layouts: 41.8 us -> 34.1 us
  transfers between devices with their start and end apart: 113 -> 113, of which waited for: 71 -> 68; matrix products, arithmetic and copies ran while one was open for 33% -> 31% of each run, Pallas kernels for 12% -> 13%
where the time goes in v6:
time: 901 us; the launch traced here: 893 us
  waiting for transfers between devices  309 us (34%)
  matrix products  194 us (22%)
  local copies, waits for them, and re-layouts  124 us (14%)
  Pallas kernels  116 us (13%)
  starting transfers between devices  102 us (11%)
  other arithmetic  42.6 us (5%)
    ppermute x21, waiting for transfers between devices, send(): self.first.append(lax.ppermute(first, 'dp', ahead))  161 us
    dot_general x24, matrix products, times_transposed(): lax.dot_general(left, right, (((1,), (1,)), ((), ())), preferred_element_...  84.7 us
    ppermute x21, waiting for transfers between devices, send(): lax.ppermute(first, 'dp', ahead)  82.8 us
    pallas_call x4, Pallas kernels, mixer_bwd(): pl.pallas_call(functools.partial(bwd_kernel, H, DV, end, before is None),...  58.4 us
    dot_general x18, matrix products, contract_rows(): lax.dot_general(left, right, (((0,), (0,)), ((), ())), preferred_element_...  51.5 us
    unnamed x296, local copies, waits for them, and re-layouts  34.1 us
    pallas_call x4, Pallas kernels, mixer_fwd(): pl.pallas_call(functools.partial(fwd_kernel, H, DV, NC, start), grid=(cou...  33.8 us
    dynamic_update_slice x53, local copies, waits for them, and re-layouts, finish(): lax.dynamic_update_slice(full, part, (at, 0))  33.4 us
  transfers between devices with their start and end apart: 113, of which 68 were waited for; matrix products, arithmetic and copies ran while one was open for 31% of the time, Pallas kernels for 13%

profile of v6, /device:TPU:0, one launch (start us, length us, event | category | flops | bytes accessed | tf_op | source)
XLA Modules:
  0.0 893.2 jit_solution(9162497200264108042)
XLA Ops:
  10.5 11.1 %collective-permute-done = bf16[128,2176]{1,0:T(8,128)(2,1)} collective-permute-done((bf16[128,2176]{1,0:T(8,128)(2,1)}, bf16[128,2176]{1,0:T(8,128)(2,1)}, u32[]{:S(2)}, u32[]{:S(2)}) %collective-permute-start) | collective-permute-done | bytes 557088 | tf_op jit(solution)/shard_map/ppermute | solution.py:500
  48.6 8.1 collective-permute-done.7
  112.1 8.6 collective-permute-done.15
  125.4 13.0 %fusion.39.p_ref.halo_ref = f32[1024,2176]{1,0:T(8,128)S(1)} fusion(bf16[1024,2048]{1,0:T(8,128)(2,1)S(1)} %constant_dynamic-update-slice_fusion.37, bf16[2048,2176]{1,0:T(8,128)(2,1)} %constant_dynamic-update-slice_fusion.21), kind=kOutput, calls=%fused_computation.308 | convolution fusion | flops 9126805504 | bytes 22020096 | tf_op jit(solution)/shard_map/dot_general | solution.py:890
  141.0 8.2 mixer_fwd.4
  156.1 8.3 mixer_fwd.5
  173.0 8.3 mixer_fwd.6
  187.2 9.1 %mixer_fwd.7 = (f32[1024,1024]{1,0:T(8,128)S(1)}, f32[1024,1024]{1,0:T(8,128)S(1)}, f32[1024,512]{1,0:T(8,128)S(1)}, f32[8,512,256]{2,1,0:T(8,128)S(1)}, f32[512,256]{1,0:T(8,128)}) custom-call(f32[1024,2176]{1,0:T(8,128)S(1)} %fusion.39.p_ref.halo_ref, ...), custom_call_target="tpu_custom_call", output_to_operand_aliasing={{0}: (5, {}), {1}: (6, {}), {2}: (7, {}), {3}: (8, {})} | custom-call | flops 6000000000 | bytes 6291456 | tf_op jit(solution)/shard_map/mixer_fwd/pallas_call | solution.py:331
  202.4 9.1 %collective-permute-done.27 = bf16[128,2048]{0,1:T(8,128)(2,1)S(1)} collective-permute-done((bf16[128,2048]{0,1:T(8,128)(2,1)S(1)}, bf16[128,2048]{0,1:T(8,128)(2,1)S(1)}, u32[]{:S(2)}, u32[]{:S(2)}) %collective-permute-start.27) | collective-permute-done | bytes 524320 | tf_op jit(solution)/shard_map/ppermute | solution.py:500
  214.6 12.3 %collective-permute-done.29 = bf16[128,2048]{0,1:T(8,128)(2,1)S(1)} collective-permute-done((bf16[128,2048]{0,1:T(8,128)(2,1)S(1)}, bf16[128,2048]{0,1:T(8,128)(2,1)S(1)}, u32[]{:S(2)}, u32[]{:S(2)}) %collective-permute-start.29) | collective-permute-done | bytes 524320 | tf_op jit(solution)/shard_map/ppermute | solution.py:500
  238.3 15.0 %collective-permute-done.31 = bf16[128,4224]{0,1:T(8,128)(2,1)} collective-permute-done((bf16[128,4224]{0,1:T(8,128)(2,1)S(1)}, bf16[128,4224]{0,1:T(8,128)(2,1)}, u32[]{:S(2)}, u32[]{:S(2)}) %collective-permute-start.31) | collective-permute-done | bytes 1081376 | tf_op jit(solution)/shard_map/ppermute | solution.py:500
  263.8 9.9 %collective-permute-done.34 = bf16[128,4224]{0,1:T(8,128)(2,1)S(1)} collective-permute-done((bf16[128,4224]{0,1:T(8,128)(2,1)}, bf16[128,4224]{0,1:T(8,128)(2,1)S(1)}, u32[]{:S(2)}, u32[]{:S(2)}) %collective-permute-start.34) | collective-permute-done | bytes 1081376 | tf_op jit(solution)/shard_map/ppermute | solution.py:500
  280.4 12.9 %collective-permute-done.36 = bf16[128,4224]{0,1:T(8,128)(2,1)S(1)} collective-permute-done((bf16[128,4224]{0,1:T(8,128)(2,1)S(1)}, bf16[128,4224]{0,1:T(8,128)(2,1)S(1)}, u32[]{:S(2)}, u32[]{:S(2)}) %collective-permute-start.36) | collective-permute-done | bytes 1081376 | tf_op jit(solution)/shard_map/ppermute | solution.py:500
  299.7 14.6 %collective-permute-done.49 = bf16[256,2048]{1,0:T(8,128)(2,1)S(1)} collective-permute-done((bf16[256,2048]{1,0:T(8,128)(2,1)S(1)}, bf16[256,2048]{1,0:T(8,128)(2,1)S(1)}, u32[]{:S(2)}, u32[]{:S(2)}) %collective-permute-start.49) | collective-permute-done | bytes 1048608 | tf_op jit(solution)/shard_map/ppermute | solution.py:672
  323.5 18.0 %collective-permute-done.42 = bf16[128,4224]{0,1:T(8,128)(2,1)S(1)} collective-permute-done((bf16[128,4224]{0,1:T(8,128)(2,1)S(1)}, bf16[128,4224]{0,1:T(8,128)(2,1)S(1)}, u32[]{:S(2)}, u32[]{:S(2)}) %collective-permute-start.42) | collective-permute-done | bytes 1081376 | tf_op jit(solution)/shard_map/ppermute | solution.py:500
  344.9 20.7 %collective-permute-done.44 = bf16[128,4224]{0,1:T(8,128)(2,1)S(1)} collective-permute-done((bf16[128,4224]{0,1:T(8,128)(2,1)S(1)}, bf16[128,4224]{0,1:T(8,128)(2,1)S(1)}, u32[]{:S(2)}, u32[]{:S(2)}) %collective-permute-start.44) | collective-permute-done | bytes 1081376 | tf_op jit(solution)/shard_map/ppermute | solution.py:500
  370.8 17.2 %collective-permute-done.46 = bf16[128,4224]{0,1:T(8,128)(2,1)S(1)} collective-permute-done((bf16[128,4224]{0,1:T(8,128)(2,1)S(1)}, bf16[128,4224]{0,1:T(8,128)(2,1)S(1)}, u32[]{:S(2)}, u32[]{:S(2)}) %collective-permute-start.46) | collective-permute-done | bytes 1081376 | tf_op jit(solution)/shard_map/ppermute | solution.py:500
  389.7 8.5 fusion.44
  398.2 8.5 fusion.43
  406.7 14.9 %multiply_convert_fusion = (bf16[1024,1408]{1,0:T(8,128)(2,1)S(1)}, bf16[1024,1408]{1,0:T(8,128)(2,1)S(1)}, bf16[1024,1408]{1,0:T(8,128)(2,1)S(1)}) fusion(f32[1024,1408]{1,0:T(8,128)} %fusion.43, f32[1024,1408]{1,0:T(8,128)} %fusion.44, bf16[1024,2048]{1,0:T(8,128)(2,1)} %copy-done.56, bf16[2048,1408]{0,1:T(8,128)(2,1)} %copy-done.49), kind=kOutput, calls=%fused_computation.4 | convolution fusion | flops 5927206912 | bytes 30146560 | tf_op jit(solution)/shard_map/dot_general | solution.py:964
  469.3 17.7 %collective-permute-done.56.first = bf16[128,4224]{1,0:T(8,128)(2,1)S(1)} collective-permute-done((bf16[128,4224]{1,0:T(8,128)(2,1)S(1)}, bf16[128,4224]{1,0:T(8,128)(2,1)S(1)}, u32[]{:S(2)}, u32[]{:S(2)}) %collective-permute-start.56) | collective-permute-done | bytes 1081376 | tf_op jit(solution)/shard_map/ppermute | solution.py:597
  525.4 16.3 %collective-permute-done.65.first = bf16[128,4224]{1,0:T(8,128)(2,1)S(1)} collective-permute-done((bf16[128,4224]{1,0:T(8,128)(2,1)S(1)}, bf16[128,4224]{1,0:T(8,128)(2,1)S(1)}, u32[]{:S(2)}, u32[]{:S(2)}) %collective-permute-start.65) | collective-permute-done | bytes 1081376 | tf_op jit(solution)/shard_map/ppermute | solution.py:597
  566.7 12.2 %collective-permute-done.69.first = bf16[128,4224]{1,0:T(8,128)(2,1)S(1)} collective-permute-done((bf16[128,4224]{1,0:T(8,128)(2,1)S(1)}, bf16[128,4224]{1,0:T(8,128)(2,1)S(1)}, u32[]{:S(2)}, u32[]{:S(2)}) %collective-permute-start.69) | collective-permute-done | bytes 1081376 | tf_op jit(solution)/shard_map/ppermute | solution.py:597
  583.5 8.0 fusion.49.in_ref
  596.7 10.2 %collective-permute-done.71.first = bf16[128,4224]{1,0:T(8,128)(2,1)S(1)} collective-permute-done((bf16[128,4224]{1,0:T(8,128)(2,1)}, bf16[128,4224]{1,0:T(8,128)(2,1)S(1)}, u32[]{:S(2)}, u32[]{:S(2)}) %collective-permute-start.71) | collective-permute-done | bytes 1081376 | tf_op jit(solution)/shard_map/ppermute | solution.py:597
  617.7 14.4 %mixer_bwd.4 = (bf16[1024,2176]{1,0:T(8,128)(2,1)S(1)}, f32[4,2048]{1,0:T(4,128)S(1)}, f32[8,128]{1,0:T(8,128)S(1)}, f32[512,256]{1,0:T(8,128)S(1)}, f32[8,2048]{1,0:T(8,128)S(1)}) custom-call(f32[1024,2176]{1,0:T(8,128)S(1)} %copy-done.11, f32[1024,2176]{1,0:T(8,128)S(1)} %copy-done.11, f32[4,2048]{1,0:T(4,128)S(1)} %pad_maximum_fusion.10.taps_ref, ...), custom_call_target="tpu_custom_call" | custom-call | flops 12000000000 | bytes 8388608 | tf_op jit(solution)/shard_map/mixer_bwd/pallas_call | solution.py:375
  646.9 7.2 convolution_convert_fusion.5.refs_0_.refs_2_
  659.0 14.5 %mixer_bwd.5 = (bf16[1024,2176]{1,0:T(8,128)(2,1)S(1)}, f32[4,2048]{1,0:T(4,128)S(1)}, f32[8,128]{1,0:T(8,128)S(1)}, f32[512,256]{1,0:T(8,128)S(1)}, f32[8,2048]{1,0:T(8,128)S(1)}) custom-call(f32[1024,2176]{1,0:T(8,128)S(1)} %bitcast.157, f32[1024,2176]{1,0:T(8,128)S(1)} %bitcast.157, f32[4,2048]{1,0:T(4,128)S(1)} %copy-done.30, ...), custom_call_target="tpu_custom_call", output_to_operand_aliasing={{0}: (8, {})} | custom-call | flops 12000000000 | bytes 8388608 | tf_op jit(solution)/shard_map/mixer_bwd/pallas_call | solution.py:375
  676.7 14.5 %mixer_bwd.6 = (bf16[1024,2176]{1,0:T(8,128)(2,1)S(1)}, f32[4,2048]{1,0:T(4,128)S(1)}, f32[8,128]{1,0:T(8,128)S(1)}, f32[512,256]{1,0:T(8,128)S(1)}, f32[8,2048]{1,0:T(8,128)S(1)}) custom-call(f32[1024,2176]{1,0:T(8,128)S(1)} %bitcast.157, f32[1024,2176]{1,0:T(8,128)S(1)} %bitcast.157, f32[4,2048]{1,0:T(4,128)S(1)} %copy-done.30, ...), custom_call_target="tpu_custom_call", output_to_operand_aliasing={{0}: (8, {})} | custom-call | flops 12000000000 | bytes 8388608 | tf_op jit(solution)/shard_map/mixer_bwd/pallas_call | solution.py:375
  694.5 15.0 %mixer_bwd.7 = (bf16[1024,2176]{1,0:T(8,128)(2,1)S(1)}, f32[4,2048]{1,0:T(4,128)S(1)}, f32[8,128]{1,0:T(8,128)S(1)}, f32[512,256]{1,0:T(8,128)}, f32[8,2048]{1,0:T(8,128)}) custom-call(f32[1024,2176]{1,0:T(8,128)S(1)} %bitcast.157, f32[1024,2176]{1,0:T(8,128)S(1)} %bitcast.157, f32[4,2048]{1,0:T(4,128)S(1)} %copy-done.30, ...), custom_call_target="tpu_custom_call", output_to_operand_aliasing={{0}: (8, {})} | custom-call | flops 12000000000 | bytes 8388608 | tf_op jit(solution)/shard_map/mixer_bwd/pallas_call | solution.py:375
  728.7 8.4 fusion.6
  767.2 11.0 %convolution_convert_fusion.refs_0_.refs_1_ = bf16[2048,2176]{1,0:T(8,128)(2,1)S(1)} fusion(bf16[1024,2048]{1,0:T(8,128)(2,1)S(1)} %copy-done.53, bf16[1024,2176]{1,0:T(8,128)(2,1)S(1)} %get-tuple-element.643), kind=kOutput, calls=%fused_computation | convolution fusion | flops 9131261952 | bytes 17563648 | tf_op jit(solution)/shard_map/dot_general | solution.py:652
  (755 shorter events, 502.5 us)
Async XLA Ops:
  24.5 24.0 %collective-permute-start.3 = (bf16[256,2048]{1,0:T(8,128)(2,1)}, bf16[256,2048]{1,0:T(8,128)(2,1)}, u32[]{:S(2)}, u32[]{:S(2)}) collective-permute-start(bf16[256,2048]{1,0:T(8,128)(2,1)} %fusion.9), channel_id=1, source_target_pairs={{0,2},{2,0},{1,3},{3,1},{4,6},{6,4},{5,7},{7,5},{8,10},{10,8},{9,1... | collective-permute-start | bytes 3145736 | tf_op jit(solution)/shard_map/ppermute | solution.py:672
  26.1 63.4 %collective-permute-start.2 = (bf16[256,2048]{1,0:T(8,128)(2,1)}, bf16[256,2048]{1,0:T(8,128)(2,1)}, u32[]{:S(2)}, u32[]{:S(2)}) collective-permute-start(bf16[256,2048]{1,0:T(8,128)(2,1)} %fusion.9), channel_id=1, source_target_pairs={{0,1},{1,0},{2,3},{3,2},{4,5},{5,4},{6,7},{7,6},{8,9},{9,8},{10,11... | collective-permute-start | bytes 3145736 | tf_op jit(solution)/shard_map/ppermute | solution.py:673
  48.6 40.9 %collective-permute-start.4 = (bf16[256,2048]{1,0:T(8,128)(2,1)}, bf16[256,2048]{1,0:T(8,128)(2,1)}, u32[]{:S(2)}, u32[]{:S(2)}) collective-permute-start(bf16[256,2048]{1,0:T(8,128)(2,1)} %collective-permute-done.3), channel_id=1, source_target_pairs={{0,1},{1,0},{2,3},{3,2},{4,5},{5,4},{6,7},{7,6},{8,9},{9,8},{10,11... | collective-permute-start | bytes 3145736 | tf_op jit(solution)/shard_map/ppermute | solution.py:679
  227.6 25.7 %collective-permute-start.31 = (bf16[128,4224]{0,1:T(8,128)(2,1)S(1)}, bf16[128,4224]{0,1:T(8,128)(2,1)}, u32[]{:S(2)}, u32[]{:S(2)}) collective-permute-start(bf16[128,4224]{0,1:T(8,128)(2,1)S(1)} %get-tuple-element.422), channel_id=1, source_target_pairs={{0,8},{8,16},{16,24},{24,28},{28,20},{20,12},{12,4},{4,0},{1,9},{9... | collective-permute-start | bytes 3244040 | tf_op jit(solution)/shard_map/ppermute | solution.py:500
  228.4 26.3 %collective-permute-start.32 = (bf16[128,4224]{0,1:T(8,128)(2,1)S(1)}, bf16[128,4224]{0,1:T(8,128)(2,1)}, u32[]{:S(2)}, u32[]{:S(2)}) collective-permute-start(bf16[128,4224]{0,1:T(8,128)(2,1)S(1)} %get-tuple-element.423), channel_id=1, source_target_pairs={{8,0},{16,8},{24,16},{28,24},{20,28},{12,20},{4,12},{0,4},{9,1},{1... | collective-permute-start | bytes 3244040 | tf_op jit(solution)/shard_map/ppermute | solution.py:501
  263.2 30.1 %collective-permute-start.39 = (bf16[256,2048]{1,0:T(8,128)(2,1)S(1)}, bf16[256,2048]{1,0:T(8,128)(2,1)S(1)}, u32[]{:S(2)}, u32[]{:S(2)}) collective-permute-start(bf16[256,2048]{1,0:T(8,128)(2,1)S(1)} %add_convert_fusion.2), channel_id=1, source_target_pairs={{0,2},{2,0},{1,3},{3,1},{4,6},{6,4},{5,7},{7,5},{8,10},{10,8},{9,1... | collective-permute-start | bytes 3145736 | tf_op jit(solution)/shard_map/ppermute | solution.py:724
  317.4 24.1 %collective-permute-start.42 = (bf16[128,4224]{0,1:T(8,128)(2,1)S(1)}, bf16[128,4224]{0,1:T(8,128)(2,1)S(1)}, u32[]{:S(2)}, u32[]{:S(2)}) collective-permute-start(bf16[128,4224]{0,1:T(8,128)(2,1)S(1)} %collective-permute-done.40), channel_id=1, source_target_pairs={{0,8},{8,16},{16,24},{24,28},{28,20},{20,12},{12,4},{4,0},{1,9},{9... | collective-permute-start | bytes 3244040 | tf_op jit(solution)/shard_map/ppermute | solution.py:500
  321.6 22.9 %collective-permute-start.52 = (bf16[256,2048]{1,0:T(8,128)(2,1)S(1)}, bf16[256,2048]{1,0:T(8,128)(2,1)S(1)}, u32[]{:S(2)}, u32[]{:S(2)}) collective-permute-start(bf16[256,2048]{1,0:T(8,128)(2,1)S(1)} %copy-done.69), channel_id=1, source_target_pairs={{0,2},{2,0},{1,3},{3,1},{4,6},{6,4},{5,7},{7,5},{8,10},{10,8},{9,1... | collective-permute-start | bytes 3145736 | tf_op jit(solution)/shard_map/ppermute | solution.py:672
  323.4 45.3 %collective-permute-start.51 = (bf16[256,2048]{1,0:T(8,128)(2,1)S(1)}, bf16[256,2048]{1,0:T(8,128)(2,1)S(1)}, u32[]{:S(2)}, u32[]{:S(2)}) collective-permute-start(bf16[256,2048]{1,0:T(8,128)(2,1)S(1)} %copy-done.69), channel_id=1, source_target_pairs={{0,1},{1,0},{2,3},{3,2},{4,5},{5,4},{6,7},{7,6},{8,9},{9,8},{10,11... | collective-permute-start | bytes 3145736 | tf_op jit(solution)/shard_map/ppermute | solution.py:673
  341.5 24.0 %collective-permute-start.44 = (bf16[128,4224]{0,1:T(8,128)(2,1)S(1)}, bf16[128,4224]{0,1:T(8,128)(2,1)S(1)}, u32[]{:S(2)}, u32[]{:S(2)}) collective-permute-start(bf16[128,4224]{0,1:T(8,128)(2,1)S(1)} %collective-permute-done.42), channel_id=1, source_target_pairs={{0,8},{8,16},{16,24},{24,28},{28,20},{20,12},{12,4},{4,0},{1,9},{9... | collective-permute-start | bytes 3244040 | tf_op jit(solution)/shard_map/ppermute | solution.py:500
  344.5 24.2 %collective-permute-start.53 = (bf16[256,2048]{1,0:T(8,128)(2,1)S(1)}, bf16[256,2048]{1,0:T(8,128)(2,1)S(1)}, u32[]{:S(2)}, u32[]{:S(2)}) collective-permute-start(bf16[256,2048]{1,0:T(8,128)(2,1)S(1)} %collective-permute-done.52), channel_id=1, source_target_pairs={{0,1},{1,0},{2,3},{3,2},{4,5},{5,4},{6,7},{7,6},{8,9},{9,8},{10,11... | collective-permute-start | bytes 3145736 | tf_op jit(solution)/shard_map/ppermute | solution.py:679
  365.6 22.4 %collective-permute-start.46 = (bf16[128,4224]{0,1:T(8,128)(2,1)S(1)}, bf16[128,4224]{0,1:T(8,128)(2,1)S(1)}, u32[]{:S(2)}, u32[]{:S(2)}) collective-permute-start(bf16[128,4224]{0,1:T(8,128)(2,1)S(1)} %collective-permute-done.44), channel_id=1, source_target_pairs={{0,8},{8,16},{16,24},{24,28},{28,20},{20,12},{12,4},{4,0},{1,9},{9... | collective-permute-start | bytes 3244040 | tf_op jit(solution)/shard_map/ppermute | solution.py:500
  425.5 25.1 %collective-permute-start.54 = (bf16[128,4224]{1,0:T(8,128)(2,1)S(1)}, bf16[128,4224]{1,0:T(8,128)(2,1)S(1)}, u32[]{:S(2)}, u32[]{:S(2)}) collective-permute-start(bf16[128,4224]{1,0:T(8,128)(2,1)S(1)} %pad_maximum_fusion.3), channel_id=1, source_target_pairs={{0,8},{8,16},{16,24},{24,28},{28,20},{20,12},{12,4},{4,0},{1,9},{9... | collective-permute-start | bytes 3244040 | tf_op jit(solution)/shard_map/ppermute | solution.py:597
  427.5 23.2 %collective-permute-start.55 = (bf16[128,4224]{1,0:T(8,128)(2,1)S(1)}, bf16[128,4224]{1,0:T(8,128)(2,1)S(1)}, u32[]{:S(2)}, u32[]{:S(2)}) collective-permute-start(bf16[128,4224]{1,0:T(8,128)(2,1)S(1)} %pad_maximum_fusion.4), channel_id=1, source_target_pairs={{8,0},{16,8},{24,16},{28,24},{20,28},{12,20},{4,12},{0,4},{9,1},{1... | collective-permute-start | bytes 3244040 | tf_op jit(solution)/shard_map/ppermute | solution.py:597
  460.8 26.3 %collective-permute-start.56 = (bf16[128,4224]{1,0:T(8,128)(2,1)S(1)}, bf16[128,4224]{1,0:T(8,128)(2,1)S(1)}, u32[]{:S(2)}, u32[]{:S(2)}) collective-permute-start(bf16[128,4224]{1,0:T(8,128)(2,1)S(1)} %get-tuple-element.481), channel_id=1, source_target_pairs={{0,8},{8,16},{16,24},{24,28},{28,20},{20,12},{12,4},{4,0},{1,9},{9... | collective-permute-start | bytes 3244040 | tf_op jit(solution)/shard_map/ppermute | solution.py:597
  462.7 26.0 %collective-permute-start.57 = (bf16[128,4224]{1,0:T(8,128)(2,1)S(1)}, bf16[128,4224]{1,0:T(8,128)(2,1)S(1)}, u32[]{:S(2)}, u32[]{:S(2)}) collective-permute-start(bf16[128,4224]{1,0:T(8,128)(2,1)S(1)} %get-tuple-element.482), channel_id=1, source_target_pairs={{8,0},{16,8},{24,16},{28,24},{20,28},{12,20},{4,12},{0,4},{9,1},{1... | collective-permute-start | bytes 3244040 | tf_op jit(solution)/shard_map/ppermute | solution.py:597
  469.2 50.7 %collective-permute-start.62 = (bf16[256,2048]{1,0:T(8,128)(2,1)S(1)}, bf16[256,2048]{1,0:T(8,128)(2,1)S(1)}, u32[]{:S(2)}, u32[]{:S(2)}) collective-permute-start(bf16[256,2048]{1,0:T(8,128)(2,1)S(1)} %add_convert_fusion.1), channel_id=1, source_target_pairs={{0,2},{2,0},{1,3},{3,1},{4,6},{6,4},{5,7},{7,5},{8,10},{10,8},{9,1... | collective-permute-start | bytes 3145736 | tf_op jit(solution)/shard_map/ppermute | solution.py:724
  489.8 25.2 %collective-permute-start.59 = (bf16[128,4224]{1,0:T(8,128)(2,1)S(1)}, bf16[128,4224]{1,0:T(8,128)(2,1)S(1)}, u32[]{:S(2)}, u32[]{:S(2)}) collective-permute-start(bf16[128,4224]{1,0:T(8,128)(2,1)S(1)} %get-tuple-element.503), channel_id=1, source_target_pairs={{0,8},{8,16},{16,24},{24,28},{28,20},{20,12},{12,4},{4,0},{1,9},{9... | collective-permute-start | bytes 3244040 | tf_op jit(solution)/shard_map/ppermute | solution.py:597
  491.6 24.9 %collective-permute-start.60 = (bf16[128,4224]{1,0:T(8,128)(2,1)S(1)}, bf16[128,4224]{1,0:T(8,128)(2,1)S(1)}, u32[]{:S(2)}, u32[]{:S(2)}) collective-permute-start(bf16[128,4224]{1,0:T(8,128)(2,1)S(1)} %get-tuple-element.504), channel_id=1, source_target_pairs={{8,0},{16,8},{24,16},{28,24},{20,28},{12,20},{4,12},{0,4},{9,1},{1... | collective-permute-start | bytes 3244040 | tf_op jit(solution)/shard_map/ppermute | solution.py:597
  517.7 24.0 %collective-permute-start.65 = (bf16[128,4224]{1,0:T(8,128)(2,1)S(1)}, bf16[128,4224]{1,0:T(8,128)(2,1)S(1)}, u32[]{:S(2)}, u32[]{:S(2)}) collective-permute-start(bf16[128,4224]{1,0:T(8,128)(2,1)S(1)} %get-tuple-element.510), channel_id=1, source_target_pairs={{0,8},{8,16},{16,24},{24,28},{28,20},{20,12},{12,4},{4,0},{1,9},{9... | collective-permute-start | bytes 3244040 | tf_op jit(solution)/shard_map/ppermute | solution.py:597
  518.6 23.9 %collective-permute-start.66 = (bf16[128,4224]{1,0:T(8,128)(2,1)S(1)}, bf16[128,4224]{1,0:T(8,128)(2,1)S(1)}, u32[]{:S(2)}, u32[]{:S(2)}) collective-permute-start(bf16[128,4224]{1,0:T(8,128)(2,1)S(1)} %get-tuple-element.511), channel_id=1, source_target_pairs={{8,0},{16,8},{24,16},{28,24},{20,28},{12,20},{4,12},{0,4},{9,1},{1... | collective-permute-start | bytes 3244040 | tf_op jit(solution)/shard_map/ppermute | solution.py:597
  524.0 22.8 %collective-permute-start.64 = (bf16[256,2048]{1,0:T(8,128)(2,1)S(1)}, bf16[256,2048]{1,0:T(8,128)(2,1)}, u32[]{:S(2)}, u32[]{:S(2)}) collective-permute-start(bf16[256,2048]{1,0:T(8,128)(2,1)S(1)} %get-tuple-element.521), channel_id=1, source_target_pairs={{0,2},{2,0},{1,3},{3,1},{4,6},{6,4},{5,7},{7,5},{8,10},{10,8},{9,1... | collective-permute-start | bytes 3145736 | tf_op jit(solution)/shard_map/ppermute | solution.py:672
  552.7 26.3 %collective-permute-start.69 = (bf16[128,4224]{1,0:T(8,128)(2,1)S(1)}, bf16[128,4224]{1,0:T(8,128)(2,1)S(1)}, u32[]{:S(2)}, u32[]{:S(2)}) collective-permute-start(bf16[128,4224]{1,0:T(8,128)(2,1)S(1)} %get-tuple-element.525), channel_id=1, source_target_pairs={{0,8},{8,16},{16,24},{24,28},{28,20},{20,12},{12,4},{4,0},{1,9},{9... | collective-permute-start | bytes 3244040 | tf_op jit(solution)/shard_map/ppermute | solution.py:597
  553.6 26.0 %collective-permute-start.70 = (bf16[128,4224]{1,0:T(8,128)(2,1)S(1)}, bf16[128,4224]{1,0:T(8,128)(2,1)S(1)}, u32[]{:S(2)}, u32[]{:S(2)}) collective-permute-start(bf16[128,4224]{1,0:T(8,128)(2,1)S(1)} %get-tuple-element.526), channel_id=1, source_target_pairs={{8,0},{16,8},{24,16},{28,24},{20,28},{12,20},{4,12},{0,4},{9,1},{1... | collective-permute-start | bytes 3244040 | tf_op jit(solution)/shard_map/ppermute | solution.py:597
  560.8 221.6 %collective-permute-start.93 = (bf16[256,2048]{1,0:T(8,128)(2,1)}, bf16[256,2048]{1,0:T(8,128)(2,1)}, u32[]{:S(2)}, u32[]{:S(2)}) collective-permute-start(bf16[256,2048]{1,0:T(8,128)(2,1)} %add_convert_fusion), channel_id=1, source_target_pairs={{0,2},{2,0},{1,3},{3,1},{4,6},{6,4},{5,7},{7,5},{8,10},{10,8},{9,1... | collective-permute-start | bytes 3145736 | tf_op jit(solution)/shard_map/ppermute | solution.py:724
  581.5 25.5 %collective-permute-start.71 = (bf16[128,4224]{1,0:T(8,128)(2,1)}, bf16[128,4224]{1,0:T(8,128)(2,1)S(1)}, u32[]{:S(2)}, u32[]{:S(2)}) collective-permute-start(bf16[128,4224]{1,0:T(8,128)(2,1)} %get-tuple-element.534), channel_id=1, source_target_pairs={{0,8},{8,16},{16,24},{24,28},{28,20},{20,12},{12,4},{4,0},{1,9},{9... | collective-permute-start | bytes 3244040 | tf_op jit(solution)/shard_map/ppermute | solution.py:597
  582.2 25.0 %collective-permute-start.72 = (bf16[128,4224]{1,0:T(8,128)(2,1)S(1)}, bf16[128,4224]{1,0:T(8,128)(2,1)S(1)}, u32[]{:S(2)}, u32[]{:S(2)}) collective-permute-start(bf16[128,4224]{1,0:T(8,128)(2,1)S(1)} %get-tuple-element.535), channel_id=1, source_target_pairs={{8,0},{16,8},{24,16},{28,24},{20,28},{12,20},{4,12},{0,4},{9,1},{1... | collective-permute-start | bytes 3244040 | tf_op jit(solution)/shard_map/ppermute | solution.py:597
  609.2 24.9 %collective-permute-start.73 = (bf16[128,4224]{1,0:T(8,128)(2,1)}, bf16[128,4224]{1,0:T(8,128)(2,1)S(1)}, u32[]{:S(2)}, u32[]{:S(2)}) collective-permute-start(bf16[128,4224]{1,0:T(8,128)(2,1)} %get-tuple-element.541), channel_id=1, source_target_pairs={{0,8},{8,16},{16,24},{24,28},{28,20},{20,12},{12,4},{4,0},{1,9},{9... | collective-permute-start | bytes 3244040 | tf_op jit(solution)/shard_map/ppermute | solution.py:597
  610.0 24.4 %collective-permute-start.74 = (bf16[128,4224]{1,0:T(8,128)(2,1)}, bf16[128,4224]{1,0:T(8,128)(2,1)S(1)}, u32[]{:S(2)}, u32[]{:S(2)}) collective-permute-start(bf16[128,4224]{1,0:T(8,128)(2,1)} %get-tuple-element.542), channel_id=1, source_target_pairs={{8,0},{16,8},{24,16},{28,24},{20,28},{12,20},{4,12},{0,4},{9,1},{1... | collective-permute-start | bytes 3244040 | tf_op jit(solution)/shard_map/ppermute | solution.py:597
  742.4 40.5 %collective-permute-start.92 = (bf16[256,2048]{1,0:T(8,128)(2,1)}, bf16[256,2048]{1,0:T(8,128)(2,1)}, u32[]{:S(2)}, u32[]{:S(2)}) collective-permute-start(bf16[256,2048]{1,0:T(8,128)(2,1)} %convolution_convert_fusion.10), channel_id=1, source_target_pairs={{0,1},{1,0},{2,3},{3,2},{4,5},{5,4},{6,7},{7,6},{8,9},{9,8},{10,11... | collective-permute-start | bytes 3145736 | tf_op jit(solution)/shard_map/ppermute | solution.py:731
  752.9 44.9 %collective-permute-start.96 = (bf16[256,2048]{1,0:T(8,128)(2,1)}, bf16[256,2048]{1,0:T(8,128)(2,1)}, u32[]{:S(2)}, u32[]{:S(2)}) collective-permute-start(bf16[256,2048]{1,0:T(8,128)(2,1)} %fusion.5), channel_id=1, source_target_pairs={{0,1},{1,0},{2,3},{3,2},{4,5},{5,4},{6,7},{7,6},{8,9},{9,8},{10,11... | collective-permute-start | bytes 3145736 | tf_op jit(solution)/shard_map/ppermute | solution.py:731
  778.9 23.8 %collective-permute-start.97 = (bf16[256,2048]{1,0:T(8,128)(2,1)}, bf16[256,2048]{1,0:T(8,128)(2,1)S(1)}, u32[]{:S(2)}, u32[]{:S(2)}) collective-permute-start(bf16[256,2048]{1,0:T(8,128)(2,1)} %fusion.6), channel_id=1, source_target_pairs={{0,2},{2,0},{1,3},{3,1},{4,6},{6,4},{5,7},{7,5},{8,10},{10,8},{9,1... | collective-permute-start | bytes 3145736 | tf_op jit(solution)/shard_map/ppermute | solution.py:724
  (222 other events, 4603.1 us)
